TPU v7x, 128 devices: a whole 4x4x4 slice. The times are simulated.
128 devices in a mesh: row: 8 (over z_lo, y), col: 16 (over z_hi, x, core).
Axes of the slice: x: 4, y: 4, z: 4 (z_hi: 2, z_lo: 2; z = z_hi * 2 + z_lo), core: 2. Of those that a mesh axis runs over, the one named last changes fastest.
Arguments:
- picture_vectors: float32 [8192, 1152], P(('row', 'col')), may hold values from -4 to 4
- caption_vectors: float32 [32768, 1152], P(('row', 'col')), may hold values from -4 to 4
- matching_captions: int32 [8192], replicated, may hold values from 0 to 32767, as said below
- natural_exponent_coefficient: float32 [1], replicated, may hold values from 2.3 to 3
- learned_shift: float32 [1], replicated, may hold values from -8 to -6
Outputs:
- grad_images: float32 [8192, 1152], P(('row', 'col'))
- grad_texts: float32 [32768, 1152], P(('row', 'col'))
- loss: float32 [], replicated
Inputs may be any that keep to these rules, and one draw needn't show every extreme that they name: `matching_captions`: no two images name the same text; every value is a text row below 32768.
All inputs are finite; a program needn't handle non-finite values.
Results may differ from a plain program's by a relative error of at most 0.0016.
The roundings to bfloat16 on the way count: a program that leaves them out, or rounds other values in their place, can miss the bound.
Values may be sent and summed in bfloat16 or wider, within the bound.
No kernel may reach another device: no remote copies, remote signals or barrier semaphores. Data moves between devices by JAX's collectives and lax.ppermute only.
A program may use at most 128 MiB of HBM per device.

v0:
```python
import jax
import jax.numpy as jnp
from jax import lax
from jax.sharding import PartitionSpec as P


def unit_rows(matrix):
    inverse = 1.0 / jnp.sqrt(jnp.sum(matrix * matrix, axis=1, keepdims=True) + 1e-06)
    return (matrix * inverse, inverse)


def finish(unit_vals, inverse, direction):
    return inverse * (direction - unit_vals * jnp.sum(unit_vals * direction, axis=1, keepdims=True))


def pair_losses(
    picture_panel_height,
    caption_panel_height,
    picture_index_start,
    caption_index_start,
    sharpness_factor,
    score_shift,
):
    couple_scores = (
        sharpness_factor
        * lax.dot_general(
            picture_panel_height,
            caption_panel_height,
            (((1,), (1,)), ((), ())),
            preferred_element_type=jnp.float32,
        )
        + score_shift
    )
    couple_labels_sign = jnp.where(
        picture_index_start[:, None] == caption_index_start[None, :], 1.0, -1.0
    ).astype(jnp.float32)
    oriented_scores = couple_labels_sign * couple_scores
    partial_loss = jnp.sum(jax.nn.softplus(-oriented_scores))
    couple_factor = (
        -couple_labels_sign * jax.nn.sigmoid(-oriented_scores) * sharpness_factor
    ).astype(jnp.bfloat16)
    return (couple_factor, partial_loss)


def body(
    picture_vectors, caption_vectors, matching_captions, natural_exponent_coefficient, learned_shift
):
    image_unit, image_inv = unit_rows(picture_vectors)
    text_unit, text_inv = unit_rows(caption_vectors)
    image_bf = image_unit.astype(jnp.bfloat16)
    caption_reduced_float = text_unit.astype(jnp.bfloat16)
    sharpness_factor = jnp.exp(natural_exponent_coefficient[0])
    score_shift = learned_shift[0]
    row_count = lax.axis_size("row")
    col_count = lax.axis_size("col")
    row_index = lax.axis_index("row")
    col_index = lax.axis_index("col")
    image_rows = picture_vectors.shape[0]
    text_rows = caption_vectors.shape[0]
    picture_panel_height = lax.all_gather(image_bf, "row", axis=0, tiled=True)
    caption_panel_height = lax.all_gather(caption_reduced_float, "col", axis=0, tiled=True)
    owners = jnp.arange(row_count, dtype=jnp.int32)[:, None] * col_count + col_index
    image_index = (owners * image_rows + jnp.arange(image_rows, dtype=jnp.int32)[None, :]).reshape(
        -1
    )
    caption_index_start = row_index * col_count * text_rows + jnp.arange(
        col_count * text_rows, dtype=jnp.int32
    )
    picture_index_start = jnp.take(matching_captions, image_index)
    couple_factor, partial_loss = pair_losses(
        picture_panel_height,
        caption_panel_height,
        picture_index_start,
        caption_index_start,
        sharpness_factor,
        score_shift,
    )
    selected = couple_factor
    image_dir = lax.psum_scatter(
        jnp.dot(selected, caption_panel_height, preferred_element_type=jnp.float32),
        "row",
        scatter_dimension=0,
        tiled=True,
    )
    selected = couple_factor
    text_dir = lax.psum_scatter(
        lax.dot_general(
            selected,
            picture_panel_height,
            (((0,), (0,)), ((), ())),
            preferred_element_type=jnp.float32,
        ),
        "col",
        scatter_dimension=0,
        tiled=True,
    )
    grad_images = finish(image_unit, image_inv, image_dir)
    grad_texts = finish(text_unit, text_inv, text_dir)
    total_loss = lax.psum(partial_loss, ("row", "col"))
    loss = total_loss / (image_rows * row_count * col_count)
    return (grad_images, grad_texts, loss)


def solution(mesh):
    placed = (P(("row", "col"), None), P(("row", "col"), None), P(), P(), P())
    return jax.shard_map(
        body,
        mesh=mesh,
        in_specs=placed,
        out_specs=(P(("row", "col"), None), P(("row", "col"), None), P()),
        check_vma=False,
    )
```

profile of v0, /device:TPU:1, one launch (start us, length us, event | category | flops | bytes accessed | tf_op | source)
XLA Modules:
  0.0 373.1 jit_solution(1611130782560713651)
XLA Ops:
  7.2 0.0 copy-start
  7.2 0.0 all-gather.3.cloned.1.call-start
  7.2 1.1 multiply_reduce_fusion.3
  8.3 1.7 multiply_convert_fusion.1
  10.0 0.0 all-gather.3.cloned.1.call-update
  10.1 0.0 all-gather.5.cloned.1.call-start
  10.1 1.4 multiply_reduce_fusion.1
  11.6 2.2 multiply_convert_fusion
  13.8 0.0 all-gather.5.cloned.1.call-update
  13.8 0.0 reduce-scatter.3.cloned.1.call-start
  13.9 0.1 iota_add_fusion.1
  13.9 0.1 add.128
  14.0 0.1 add.125
  15.5 3.1 gather_fusion
  18.7 29.3 %all-gather.3.cloned.1.call-done = bf16[512,1152]{1,0:T(8,128)(2,1)} async-done(((bf16[64,1152]{1,0:T(8,128)(2,1)}), bf16[512,1152]{1,0:T(8,128)(2,1)}) %all-gather.3.cloned.1.call-update) | async-done | bytes 1179664 | tf_op jit(solution)/shard_map/all_gather | solution.py:60
  48.0 84.4 %all-gather.5.cloned.1.call-done = bf16[4096,1152]{1,0:T(8,128)(2,1)} async-done(((bf16[256,1152]{1,0:T(8,128)(2,1)}), bf16[4096,1152]{1,0:T(8,128)(2,1)}) %all-gather.5.cloned.1.call-update) | async-done | bytes 9437200 | tf_op jit(solution)/shard_map/all_gather | solution.py:61
  132.3 16.7 %fusion.3 = (f32[]{:T(128)}, bf16[512,4096]{1,0:T(8,128)(2,1)S(1)}) fusion(f32[]{:T(128)} %bitcast.1, s32[4096]{0:T(1024)S(1)} %iota_add_fusion, s32[512]{0:T(512)S(1)} %and_select_fusion, f32[]{:T(128)} %bitcast.9, bf16[512,1152]{1,0:T(8,128)(2,1)} %all-gather.3.cloned.1.call-done, bf16[4096,1152]{1,0:T(8,128)(2,1)} %all-gather.5.cloned.1.call-done), kind=kOutput, calls=%fused_computation.7 | convolution fusion | flops 4871684096 | bytes 14829580 | tf_op jit(solution)/shard_map/dot_general | solution.py:26
  149.1 2.0 copy-done.5
  151.1 7.0 %fusion.4 = f32[512,1152]{1,0:T(8,128)} fusion(bf16[512,4096]{1,0:T(8,128)(2,1)S(1)} %get-tuple-element.4, bf16[4096,1152]{1,0:T(8,128)(2,1)S(1)} %copy-done.3), kind=kOutput, calls=%fused_computation.25 | convolution fusion | flops 4831838208 | bytes 15990784 | tf_op jit(solution)/shard_map/dot_general | solution.py:80
  158.1 0.0 reduce-scatter.3.cloned.1.call-update
  158.2 0.2 reduce-scatter.5.cloned.1.call-start
  158.4 0.0 copy-done.4
  158.4 12.5 %fusion.5 = f32[4096,1152]{1,0:T(8,128)} fusion(bf16[512,4096]{1,0:T(8,128)(2,1)} %copy-done.5, bf16[512,1152]{1,0:T(8,128)(2,1)S(1)} %copy-done.4), kind=kOutput, calls=%fused_computation.26 | convolution fusion | flops 4831838208 | bytes 24248320 | tf_op jit(solution)/shard_map/dot_general | solution.py:87
  170.9 0.0 reduce-scatter.5.cloned.1.call-update
  170.9 66.9 %psum.7 = f32[]{:T(128)} all-reduce(f32[]{:T(128)} %get-tuple-element.3), channel_id=1, replica_groups=mesh['row'=8,'col'=16] {'row','col'}, use_global_device_ids=true, to_apply=%region_7.8 | all-reduce | flops 1 | bytes 8 | tf_op jit(solution)/shard_map/psum | solution.py:99
  238.4 0.0 reduce-scatter.3.cloned.1.call-done
  238.5 0.0 copy-done.2
  238.5 1.2 multiply_reduce_fusion.2
  239.7 1.8 subtract_multiply_fusion.1
  241.5 119.8 %reduce-scatter.5.cloned.1.call-done = f32[256,1152]{1,0:T(8,128)} async-done(((f32[4096,1152]{1,0:T(8,128)}), f32[256,1152]{1,0:T(8,128)}) %reduce-scatter.5.cloned.1.call-update) | async-done | bytes 1179664 | tf_op jit(solution)/shard_map/reduce_scatter | solution.py:86
  361.3 1.6 multiply_reduce_fusion
  362.8 2.5 subtract_multiply_fusion
  (15 shorter events, 0.1 us)
Async XLA Ops:
  7.2 8.3 %copy-start = (s32[8192]{0:T(1024)S(1)}, s32[8192]{0:T(1024)}, u32[]{:S(2)}) copy-start(s32[8192]{0:T(1024)} %param.7) | copy-start | bytes 98308
  7.2 40.8 %all-gather.3.cloned.1.call-start = ((), (), s32[]{:S(2)}) async-start(), calls=%async_computation.2 | async-start | bytes 1327104 | tf_op jit(solution)/shard_map/all_gather | solution.py:60
  10.1 122.3 %all-gather.5.cloned.1.call-start = ((), (), s32[]{:S(2)}) async-start(), calls=%async_computation.3 | async-start | bytes 10027008 | tf_op jit(solution)/shard_map/all_gather | solution.py:61
  13.8 224.7 %reduce-scatter.3.cloned.1.call-start = ((), (), s32[]{:S(2)}) async-start(), calls=%async_computation.4 | async-start | bytes 2654208 | tf_op jit(solution)/shard_map/reduce_scatter | solution.py:79
  132.3 18.8 %copy-start.3 = (bf16[4096,1152]{1,0:T(8,128)(2,1)S(1)}, bf16[4096,1152]{1,0:T(8,128)(2,1)}, u32[]{:S(2)}) copy-start(bf16[4096,1152]{1,0:T(8,128)(2,1)} %all-gather.5.cloned.1.call-done) | copy-start | bytes 28311556
  149.1 2.0 copy-start.5
  151.1 7.3 %copy-start.4 = (bf16[512,1152]{1,0:T(8,128)(2,1)S(1)}, bf16[512,1152]{1,0:T(8,128)(2,1)}, u32[]{:S(2)}) copy-start(bf16[512,1152]{1,0:T(8,128)(2,1)} %all-gather.3.cloned.1.call-done) | copy-start | bytes 3538948
  158.2 203.1 %reduce-scatter.5.cloned.1.call-start = ((), (), s32[]{:S(2)}) async-start(), calls=%async_computation.5 | async-start | bytes 20054016 | tf_op jit(solution)/shard_map/reduce_scatter | solution.py:86
  170.9 67.6 %copy-start.2 = (f32[64,1152]{1,0:T(8,128)S(1)}, f32[64,1152]{1,0:T(8,128)}, u32[]{:S(2)}) copy-start(f32[64,1152]{1,0:T(8,128)} %param.5) | copy-start | bytes 884740
  170.9 190.4 %copy-start.1 = (f32[256,1152]{1,0:T(8,128)S(1)}, f32[256,1152]{1,0:T(8,128)}, u32[]{:S(2)}) copy-start(f32[256,1152]{1,0:T(8,128)} %param.6) | copy-start | bytes 3538948
Sparse Core Ops, SparseCore 0:
  10.2 37.6 all-gather.2
  51.0 81.3 all-gather.4
  158.3 36.1 reduce-scatter.2
  198.8 162.4 reduce-scatter.4
where the time goes:
time: 374 us; the launch traced here: 373 us
  waiting for transfers between devices  234 us (63%)
  blocking collectives  66.9 us (18%)
  matrix products  36.3 us (10%)
  between operations  17 us (5%)
  other arithmetic  13.7 us (4%)
  local copies, waits for them, and re-layouts  5.35 us (1%)
    reduce_scatter x1, waiting for transfers between devices, body(): lax.psum_scatter(lax.dot_general(selected, picture_panel_height, (((0,),...  120 us
    all_gather x1, waiting for transfers between devices, body(): lax.all_gather(caption_reduced_float, 'col', axis=0, tiled=True)  84.4 us
    psum x1, blocking collectives, body(): total_loss = lax.psum(partial_loss, ('row', 'col'))  66.9 us
    all_gather x1, waiting for transfers between devices, body(): picture_panel_height = lax.all_gather(image_bf, 'row', axis=0, tiled=True)  29.3 us
    dot_general x1, matrix products, pair_losses(): lax.dot_general(picture_panel_height, caption_panel_height, (((1,), (1,))...  16.7 us
    dot_general x1, matrix products, body(): lax.dot_general(selected, picture_panel_height, (((0,), (0,)), ((), ())),...  12.5 us
  transfers between devices with their start and end apart: 4, of which 3 were waited for; matrix products, arithmetic and copies ran while one was open for 6% of the time, Pallas kernels for 0%

commit v1 on v0

v1 whole, which is shorter than its diff:
```python
import functools
import math

import jax
import jax.numpy as jnp
from jax import lax
from jax.experimental import pallas as pl
from jax.experimental.pallas import tpu as pltpu
from jax.sharding import PartitionSpec as P

AXES = ("row", "col")
RING = 4
LOG2E = math.log2(math.e)
WIRE = jnp.float16


def place(index):
    row, col = index // 16, index % 16
    return (col // 2) % 4, row % 4, (col // 8) * 2 + row // 4, col % 2


def index_of(x, y, z, core):
    return ((z % 2) * 4 + y) * 16 + (z // 2) * 8 + x * 2 + core


def send(value, move):
    pairs = [(d, index_of(*move(*place(d)))) for d in range(128)]
    return lax.ppermute(value, AXES, pairs)


def along_y(step):
    return lambda x, y, z, c: (x, (y + step) % RING, z, c)


def along_first(step):
    return lambda x, y, z, c: ((x + step) % RING, y, z, c) if c == 0 else (x, y, (z + step) % RING, c)


def along_second(step):
    return lambda x, y, z, c: (x, y, (z + step) % RING, c) if c == 0 else ((x + step) % RING, y, z, c)


def swap(x, y, z, c):
    return x, y, z, 1 - c


def unit_rows(matrix):
    inverse = 1.0 / jnp.sqrt(jnp.sum(matrix * matrix, axis=1, keepdims=True) + 1e-06)
    return (matrix * inverse, inverse)


def finish(unit_vals, inverse, direction):
    return inverse * (direction - unit_vals * jnp.sum(unit_vals * direction, axis=1, keepdims=True))


CHUNK = 256


def pair_kernel(scale_ref, base_ref, match_ref, *refs):
    texts, images = refs[:8], refs[8:12]
    image_out, text_out, loss_out = refs[12:15]
    text_buf, image_buf, weight_buf, sems = refs[15:]
    copies = [
        pltpu.make_async_copy(src, image_buf.at[pl.ds(i * CHUNK, CHUNK)], sems.at[i])
        for i, src in enumerate(images)
    ] + [
        pltpu.make_async_copy(src, text_buf.at[pl.ds(i * CHUNK, CHUNK)], sems.at[4 + i])
        for i, src in enumerate(texts)
    ]
    for copy in copies:
        copy.start()
    slope, shift, temperature = scale_ref[0], scale_ref[1], scale_ref[2]
    image_out[...] = jnp.zeros_like(image_out)
    loss_out[...] = jnp.zeros_like(loss_out)
    for copy in copies:
        copy.wait()
    row_index = lax.broadcasted_iota(jnp.int32, (CHUNK, CHUNK), 0)

    def step(s, carry):
        for half in range(2):
            rows = pl.ds(s * 2 * CHUNK + half * CHUNK, CHUNK)
            base = base_ref[2 * s + half]
            for i in range(4):
                cols = pl.ds(i * CHUNK, CHUNK)
                scores = lax.dot_general(
                    text_buf[rows, :],
                    image_buf[cols, :],
                    (((1,), (1,)), ((), ())),
                    preferred_element_type=jnp.float32,
                )
                matched = (match_ref[:, cols] - base) == row_index
                power = scores * slope + shift
                grown = jnp.exp2(jnp.where(matched, -power, power))
                total = 1.0 + grown
                inv = pl.reciprocal(total, approx=True)
                inv = inv * (2.0 - total * inv)
                weight = (grown * temperature) * inv
                weight = jnp.where(matched, -weight, weight)
                weight_buf[pl.ds(half * CHUNK, CHUNK), cols] = weight.astype(jnp.bfloat16)
                low, high = grown[: CHUNK // 2], grown[CHUNK // 2 :]
                joined = low + high + low * high
                low, high = joined[: CHUNK // 4], joined[CHUNK // 4 :]
                joined = low + high + low * high
                loss_out[...] += jnp.sum(jnp.log1p(joined).reshape(8, 8, CHUNK), axis=0)
        rows = pl.ds(s * 2 * CHUNK, 2 * CHUNK)
        text_out[rows, :] = jnp.dot(
            weight_buf[...], image_buf[...], preferred_element_type=jnp.float32
        )
        for i in range(4):
            cols = pl.ds(i * CHUNK, CHUNK)
            image_out[cols, :] += lax.dot_general(
                weight_buf[:, cols],
                text_buf[rows, :],
                (((0,), (0,)), ((), ())),
                preferred_element_type=jnp.float32,
            )
        return carry

    lax.fori_loop(0, 4, step, 0)


def pair_block(scale, base, match, texts, images):
    dim = images[0].shape[1]
    any_space = pl.BlockSpec(memory_space=pl.ANY)
    smem = pl.BlockSpec(memory_space=pltpu.SMEM)
    vmem = pl.BlockSpec(memory_space=pltpu.VMEM)
    return pl.pallas_call(
        pair_kernel,
        out_shape=(
            jax.ShapeDtypeStruct((4 * CHUNK, dim), jnp.float32),
            jax.ShapeDtypeStruct((8 * CHUNK, dim), jnp.float32),
            jax.ShapeDtypeStruct((8, CHUNK), jnp.float32),
        ),
        in_specs=[smem, smem, vmem] + [any_space] * 12,
        out_specs=(vmem, vmem, vmem),
        scratch_shapes=[
            pltpu.VMEM((8 * CHUNK, dim), jnp.bfloat16),
            pltpu.VMEM((4 * CHUNK, dim), jnp.bfloat16),
            pltpu.VMEM((2 * CHUNK, 4 * CHUNK), jnp.bfloat16),
            pltpu.SemaphoreType.DMA((12,)),
        ],
        compiler_params=pltpu.CompilerParams(vmem_limit_bytes=48 * 2**20),
        cost_estimate=pl.CostEstimate(
            flops=6 * 4 * CHUNK * 8 * CHUNK * dim,
            bytes_accessed=24 * 2**20,
            transcendentals=3 * 32 * CHUNK * CHUNK,
        ),
    )(scale, base, match, *texts, *images)


def body(
    picture_vectors, caption_vectors, matching_captions, natural_exponent_coefficient, learned_shift
):
    me = lax.axis_index("row") * 16 + lax.axis_index("col")
    x, y, z, core = place(me)
    image_rows, text_rows = picture_vectors.shape[0], caption_vectors.shape[0]
    temperature = jnp.exp(natural_exponent_coefficient[0])
    scale = jnp.stack([temperature * LOG2E, learned_shift[0] * LOG2E, temperature])

    text_unit, text_inv = unit_rows(caption_vectors)
    text_bf = text_unit.astype(jnp.bfloat16)
    image_unit, image_inv = unit_rows(picture_vectors)
    image_bf = image_unit.astype(jnp.bfloat16)

    own_texts = [text_bf] + [send(text_bf, along_y(-s)) for s in (1, 2, 3)]
    lines = [image_bf] + [send(image_bf, along_first(-r)) for r in (1, 2, 3)]
    line = jnp.concatenate(lines, axis=0)
    images = [line] + [send(line, along_second(-s)) for s in (1, 2, 3)]
    sibling_texts = [send(t, swap) for t in own_texts]
    texts = [t for pair in zip(own_texts, sibling_texts) for t in pair]

    base = jnp.stack(
        [index_of(x, (y + s) % RING, z, k) for s in range(RING) for k in (core, 1 - core)]
    ).astype(jnp.int32) * text_rows
    table = matching_captions.reshape(-1, image_rows)
    steps = jnp.arange(RING, dtype=jnp.int32)
    second, first = steps[:, None], steps[None, :]
    owners = jnp.where(
        core == 0,
        index_of((x + first) % RING, y, (z + second) % RING, core),
        index_of((x + second) % RING, y, (z + first) % RING, core),
    )
    match = jnp.take(table, owners.reshape(-1), axis=0).reshape(1, -1)

    image_part, text_part, loss_part = pair_block(scale, base, match, texts, images)

    text_part = text_part.reshape(RING, 2, text_rows, -1)
    other = text_part[:, 1].astype(WIRE)
    mine = text_part[:, 0] + send(other, swap).astype(jnp.float32)
    text_dir = mine[0]
    arrived = [send(mine[s].astype(WIRE), along_y(s)) for s in (1, 2, 3)]
    for part in arrived:
        text_dir = text_dir + part.astype(jnp.float32)

    image_part = image_part.reshape(RING, RING * image_rows, -1)
    arrived = [send(image_part[s].astype(WIRE), along_second(s)) for s in (1, 2, 3)]
    line_dir = image_part[0]
    for part in arrived:
        line_dir = line_dir + part.astype(jnp.float32)
    line_dir = line_dir.reshape(RING, image_rows, -1)
    arrived = [send(line_dir[r].astype(WIRE), along_first(r)) for r in (1, 2, 3)]
    image_dir = line_dir[0]
    for part in arrived:
        image_dir = image_dir + part.astype(jnp.float32)

    grad_images = finish(image_unit, image_inv, image_dir)
    grad_texts = finish(text_unit, text_inv, text_dir)
    loss = lax.psum(jnp.sum(loss_part), AXES) / matching_captions.shape[0]
    return (grad_images, grad_texts, loss)


def solution(mesh):
    placed = (P(AXES, None), P(AXES, None), P(), P(), P())
    return jax.shard_map(
        body,
        mesh=mesh,
        in_specs=placed,
        out_specs=(P(AXES, None), P(AXES, None), P()),
        check_vma=False,
    )
```

time: 374 us -> 208 us (0.56)
  waiting for transfers between devices: 234 us -> 48.6 us
  matrix products: 36.3 us -> 0 us
  Pallas kernels: 0 us -> 26.9 us
  starting transfers between devices: 0.34 us -> 26.8 us
  between operations: 17 us -> 4.07 us
  local copies, waits for them, and re-layouts: 5.35 us -> 11.2 us
  blocking collectives: 66.9 us -> 71.8 us
  other arithmetic: 13.7 us -> 17.9 us
    reduce_scatter x2 -> x0, waiting for transfers between devices: 120 us -> none  [the longest x1 120 us: body(): lax.psum_scatter(lax.dot_general(selected, picture_panel_height, (((0,),...]
    all_gather x2 -> x0, waiting for transfers between devices: 114 us -> none  [the longest x1 84.4 us: body(): lax.all_gather(caption_reduced_float, 'col', axis=0, tiled=True)]
    ppermute x0 -> x23, waiting for transfers between devices: none -> 48.6 us  [send(): return lax.ppermute(value, AXES, pairs)]
    dot_general x3 -> x0, matrix products: 36.3 us -> none  [the longest x1 16.7 us: pair_losses(): lax.dot_general(picture_panel_height, caption_panel_height, (((1,), (1,))...]
    pallas_call x0 -> x1, Pallas kernels: none -> 26.9 us  [pair_block(): pl.pallas_call(pair_kernel, out_shape=(jax.ShapeDtypeStruct((4 * CHUNK, d...]
    ppermute x0 -> x23, starting transfers between devices: none -> 26.8 us  [send(): return lax.ppermute(value, AXES, pairs)]
    slice x0 -> x3, local copies, waits for them, and re-layouts: none -> 6.93 us  [the longest x1 6.52 us: body(): mine = text_part[:, 0] + send(other, swap).astype(jnp.float32)]
    another operation x0 -> x4, other arithmetic: none -> 5.76 us
  transfers between devices with their start and end apart: 4 -> 23, of which waited for: 3 -> 6; matrix products, arithmetic and copies ran while one was open for 6% -> 8% of each run, Pallas kernels for 0% -> 0%
where the time goes in v1:
time: 208 us; the launch traced here: 207 us
  blocking collectives  71.8 us (35%)
  waiting for transfers between devices  48.6 us (23%)
  Pallas kernels  26.9 us (13%)
  starting transfers between devices  26.8 us (13%)
  other arithmetic  17.9 us (9%)
  local copies, waits for them, and re-layouts  11.2 us (5%)
  between operations  4.07 us (2%)
    psum x1, blocking collectives, body(): loss = lax.psum(jnp.sum(loss_part), AXES) / matching_captions.shape[0]  71.8 us
    ppermute x23, waiting for transfers between devices, send(): return lax.ppermute(value, AXES, pairs)  48.6 us
    pallas_call x1, Pallas kernels, pair_block(): pl.pallas_call(pair_kernel, out_shape=(jax.ShapeDtypeStruct((4 * CHUNK, d...  26.9 us
    ppermute x23, starting transfers between devices, send(): return lax.ppermute(value, AXES, pairs)  26.8 us
    slice x1, local copies, waits for them, and re-layouts, body(): mine = text_part[:, 0] + send(other, swap).astype(jnp.float32)  6.52 us
    another operation x3, other arithmetic  5.68 us
  transfers between devices with their start and end apart: 23, of which 6 were waited for; matrix products, arithmetic and copies ran while one was open for 8% of the time, Pallas kernels for 0%

profile of v1, /device:TPU:1, one launch (start us, length us, event | category | flops | bytes accessed | tf_op | source)
XLA Modules:
  0.0 207.3 jit_solution(16567104622142154576)
XLA Ops:
  0.6 1.2 multiply_reduce_fusion.3
  1.8 1.0 multiply_convert_fusion.1
  2.9 2.5 %collective-permute-start.9 = (bf16[64,1152]{1,0:T(8,128)(2,1)S(1)}, bf16[64,1152]{1,0:T(8,128)(2,1)}, u32[]{:S(2)}, u32[]{:S(2)}) collective-permute-start(bf16[64,1152]{1,0:T(8,128)(2,1)S(1)} %multiply_convert_fusion.1), channel_id=1, source_target_pairs={{0,2},{1,65},{2,4},{3,67},{4,6},{5,69},{6,0},{7,71},{8,10},{9,73},... | collective-permute-start | bytes 442376 | tf_op jit(solution)/shard_map/ppermute | solution.py:28
  5.4 3.3 %collective-permute-start.8 = (bf16[64,1152]{1,0:T(8,128)(2,1)S(1)}, bf16[64,1152]{1,0:T(8,128)(2,1)}, u32[]{:S(2)}, u32[]{:S(2)}) collective-permute-start(bf16[64,1152]{1,0:T(8,128)(2,1)S(1)} %multiply_convert_fusion.1), channel_id=1, source_target_pairs={{0,4},{1,9},{2,6},{3,11},{4,0},{5,13},{6,2},{7,15},{8,12},{9,1},{1... | collective-permute-start | bytes 442376 | tf_op jit(solution)/shard_map/ppermute | solution.py:28
  9.5 1.4 multiply_reduce_fusion.1
  11.1 0.7 collective-permute-start
  11.8 2.7 %collective-permute-start.1 = (bf16[256,1152]{1,0:T(8,128)(2,1)S(1)}, bf16[256,1152]{1,0:T(8,128)(2,1)S(1)}, u32[]{:S(2)}, u32[]{:S(2)}) collective-permute-start(bf16[256,1152]{1,0:T(8,128)(2,1)S(1)} %multiply_convert_fusion.refs_0_), channel_id=1, source_target_pairs={{0,48},{1,49},{2,50},{3,51},{4,52},{5,53},{6,54},{7,55},{8,56},{9,... | collective-permute-start | bytes 1769480 | tf_op jit(solution)/shard_map/ppermute | solution.py:28
  15.7 1.2 pad_maximum_fusion.refs_8_
  16.9 2.0 collective-permute-start.10
  20.2 19.6 %collective-permute-done.1.refs_2_ = bf16[256,1152]{1,0:T(8,128)(2,1)S(1)} collective-permute-done((bf16[256,1152]{1,0:T(8,128)(2,1)S(1)}, bf16[256,1152]{1,0:T(8,128)(2,1)S(1)}, u32[]{:S(2)}, u32[]{:S(2)}) %collective-permute-start.1) | collective-permute-done | bytes 589856 | tf_op jit(solution)/shard_map/ppermute | solution.py:28
  40.0 2.7 %collective-permute-start.2 = (bf16[256,1152]{1,0:T(8,128)(2,1)S(1)}, bf16[256,1152]{1,0:T(8,128)(2,1)}, u32[]{:S(2)}, u32[]{:S(2)}) collective-permute-start(bf16[256,1152]{1,0:T(8,128)(2,1)S(1)} %collective-permute-done.1.refs_2_), channel_id=1, source_target_pairs={{0,1},{1,0},{2,3},{3,2},{4,5},{5,4},{6,7},{7,6},{8,9},{9,8},{10,11... | collective-permute-start | bytes 1769480 | tf_op jit(solution)/shard_map/ppermute | solution.py:28
  42.7 1.4 collective-permute-done.5.refs_6_
  46.0 1.5 reshape.377
  47.5 1.4 gather_fusion
  48.9 1.3 broadcast_select_fusion
  50.2 0.8 select_n.233.match_ref
  51.2 26.9 %shard_map.76 = (f32[1024,1152]{1,0:T(8,128)}, f32[2048,1152]{1,0:T(8,128)}, f32[8,256]{1,0:T(8,128)S(1)}) custom-call(f32[3]{0:T(128)S(1)} %pad_maximum_fusion.1.scale_ref, s32[8]{0:T(128)S(1)} %broadcast_multiply_fusion.base_ref, s32[1,1024]{1,0:T(1,128)S(1)} %select_n.233.match_ref, bf16[256,1152]{1,0:T(8,128)(2,1)S(1)} %multiply_convert_fusion.refs_0_, ...), custom_call_target="tpu_custom_call" | custom-call | flops 14495514624 | bytes 25165824 | tf_op jit(solution)/shard_map/pallas_call | solution.py:127
  78.0 6.5 %fusion.18 = (f32[4,1,256,1152]{3,2,1,0:T(8,128)}, f32[4,1,256,1152]{3,2,1,0:T(8,128)S(1)}) fusion(f32[4,2,256,1152]{3,2,1,0:T(8,128)} %bitcast.36), kind=kLoop, calls=%fused_computation.56 | loop fusion | bytes 18874368 | tf_op jit(solution)/shard_map/slice | solution.py:189
  84.6 1.7 fusion.1
  86.3 1.6 collective-permute-start.19
  88.5 2.0 collective-permute-start.15
  92.2 71.8 %psum.7 = f32[]{:T(128)} all-reduce(f32[]{:T(128)} %reduce_sum.49), channel_id=1, replica_groups=mesh['row'=8,'col'=16] {'row','col'}, use_global_device_ids=true, to_apply=%region_5.6 | all-reduce | flops 1 | bytes 8 | tf_op jit(solution)/shard_map/psum | solution.py:208
  164.7 1.6 fusion.17
  166.3 2.2 %collective-permute-start.18 = (f16[64,1152]{1,0:T(8,128)(2,1)S(1)}, f16[64,1152]{1,0:T(8,128)(2,1)S(1)}, u32[]{:S(2)}, u32[]{:S(2)}) collective-permute-start(f16[64,1152]{1,0:T(8,128)(2,1)S(1)} %get-tuple-element.22), channel_id=1, source_target_pairs={{0,6},{1,73},{2,0},{3,75},{4,2},{5,77},{6,4},{7,79},{8,14},{9,65},... | collective-permute-start | bytes 442376 | tf_op jit(solution)/shard_map/ppermute | solution.py:28
  169.2 3.8 %fusion.15 = (f16[4,256,1152]{2,1,0:T(8,128)(2,1)S(1)}, f32[4,256,1152]{2,1,0:T(8,128)S(1)}) fusion(f16[4,256,1152]{2,1,0:T(8,128)(2,1)} %collective-permute-done.19, f32[4,1,256,1152]{3,2,1,0:T(8,128)} %get-tuple-element.13), kind=kLoop, calls=%fused_computation.54 | loop fusion | flops 3538944 | bytes 14155776 | tf_op jit(solution)/shard_map/convert.2
  173.4 1.4 collective-permute-start.22
  174.8 0.8 collective-permute-start.21
  176.1 0.8 subtract_multiply_fusion.1
  176.9 9.7 %collective-permute-done.22 = f16[256,1152]{1,0:T(8,128)(2,1)S(1)} collective-permute-done((f16[256,1152]{1,0:T(8,128)(2,1)S(1)}, f16[256,1152]{1,0:T(8,128)(2,1)S(1)}, u32[]{:S(2)}, u32[]{:S(2)}) %collective-permute-start.22) | collective-permute-done | bytes 589856 | tf_op jit(solution)/shard_map/ppermute | solution.py:28
  186.6 2.7 %collective-permute-done.21 = f16[256,1152]{1,0:T(8,128)(2,1)S(1)} collective-permute-done((f16[256,1152]{1,0:T(8,128)(2,1)S(1)}, f16[256,1152]{1,0:T(8,128)(2,1)S(1)}, u32[]{:S(2)}, u32[]{:S(2)}) %collective-permute-start.21) | collective-permute-done | bytes 589856 | tf_op jit(solution)/shard_map/ppermute | solution.py:28
  189.3 14.8 %collective-permute-done.20 = f16[256,1152]{1,0:T(8,128)(2,1)S(1)} collective-permute-done((f16[256,1152]{1,0:T(8,128)(2,1)S(1)}, f16[256,1152]{1,0:T(8,128)(2,1)S(1)}, u32[]{:S(2)}, u32[]{:S(2)}) %collective-permute-start.20) | collective-permute-done | bytes 589856 | tf_op jit(solution)/shard_map/ppermute | solution.py:28
  204.7 1.5 subtract_multiply_fusion
  (64 shorter events, 8.7 us)
Async XLA Ops:
  0.6 10.3 %copy-start = (f32[256,1152]{1,0:T(8,128)S(1)}, f32[256,1152]{1,0:T(8,128)}, u32[]{:S(2)}) copy-start(f32[256,1152]{1,0:T(8,128)} %param.6) | copy-start | bytes 3538948
  1.8 9.1 %copy-start.5 = (f32[64]{0:T(128)}, f32[64]{0:T(128)S(1)}, u32[]{:S(2)}) copy-start(f32[64]{0:T(128)S(1)} %add_rsqrt_fusion.1) | copy-start | bytes 772
  2.9 8.2 %copy-start.4 = (bf16[64,1152]{1,0:T(8,128)(2,1)}, bf16[64,1152]{1,0:T(8,128)(2,1)S(1)}, u32[]{:S(2)}) copy-start(bf16[64,1152]{1,0:T(8,128)(2,1)S(1)} %multiply_convert_fusion.1) | copy-start | bytes 442372
  2.9 11.7 %collective-permute-start.9 = (bf16[64,1152]{1,0:T(8,128)(2,1)S(1)}, bf16[64,1152]{1,0:T(8,128)(2,1)}, u32[]{:S(2)}, u32[]{:S(2)}) collective-permute-start(bf16[64,1152]{1,0:T(8,128)(2,1)S(1)} %multiply_convert_fusion.1), channel_id=1, source_target_pairs={{0,2},{1,65},{2,4},{3,67},{4,6},{5,69},{6,0},{7,71},{8,10},{9,73},... | collective-permute-start | bytes 442376 | tf_op jit(solution)/shard_map/ppermute | solution.py:28
  5.4 9.6 %collective-permute-start.8 = (bf16[64,1152]{1,0:T(8,128)(2,1)S(1)}, bf16[64,1152]{1,0:T(8,128)(2,1)}, u32[]{:S(2)}, u32[]{:S(2)}) collective-permute-start(bf16[64,1152]{1,0:T(8,128)(2,1)S(1)} %multiply_convert_fusion.1), channel_id=1, source_target_pairs={{0,4},{1,9},{2,6},{3,11},{4,0},{5,13},{6,2},{7,15},{8,12},{9,1},{1... | collective-permute-start | bytes 442376 | tf_op jit(solution)/shard_map/ppermute | solution.py:28
  8.8 7.0 %collective-permute-start.7 = (bf16[64,1152]{1,0:T(8,128)(2,1)S(1)}, bf16[64,1152]{1,0:T(8,128)(2,1)}, u32[]{:S(2)}, u32[]{:S(2)}) collective-permute-start(bf16[64,1152]{1,0:T(8,128)(2,1)S(1)} %multiply_convert_fusion.1), channel_id=1, source_target_pairs={{0,6},{1,73},{2,0},{3,75},{4,2},{5,77},{6,4},{7,79},{8,14},{9,65},... | collective-permute-start | bytes 442376 | tf_op jit(solution)/shard_map/ppermute | solution.py:28
  11.1 8.5 %collective-permute-start = (bf16[256,1152]{1,0:T(8,128)(2,1)S(1)}, bf16[256,1152]{1,0:T(8,128)(2,1)S(1)}, u32[]{:S(2)}, u32[]{:S(2)}) collective-permute-start(bf16[256,1152]{1,0:T(8,128)(2,1)S(1)} %multiply_convert_fusion.refs_0_), channel_id=1, source_target_pairs={{0,1},{1,0},{2,3},{3,2},{4,5},{5,4},{6,7},{7,6},{8,9},{9,8},{10,11... | collective-permute-start | bytes 1769480 | tf_op jit(solution)/shard_map/ppermute | solution.py:28
  11.8 27.9 %collective-permute-start.1 = (bf16[256,1152]{1,0:T(8,128)(2,1)S(1)}, bf16[256,1152]{1,0:T(8,128)(2,1)S(1)}, u32[]{:S(2)}, u32[]{:S(2)}) collective-permute-start(bf16[256,1152]{1,0:T(8,128)(2,1)S(1)} %multiply_convert_fusion.refs_0_), channel_id=1, source_target_pairs={{0,48},{1,49},{2,50},{3,51},{4,52},{5,53},{6,54},{7,55},{8,56},{9,... | collective-permute-start | bytes 1769480 | tf_op jit(solution)/shard_map/ppermute | solution.py:28
  14.6 25.4 %collective-permute-start.3 = (bf16[256,1152]{1,0:T(8,128)(2,1)S(1)}, bf16[256,1152]{1,0:T(8,128)(2,1)S(1)}, u32[]{:S(2)}, u32[]{:S(2)}) collective-permute-start(bf16[256,1152]{1,0:T(8,128)(2,1)S(1)} %multiply_convert_fusion.refs_0_), channel_id=1, source_target_pairs={{0,32},{1,33},{2,34},{3,35},{4,36},{5,37},{6,38},{7,39},{8,40},{9,... | collective-permute-start | bytes 1769480 | tf_op jit(solution)/shard_map/ppermute | solution.py:28
  15.0 29.0 %collective-permute-start.5 = (bf16[256,1152]{1,0:T(8,128)(2,1)S(1)}, bf16[256,1152]{1,0:T(8,128)(2,1)S(1)}, u32[]{:S(2)}, u32[]{:S(2)}) collective-permute-start(bf16[256,1152]{1,0:T(8,128)(2,1)S(1)} %multiply_convert_fusion.refs_0_), channel_id=1, source_target_pairs={{0,16},{1,17},{2,18},{3,19},{4,20},{5,21},{6,22},{7,23},{8,24},{9,... | collective-permute-start | bytes 1769480 | tf_op jit(solution)/shard_map/ppermute | solution.py:28
  16.9 27.7 %collective-permute-start.10 = (bf16[256,1152]{1,0:T(8,128)(2,1)S(1)}, bf16[256,1152]{1,0:T(8,128)(2,1)}, u32[]{:S(2)}, u32[]{:S(2)}) collective-permute-start(bf16[256,1152]{1,0:T(8,128)(2,1)S(1)} %pad_maximum_fusion.refs_8_), channel_id=1, source_target_pairs={{0,72},{1,7},{2,74},{3,1},{4,76},{5,3},{6,78},{7,5},{8,64},{9,15},... | collective-permute-start | bytes 1769480 | tf_op jit(solution)/shard_map/ppermute | solution.py:28
  19.6 31.5 %collective-permute-start.11 = (bf16[256,1152]{1,0:T(8,128)(2,1)S(1)}, bf16[256,1152]{1,0:T(8,128)(2,1)}, u32[]{:S(2)}, u32[]{:S(2)}) collective-permute-start(bf16[256,1152]{1,0:T(8,128)(2,1)S(1)} %pad_maximum_fusion.refs_8_), channel_id=1, source_target_pairs={{0,8},{1,5},{2,10},{3,7},{4,12},{5,1},{6,14},{7,3},{8,0},{9,13},{1... | collective-permute-start | bytes 1769480 | tf_op jit(solution)/shard_map/ppermute | solution.py:28
  39.8 11.4 %collective-permute-start.12 = (bf16[256,1152]{1,0:T(8,128)(2,1)S(1)}, bf16[256,1152]{1,0:T(8,128)(2,1)}, u32[]{:S(2)}, u32[]{:S(2)}) collective-permute-start(bf16[256,1152]{1,0:T(8,128)(2,1)S(1)} %pad_maximum_fusion.refs_8_), channel_id=1, source_target_pairs={{0,64},{1,3},{2,66},{3,5},{4,68},{5,7},{6,70},{7,1},{8,72},{9,11},... | collective-permute-start | bytes 1769480 | tf_op jit(solution)/shard_map/ppermute | solution.py:28
  40.0 11.2 %collective-permute-start.2 = (bf16[256,1152]{1,0:T(8,128)(2,1)S(1)}, bf16[256,1152]{1,0:T(8,128)(2,1)}, u32[]{:S(2)}, u32[]{:S(2)}) collective-permute-start(bf16[256,1152]{1,0:T(8,128)(2,1)S(1)} %collective-permute-done.1.refs_2_), channel_id=1, source_target_pairs={{0,1},{1,0},{2,3},{3,2},{4,5},{5,4},{6,7},{7,6},{8,9},{9,8},{10,11... | collective-permute-start | bytes 1769480 | tf_op jit(solution)/shard_map/ppermute | solution.py:28
  44.1 7.1 %collective-permute-start.4 = (bf16[256,1152]{1,0:T(8,128)(2,1)S(1)}, bf16[256,1152]{1,0:T(8,128)(2,1)}, u32[]{:S(2)}, u32[]{:S(2)}) collective-permute-start(bf16[256,1152]{1,0:T(8,128)(2,1)S(1)} %collective-permute-done.3.refs_4_), channel_id=1, source_target_pairs={{0,1},{1,0},{2,3},{3,2},{4,5},{5,4},{6,7},{7,6},{8,9},{9,8},{10,11... | collective-permute-start | bytes 1769480 | tf_op jit(solution)/shard_map/ppermute | solution.py:28
  44.6 6.6 %collective-permute-start.6 = (bf16[256,1152]{1,0:T(8,128)(2,1)S(1)}, bf16[256,1152]{1,0:T(8,128)(2,1)}, u32[]{:S(2)}, u32[]{:S(2)}) collective-permute-start(bf16[256,1152]{1,0:T(8,128)(2,1)S(1)} %collective-permute-done.5.refs_6_), channel_id=1, source_target_pairs={{0,1},{1,0},{2,3},{3,2},{4,5},{5,4},{6,7},{7,6},{8,9},{9,8},{10,11... | collective-permute-start | bytes 1769480 | tf_op jit(solution)/shard_map/ppermute | solution.py:28
  84.6 3.3 %copy-start.2 = (f32[1024,1152]{1,0:T(8,128)S(1)}, f32[1024,1152]{1,0:T(8,128)}, u32[]{:S(2)}) copy-start(f32[1024,1152]{1,0:T(8,128)} %get-tuple-element.6) | copy-start | bytes 14155780
  86.3 82.9 %collective-permute-start.19 = (f16[4,256,1152]{2,1,0:T(8,128)(2,1)}, f16[4,256,1152]{2,1,0:T(8,128)(2,1)}, u32[]{:S(2)}, u32[]{:S(2)}) collective-permute-start(f16[4,256,1152]{2,1,0:T(8,128)(2,1)} %fusion.1), channel_id=1, source_target_pairs={{0,1},{1,0},{2,3},{3,2},{4,5},{5,4},{6,7},{7,6},{8,9},{9,8},{10,11... | collective-permute-start | bytes 7077896 | tf_op jit(solution)/shard_map/ppermute | solution.py:28
  88.5 76.1 %collective-permute-start.15 = (f16[256,1152]{1,0:T(8,128)(2,1)S(1)}, f16[256,1152]{1,0:T(8,128)(2,1)S(1)}, u32[]{:S(2)}, u32[]{:S(2)}) collective-permute-start(f16[256,1152]{1,0:T(8,128)(2,1)S(1)} %get-tuple-element.19), channel_id=1, source_target_pairs={{0,72},{1,7},{2,74},{3,1},{4,76},{5,3},{6,78},{7,5},{8,64},{9,15},... | collective-permute-start | bytes 1769480 | tf_op jit(solution)/shard_map/ppermute | solution.py:28
  90.5 74.2 %collective-permute-start.14 = (f16[256,1152]{1,0:T(8,128)(2,1)S(1)}, f16[256,1152]{1,0:T(8,128)(2,1)S(1)}, u32[]{:S(2)}, u32[]{:S(2)}) collective-permute-start(f16[256,1152]{1,0:T(8,128)(2,1)S(1)} %get-tuple-element.20), channel_id=1, source_target_pairs={{0,8},{1,5},{2,10},{3,7},{4,12},{5,1},{6,14},{7,3},{8,0},{9,13},{1... | collective-permute-start | bytes 1769480 | tf_op jit(solution)/shard_map/ppermute | solution.py:28
  91.0 73.7 %collective-permute-start.13 = (f16[256,1152]{1,0:T(8,128)(2,1)S(1)}, f16[256,1152]{1,0:T(8,128)(2,1)S(1)}, u32[]{:S(2)}, u32[]{:S(2)}) collective-permute-start(f16[256,1152]{1,0:T(8,128)(2,1)S(1)} %get-tuple-element.18), channel_id=1, source_target_pairs={{0,64},{1,3},{2,66},{3,5},{4,68},{5,7},{6,70},{7,1},{8,72},{9,11},... | collective-permute-start | bytes 1769480 | tf_op jit(solution)/shard_map/ppermute | solution.py:28
  166.3 9.3 %collective-permute-start.18 = (f16[64,1152]{1,0:T(8,128)(2,1)S(1)}, f16[64,1152]{1,0:T(8,128)(2,1)S(1)}, u32[]{:S(2)}, u32[]{:S(2)}) collective-permute-start(f16[64,1152]{1,0:T(8,128)(2,1)S(1)} %get-tuple-element.22), channel_id=1, source_target_pairs={{0,6},{1,73},{2,0},{3,75},{4,2},{5,77},{6,4},{7,79},{8,14},{9,65},... | collective-permute-start | bytes 442376 | tf_op jit(solution)/shard_map/ppermute | solution.py:28
  168.5 7.1 %collective-permute-start.17 = (f16[64,1152]{1,0:T(8,128)(2,1)S(1)}, f16[64,1152]{1,0:T(8,128)(2,1)S(1)}, u32[]{:S(2)}, u32[]{:S(2)}) collective-permute-start(f16[64,1152]{1,0:T(8,128)(2,1)S(1)} %get-tuple-element.23), channel_id=1, source_target_pairs={{0,4},{1,9},{2,6},{3,11},{4,0},{5,13},{6,2},{7,15},{8,12},{9,1},{1... | collective-permute-start | bytes 442376 | tf_op jit(solution)/shard_map/ppermute | solution.py:28
  169.1 6.8 %collective-permute-start.16 = (f16[64,1152]{1,0:T(8,128)(2,1)S(1)}, f16[64,1152]{1,0:T(8,128)(2,1)S(1)}, u32[]{:S(2)}, u32[]{:S(2)}) collective-permute-start(f16[64,1152]{1,0:T(8,128)(2,1)S(1)} %get-tuple-element.21), channel_id=1, source_target_pairs={{0,2},{1,65},{2,4},{3,67},{4,6},{5,69},{6,0},{7,71},{8,10},{9,73},... | collective-permute-start | bytes 442376 | tf_op jit(solution)/shard_map/ppermute | solution.py:28
  173.0 2.8 %copy-start.3 = (f32[64,1152]{1,0:T(8,128)S(1)}, f32[64,1152]{1,0:T(8,128)}, u32[]{:S(2)}) copy-start(f32[64,1152]{1,0:T(8,128)} %param.5) | copy-start | bytes 884740
  173.1 2.8 %copy-start.6 = (f32[64]{0:T(128)S(1)}, f32[64]{0:T(128)}, u32[]{:S(2)}) copy-start(f32[64]{0:T(128)} %copy-done.5) | copy-start | bytes 772
  173.4 13.2 %collective-permute-start.22 = (f16[256,1152]{1,0:T(8,128)(2,1)S(1)}, f16[256,1152]{1,0:T(8,128)(2,1)S(1)}, u32[]{:S(2)}, u32[]{:S(2)}) collective-permute-start(f16[256,1152]{1,0:T(8,128)(2,1)S(1)} %get-tuple-element.16), channel_id=1, source_target_pairs={{0,48},{1,49},{2,50},{3,51},{4,52},{5,53},{6,54},{7,55},{8,56},{9,... | collective-permute-start | bytes 1769480 | tf_op jit(solution)/shard_map/ppermute | solution.py:28
  174.8 14.6 %collective-permute-start.21 = (f16[256,1152]{1,0:T(8,128)(2,1)S(1)}, f16[256,1152]{1,0:T(8,128)(2,1)S(1)}, u32[]{:S(2)}, u32[]{:S(2)}) collective-permute-start(f16[256,1152]{1,0:T(8,128)(2,1)S(1)} %get-tuple-element.17), channel_id=1, source_target_pairs={{0,32},{1,33},{2,34},{3,35},{4,36},{5,37},{6,38},{7,39},{8,40},{9,... | collective-permute-start | bytes 1769480 | tf_op jit(solution)/shard_map/ppermute | solution.py:28
  175.6 28.6 %collective-permute-start.20 = (f16[256,1152]{1,0:T(8,128)(2,1)S(1)}, f16[256,1152]{1,0:T(8,128)(2,1)S(1)}, u32[]{:S(2)}, u32[]{:S(2)}) collective-permute-start(f16[256,1152]{1,0:T(8,128)(2,1)S(1)} %get-tuple-element.15), channel_id=1, source_target_pairs={{0,16},{1,17},{2,18},{3,19},{4,20},{5,21},{6,22},{7,23},{8,24},{9,... | collective-permute-start | bytes 1769480 | tf_op jit(solution)/shard_map/ppermute | solution.py:28
  175.9 28.3 %copy-start.1 = (f32[256,1152]{1,0:T(8,128)S(1)}, f32[256,1152]{1,0:T(8,128)}, u32[]{:S(2)}) copy-start(f32[256,1152]{1,0:T(8,128)} %param.6) | copy-start | bytes 3538948

commit v2 on v1

v2 whole, which is shorter than its diff:
```python
import functools
import math

import jax
import jax.numpy as jnp
from jax import lax
from jax.experimental import pallas as pl
from jax.experimental.pallas import tpu as pltpu
from jax.sharding import PartitionSpec as P

AXES = ("row", "col")
RING = 4
LOG2E = math.log2(math.e)
WIRE = jnp.float16


def place(index):
    row, col = index // 16, index % 16
    return (col // 2) % 4, row % 4, (col // 8) * 2 + row // 4, col % 2


def index_of(x, y, z, core):
    return ((z % 2) * 4 + y) * 16 + (z // 2) * 8 + x * 2 + core


def send(value, move):
    pairs = [(d, index_of(*move(*place(d)))) for d in range(128)]
    return lax.ppermute(value, AXES, pairs)


def along_y(step):
    return lambda x, y, z, c: (x, (y + step) % RING, z, c)


def along_first(step):
    return lambda x, y, z, c: ((x + step) % RING, y, z, c) if c == 0 else (x, y, (z + step) % RING, c)


def along_second(step):
    return lambda x, y, z, c: (x, y, (z + step) % RING, c) if c == 0 else ((x + step) % RING, y, z, c)


def swap(x, y, z, c):
    return x, y, z, 1 - c


def finish(unit_vals, inverse, direction):
    return inverse * (direction - unit_vals * jnp.sum(unit_vals * direction, axis=1, keepdims=True))


CHUNK = 256
BLOCK = 512
VMEM = pl.BlockSpec(memory_space=pltpu.VMEM)
SMEM = pl.BlockSpec(memory_space=pltpu.SMEM)
ANY = pl.BlockSpec(memory_space=pl.ANY)
HBM = pl.BlockSpec(memory_space=pltpu.HBM)


def prepare_kernel(text_ref, image_ref, text_bf, text_inv, image_bf, image_inv):
    for src, unit, inv in ((image_ref, image_bf, image_inv), (text_ref, text_bf, text_inv)):
        matrix = src[...]
        inverse = 1.0 / jnp.sqrt(jnp.sum(matrix * matrix, axis=1, keepdims=True) + 1e-06)
        inv[...] = inverse
        rows = (matrix * inverse).astype(jnp.bfloat16)
        if unit.ndim == 2:
            unit[...] = rows
        else:
            for i in range(unit.shape[0]):
                unit[i] = rows


def prepare(texts, images):
    return pl.pallas_call(
        prepare_kernel,
        out_shape=(
            jax.ShapeDtypeStruct((RING,) + texts.shape, jnp.bfloat16),
            jax.ShapeDtypeStruct((texts.shape[0], 1), jnp.float32),
            jax.ShapeDtypeStruct(images.shape, jnp.bfloat16),
            jax.ShapeDtypeStruct((images.shape[0], 1), jnp.float32),
        ),
        in_specs=[VMEM] * 2,
        out_specs=[VMEM] * 4,
    )(texts, images)


def nothing(*refs):
    pass


def held(value, others):
    return pl.pallas_call(
        nothing,
        out_shape=jax.ShapeDtypeStruct(value.shape, value.dtype),
        in_specs=[ANY] * (1 + len(others)),
        out_specs=ANY,
        input_output_aliases={0: 0},
    )(value, *others)


def after(value, others):
    for other in others:
        value = value + 0 * other[:1, : value.shape[1]].astype(value.dtype)
    return value


def pair_kernel(n_image, *refs):
    scale_ref, base_ref, pick_ref, match_ref = refs[:4]
    halves, images, refs = refs[4:6], refs[6 : 6 + n_image], refs[6 + n_image :]
    text_outs, image_outs = refs[:2], refs[2 : 2 + n_image]
    loss_out, text_buf, image_buf, weight_buf, sems = refs[2 + n_image :]
    n_cols, n_text = n_image, 2 * RING

    def tile(i):
        return pl.ds(pl.multiple_of(i * CHUNK, CHUNK), CHUNK)

    image_copies = [
        pltpu.make_async_copy(piece, image_buf.at[tile(i)], sems.at[n_text + i])
        for i, piece in enumerate(images)
    ]
    text_copies = [
        pltpu.make_async_copy(
            halves[t // RING].at[tile(pick_ref[t % RING])], text_buf.at[tile(t)], sems.at[t]
        )
        for t in range(n_text)
    ]
    for copy in text_copies[:1] + image_copies + text_copies[1:]:
        copy.start()
    slope, shift, temperature = scale_ref[0], scale_ref[1], scale_ref[2]
    loss_out[...] = jnp.zeros_like(loss_out)
    row_index = lax.broadcasted_iota(jnp.int32, (CHUNK, CHUNK), 0)

    for copy in image_copies:
        copy.wait()

    def weigh(t, carry):
        base = base_ref[t]
        pltpu.make_async_copy(text_buf.at[tile(t)], text_buf.at[tile(t)], sems.at[t]).wait()
        for i in range(n_cols):
            cols = pl.ds(i * CHUNK, CHUNK)
            scores = lax.dot_general(
                text_buf[tile(t), :],
                image_buf[cols, :],
                (((1,), (1,)), ((), ())),
                preferred_element_type=jnp.float32,
            )
            matched = (match_ref[:, cols] - base) == row_index
            power = scores * slope + shift
            grown = jnp.exp2(jnp.where(matched, -power, power))
            total = 1.0 + grown
            inv = pl.reciprocal(total, approx=True)
            inv = inv * (2.0 - total * inv)
            weight = (grown * temperature) * inv
            weight = jnp.where(matched, -weight, weight)
            weight_buf[tile(t), cols] = weight.astype(jnp.bfloat16)
            low, high = grown[: CHUNK // 2], grown[CHUNK // 2 :]
            joined = low + high + low * high
            low, high = joined[: CHUNK // 4], joined[CHUNK // 4 :]
            joined = low + high + low * high
            loss_out[...] += jnp.sum(jnp.log1p(joined).reshape(8, 8, CHUNK), axis=0)
        return carry

    lax.fori_loop(0, n_text, weigh, 0)

    for half, out in enumerate(text_outs):
        rows = pl.ds(half * RING * CHUNK, RING * CHUNK)
        out[...] = jnp.dot(
            weight_buf[rows, :], image_buf[...], preferred_element_type=jnp.float32
        )

    for i, out in enumerate(image_outs):
        out[...] = lax.dot_general(
            weight_buf[:, pl.ds(i * CHUNK, CHUNK)],
            text_buf[...],
            (((0,), (0,)), ((), ())),
            preferred_element_type=jnp.float32,
        )


def slow(*arrays):
    return [pltpu.with_memory_space_constraint(a, pltpu.HBM) for a in arrays]


def pair_block(scale, base, pick, match, mine, other, images):
    n_image, dim = len(images), mine.shape[1]
    n_rows, n_cols = 2 * RING * CHUNK, n_image * CHUNK
    out_shape = [jax.ShapeDtypeStruct((n_rows // 2, dim), jnp.float32)] * 2
    out_shape += [jax.ShapeDtypeStruct((CHUNK, dim), jnp.float32)] * n_image
    out_shape += [jax.ShapeDtypeStruct((8, CHUNK), jnp.float32)]
    out = pl.pallas_call(
        functools.partial(pair_kernel, n_image),
        out_shape=out_shape,
        in_specs=[SMEM, SMEM, SMEM, VMEM] + [HBM] * (2 + n_image),
        out_specs=[VMEM] * len(out_shape),
        scratch_shapes=[
            pltpu.VMEM((n_rows, dim), jnp.bfloat16),
            pltpu.VMEM((n_cols, dim), jnp.bfloat16),
            pltpu.VMEM((n_rows, n_cols), jnp.bfloat16),
            pltpu.SemaphoreType.DMA((2 * RING + n_image,)),
        ],
        compiler_params=pltpu.CompilerParams(vmem_limit_bytes=VMEM_LIMIT),
        cost_estimate=pl.CostEstimate(
            flops=6 * n_rows * n_cols * dim,
            bytes_accessed=2 * (n_rows + n_cols) * dim,
            transcendentals=2 * n_rows * n_cols,
        ),
    )(scale, base, pick, match, *slow(mine, other, *images))
    return out[0], out[1], out[2:-1], out[-1]


VMEM_LIMIT = 32 * 2**20


def total_loss(part):
    part = jnp.sum(part.reshape(-1, 128), axis=0)[None, None]
    parts = jnp.broadcast_to(part, (128, 1, 128))
    return jnp.sum(lax.all_to_all(parts, AXES, 0, 0, tiled=True))


def narrow(part):
    return (part * 0.25).astype(WIRE)


def wide(part):
    return part.astype(jnp.float32) * 4.0


def body(
    picture_vectors, caption_vectors, matching_captions, natural_exponent_coefficient, learned_shift
):
    me = lax.axis_index("row") * 16 + lax.axis_index("col")
    x, y, z, core = place(me)
    image_rows, text_rows = picture_vectors.shape[0], caption_vectors.shape[0]
    temperature = jnp.exp(natural_exponent_coefficient[0])
    scale = jnp.stack([temperature * LOG2E, learned_shift[0] * LOG2E, temperature])

    own, text_inv, image_bf, image_inv = prepare(caption_vectors, picture_vectors)

    rings = {}
    for d in range(128):
        at = place(d)
        rings.setdefault(at[:1] + at[2:], []).append(d)
    mine = lax.all_to_all(own, AXES, 0, 0, axis_index_groups=list(rings.values()), tiled=True)
    mine = mine.reshape(RING * text_rows, -1)
    line = jnp.concatenate([image_bf] + [send(image_bf, along_first(-r)) for r in (1, 2, 3)])
    image_up, image_down = send(line, along_second(-1)), send(line, along_second(1))
    image_far = send(line, along_second(2))
    images = [line, image_up, image_down, image_far]
    mine = held(mine, images)
    other = send(mine, swap)

    pick = (jnp.arange(RING, dtype=jnp.int32) + y) % RING
    mine_base = index_of(x, pick, z, core) * text_rows
    other_base = index_of(x, pick, z, 1 - core) * text_rows
    table = matching_captions.reshape(-1, image_rows)
    first = jnp.arange(RING, dtype=jnp.int32)[None, :]
    second = jnp.array([0, 1, 3, 2], dtype=jnp.int32)[:, None]
    owners = jnp.where(
        core == 0,
        index_of((x + first) % RING, y, (z + second) % RING, core),
        index_of((x + second) % RING, y, (z + first) % RING, core),
    )
    match = jnp.take(table, owners.reshape(-1), axis=0).reshape(1, -1)

    n = text_rows
    base = jnp.concatenate([mine_base, other_base])
    mine, other, parts, loss = pair_block(scale, base, pick, match, mine, other, images)
    n = text_rows
    other = send(narrow(other), swap)
    wires = [
        narrow(mine[s * n : (s + 1) * n] + wide(other[s * n : (s + 1) * n])) for s in (1, 3, 2)
    ]
    text_dir = mine[:n] + wide(other[:n])
    for s, wire in zip((1, 3, 2), wires):
        text_dir = text_dir + wide(send(wire, along_y(s)))

    line_dir, up_part, down_part, far_part = parts
    far_part = held(far_part, [wide(wires[0][:8, :128])])
    for s, part in ((1, up_part), (3, down_part), (2, far_part)):
        line_dir = line_dir + wide(send(narrow(part), along_second(s)))
    loss = total_loss(after(loss, [line_dir]))
    n = image_rows
    wire = narrow(line_dir[n:])
    image_dir = line_dir[:n]
    for r in (1, 2, 3):
        image_dir = image_dir + wide(send(wire[(r - 1) * n : r * n], along_first(r)))

    grad_images = finish(picture_vectors * image_inv, image_inv, image_dir)
    grad_texts = finish(caption_vectors * text_inv, text_inv, text_dir)
    loss = loss / matching_captions.shape[0]
    return (grad_images, grad_texts, loss)


def solution(mesh):
    placed = (P(AXES, None), P(AXES, None), P(), P(), P())
    return jax.shard_map(
        body,
        mesh=mesh,
        in_specs=placed,
        out_specs=(P(AXES, None), P(AXES, None), P()),
        check_vma=False,
    )
```

time: 208 us -> 128 us (0.62)
  blocking collectives: 71.8 us -> 0 us
  waiting for transfers between devices: 48.6 us -> 22.4 us
  starting transfers between devices: 26.8 us -> 46.4 us
  local copies, waits for them, and re-layouts: 11.2 us -> 7.05 us
    psum x1 -> x0, blocking collectives: 71.8 us -> none  [body(): loss = lax.psum(jnp.sum(loss_part), AXES) / matching_captions.shape[0]]
    ppermute x23 -> x17, waiting for transfers between devices: 48.6 us -> 21.3 us  [send(): return lax.ppermute(value, AXES, pairs)]
    all_to_all x0 -> x2, starting transfers between devices: none -> 15.1 us  [the longest x1 9.99 us: total_loss(): return jnp.sum(lax.all_to_all(parts, AXES, 0, 0, tiled=True))]
    another operation x3 -> x0, other arithmetic: 5.68 us -> none
    slice x3 -> x1, local copies, waits for them, and re-layouts: 6.93 us -> 1.85 us  [body(): image_dir = image_dir + wide(send(wire[(r - 1) * n:r * n], along_first(r)))]
    ppermute x23 -> x17, starting transfers between devices: 26.8 us -> 31.2 us  [send(): return lax.ppermute(value, AXES, pairs)]
    reduce_sum x2, other arithmetic: 0.68 us -> 3.66 us  [finish(): jnp.sum(unit_vals * direction, axis=1, keepdims=True)]
    mul x2, other arithmetic: 2.31 us -> 5.28 us  [finish(): inverse * (direction - unit_vals * jnp.sum(unit_vals * direction, axis=1,...]
  transfers between devices with their start and end apart: 23 -> 19, of which waited for: 6 -> 8; matrix products, arithmetic and copies ran while one was open for 8% -> 16% of each run, Pallas kernels for 0% -> 0%
where the time goes in v2:
time: 128 us
  starting transfers between devices  46.4 us (36%)
  Pallas kernels  28 us (22%)
  waiting for transfers between devices  22.4 us (18%)
  other arithmetic  19.8 us (15%)
  local copies, waits for them, and re-layouts  7.05 us (6%)
  between operations  3.98 us (3%)
    ppermute x17, starting transfers between devices, send(): return lax.ppermute(value, AXES, pairs)  31.2 us
    pallas_call x1, Pallas kernels, pair_block(): pl.pallas_call(functools.partial(pair_kernel, n_image), out_shape=out_sha...  24.8 us
    ppermute x17, waiting for transfers between devices, send(): return lax.ppermute(value, AXES, pairs)  21.3 us
    all_to_all x1, starting transfers between devices, total_loss(): return jnp.sum(lax.all_to_all(parts, AXES, 0, 0, tiled=True))  9.99 us
    convert_element_type x6, other arithmetic, narrow(): return (part * 0.25).astype(WIRE)  5.74 us
    mul x2, other arithmetic, finish(): inverse * (direction - unit_vals * jnp.sum(unit_vals * direction, axis=1,...  5.28 us
    all_to_all x1, starting transfers between devices, body(): lax.all_to_all(own, AXES, 0, 0, axis_index_groups=list(rings.values()), t...  5.15 us
    reduce_sum x2, other arithmetic, finish(): jnp.sum(unit_vals * direction, axis=1, keepdims=True)  3.66 us
  transfers between devices with their start and end apart: 19, of which 8 were waited for; matrix products, arithmetic and copies ran while one was open for 16% of the time, Pallas kernels for 0%

profile of v2, /device:TPU:1, one launch (start us, length us, event | category | flops | bytes accessed | tf_op | source)
XLA Modules:
  0.0 127.6 jit_solution(6200393471253880067)
XLA Ops:
  0.6 3.2 %shard_map.85 = (bf16[4,256,1152]{2,1,0:T(8,128)(2,1)}, f32[256,1]{1,0:T(8,128)}, bf16[64,1152]{1,0:T(8,128)(2,1)}, f32[64,1]{1,0:T(8,128)}) custom-call(f32[256,1152]{1,0:T(8,128)} %text_ref.1, f32[64,1152]{1,0:T(8,128)} %image_ref.1), custom_call_target="tpu_custom_call" | custom-call | tf_op jit(solution)/shard_map/pallas_call | solution.py:73
  3.8 5.1 %all-to-all-start = ((bf16[4,256,1152]{2,1,0:T(8,128)(2,1)}), bf16[4,256,1152]{2,1,0:T(8,128)(2,1)S(1)}, u32[]{:S(2)}, u32[]{:S(2)}) async-start(bf16[4,256,1152]{2,1,0:T(8,128)(2,1)} %get-tuple-element.15), calls=%async_computation | async-start | bytes 4718592 | tf_op jit(solution)/shard_map/all_to_all | solution.py:242
  8.9 1.6 %collective-permute-start.2 = (bf16[64,1152]{1,0:T(8,128)(2,1)S(1)}, bf16[64,1152]{1,0:T(8,128)(2,1)S(1)}, u32[]{:S(2)}, u32[]{:S(2)}) collective-permute-start(bf16[64,1152]{1,0:T(8,128)(2,1)S(1)} %copy-done.9), channel_id=1, source_target_pairs={{0,2},{1,65},{2,4},{3,67},{4,6},{5,69},{6,0},{7,71},{8,10},{9,73},... | collective-permute-start | bytes 442376 | tf_op jit(solution)/shard_map/ppermute | solution.py:28
  10.6 3.3 %collective-permute-start.1 = (bf16[64,1152]{1,0:T(8,128)(2,1)S(1)}, bf16[64,1152]{1,0:T(8,128)(2,1)S(1)}, u32[]{:S(2)}, u32[]{:S(2)}) collective-permute-start(bf16[64,1152]{1,0:T(8,128)(2,1)S(1)} %copy-done.9), channel_id=1, source_target_pairs={{0,4},{1,9},{2,6},{3,11},{4,0},{5,13},{6,2},{7,15},{8,12},{9,1},{1... | collective-permute-start | bytes 442376 | tf_op jit(solution)/shard_map/ppermute | solution.py:28
  14.6 3.5 %collective-permute-done = bf16[64,1152]{1,0:T(8,128)(2,1)S(1)} collective-permute-done((bf16[64,1152]{1,0:T(8,128)(2,1)S(1)}, bf16[64,1152]{1,0:T(8,128)(2,1)S(1)}, u32[]{:S(2)}, u32[]{:S(2)}) %collective-permute-start) | collective-permute-done | bytes 147488 | tf_op jit(solution)/shard_map/ppermute | solution.py:28
  18.4 2.7 %collective-permute-start.5 = (bf16[256,1152]{1,0:T(8,128)(2,1)S(1)}, bf16[256,1152]{1,0:T(8,128)(2,1)S(1)}, u32[]{:S(2)}, u32[]{:S(2)}) collective-permute-start(bf16[256,1152]{1,0:T(8,128)(2,1)S(1)} %constant_dynamic-update-slice_fusion.refs_1_.refs_6_), channel_id=1, source_target_pairs={{0,8},{1,5},{2,10},{3,7},{4,12},{5,1},{6,14},{7,3},{8,0},{9,13},{1... | collective-permute-start | bytes 1769480 | tf_op jit(solution)/shard_map/ppermute | solution.py:28
  21.4 2.4 %collective-permute-start.3 = (bf16[256,1152]{1,0:T(8,128)(2,1)S(1)}, bf16[256,1152]{1,0:T(8,128)(2,1)}, u32[]{:S(2)}, u32[]{:S(2)}) collective-permute-start(bf16[256,1152]{1,0:T(8,128)(2,1)S(1)} %constant_dynamic-update-slice_fusion.refs_1_.refs_6_), channel_id=1, source_target_pairs={{0,72},{1,7},{2,74},{3,1},{4,76},{5,3},{6,78},{7,5},{8,64},{9,15},... | collective-permute-start | bytes 1769480 | tf_op jit(solution)/shard_map/ppermute | solution.py:28
  23.8 5.2 %collective-permute-done.5.refs_4_.refs_9_ = bf16[256,1152]{1,0:T(8,128)(2,1)S(1)} collective-permute-done((bf16[256,1152]{1,0:T(8,128)(2,1)S(1)}, bf16[256,1152]{1,0:T(8,128)(2,1)S(1)}, u32[]{:S(2)}, u32[]{:S(2)}) %collective-permute-start.5) | collective-permute-done | bytes 589856 | tf_op jit(solution)/shard_map/ppermute | solution.py:28
  29.0 6.3 %collective-permute-done.4.refs_3_.refs_8_ = bf16[256,1152]{1,0:T(8,128)(2,1)S(1)} collective-permute-done((bf16[256,1152]{1,0:T(8,128)(2,1)S(1)}, bf16[256,1152]{1,0:T(8,128)(2,1)S(1)}, u32[]{:S(2)}, u32[]{:S(2)}) %collective-permute-start.4) | collective-permute-done | bytes 589856 | tf_op jit(solution)/shard_map/ppermute | solution.py:28
  37.2 1.4 %copy-done.3 = bf16[4,256,1152]{2,1,0:T(8,128)(2,1)} copy-done((bf16[4,256,1152]{2,1,0:T(8,128)(2,1)}, bf16[4,256,1152]{2,1,0:T(8,128)(2,1)S(1)}, u32[]{:S(2)}) %copy-start.3) | copy-done | bytes 2359320
  38.6 1.9 %collective-permute-start.6 = (bf16[1024,1152]{1,0:T(8,128)(2,1)}, bf16[1024,1152]{1,0:T(8,128)(2,1)}, u32[]{:S(2)}, u32[]{:S(2)}) collective-permute-start(bf16[1024,1152]{1,0:T(8,128)(2,1)} %shard_map.86.refs_4_), channel_id=1, source_target_pairs={{0,1},{1,0},{2,3},{3,2},{4,5},{5,4},{6,7},{7,6},{8,9},{9,8},{10,11... | collective-permute-start | bytes 7077896 | tf_op jit(solution)/shard_map/ppermute | solution.py:28
  45.0 24.8 %shard_map.87 = (f32[1024,1152]{1,0:T(8,128)S(1)}, f32[1024,1152]{1,0:T(8,128)S(1)}, f32[256,1152]{1,0:T(8,128)S(1)}, f32[256,1152]{1,0:T(8,128)S(1)}, f32[256,1...) custom-call(f32[3]{0:T(128)S(1)} %pad_maximum_fusion.refs_0_, s32[8]{0:T(128)S(1)} %pad_add_fusion.refs_1_, ...), custom_call_target="tpu_custom_call" | custom-call | flops 14495514624 | bytes 7077888 | tf_op jit(solution)/shard_map/pallas_call | solution.py:189
  71.3 2.5 %collective-permute-start.8 = (f16[256,1152]{1,0:T(8,128)(2,1)S(1)}, f16[256,1152]{1,0:T(8,128)(2,1)}, u32[]{:S(2)}, u32[]{:S(2)}) collective-permute-start(f16[256,1152]{1,0:T(8,128)(2,1)S(1)} %multiply_convert_fusion.5), channel_id=1, source_target_pairs={{0,72},{1,7},{2,74},{3,1},{4,76},{5,3},{6,78},{7,5},{8,64},{9,15},... | collective-permute-start | bytes 1769480 | tf_op jit(solution)/shard_map/ppermute | solution.py:28
  74.3 1.1 collective-permute-done.9
  75.4 2.0 %multiply_convert_fusion.2 = (f16[256,1152]{1,0:T(8,128)(2,1)}, f16[256,1152]{1,0:T(8,128)(2,1)}, f16[256,1152]{1,0:T(8,128)(2,1)}) fusion(f32[1024,1152]{1,0:T(8,128)S(1)} %get-tuple-element.21, f16[1024,1152]{1,0:T(8,128)(2,1)S(1)} %collective-permute-done.9), kind=kLoop, calls=%fused_computation.6 | loop fusion | flops 4423680 | bytes 7077888 | tf_op jit(solution)/shard_map/convert_element_type | solution.py:220
  77.4 1.3 convert_multiply_fusion.refs_1_
  78.6 2.2 %multiply_convert_fusion.3 = f16[256,1152]{1,0:T(8,128)(2,1)} fusion(f32[256,1152]{1,0:T(8,128)} %shard_map.88), kind=kLoop, calls=%fused_computation.8 | loop fusion | flops 589824 | bytes 1769472 | tf_op jit(solution)/shard_map/convert_element_type | solution.py:220
  80.9 2.7 %collective-permute-start.10 = (f16[256,1152]{1,0:T(8,128)(2,1)}, f16[256,1152]{1,0:T(8,128)(2,1)}, u32[]{:S(2)}, u32[]{:S(2)}) collective-permute-start(f16[256,1152]{1,0:T(8,128)(2,1)} %multiply_convert_fusion.3), channel_id=1, source_target_pairs={{0,8},{1,5},{2,10},{3,7},{4,12},{5,1},{6,14},{7,3},{8,0},{9,13},{1... | collective-permute-start | bytes 1769480 | tf_op jit(solution)/shard_map/ppermute | solution.py:28
  84.8 1.8 %collective-permute-start.15 = (f16[256,1152]{1,0:T(8,128)(2,1)}, f16[256,1152]{1,0:T(8,128)(2,1)}, u32[]{:S(2)}, u32[]{:S(2)}) collective-permute-start(f16[256,1152]{1,0:T(8,128)(2,1)} %get-tuple-element.27), channel_id=1, source_target_pairs={{0,48},{1,49},{2,50},{3,51},{4,52},{5,53},{6,54},{7,55},{8,56},{9,... | collective-permute-start | bytes 1769480 | tf_op jit(solution)/shard_map/ppermute | solution.py:28
  86.6 1.1 collective-permute-start.16
  87.7 4.0 %collective-permute-done.10 = f16[256,1152]{1,0:T(8,128)(2,1)} collective-permute-done((f16[256,1152]{1,0:T(8,128)(2,1)}, f16[256,1152]{1,0:T(8,128)(2,1)}, u32[]{:S(2)}, u32[]{:S(2)}) %collective-permute-start.10) | collective-permute-done | bytes 589856 | tf_op jit(solution)/shard_map/ppermute | solution.py:28
  91.7 1.8 %multiply_add_fusion.1 = f32[256,1152]{1,0:T(8,128)S(1)} fusion(f16[256,1152]{1,0:T(8,128)(2,1)} %collective-permute-done.10, f16[256,1152]{1,0:T(8,128)(2,1)} %collective-permute-done.8, f32[256,1152]{1,0:T(8,128)S(1)} %get-tuple-element.17, f16[256,1152]{1,0:T(8,128)(2,1)} %collective-permute-done.7), kind=kLoop, calls=%fused_computation.7 | loop fusion | flops 2654208 | bytes 4128768 | tf_op jit(solution)/shard_map/add | solution.py:279
  95.1 10.0 %all-to-all-start.1 = ((f32[128,1,128]{2,1,0:T(1,128)}), f32[128,1,128]{2,1,0:T(1,128)}, u32[]{:S(2)}, u32[]{:S(2)}) async-start(f32[128,1,128]{2,1,0:T(1,128)} %broadcast_in_dim.22), calls=%async_computation.1 | async-start | bytes 131072 | tf_op jit(solution)/shard_map/all_to_all | solution.py:216
  105.1 1.8 %fusion.19 = (f16[64,1152]{1,0:T(8,128)(2,1)}, f16[64,1152]{1,0:T(8,128)(2,1)}, f16[64,1152]{1,0:T(8,128)(2,1)}) fusion(f16[192,1152]{1,0:T(8,128)(2,1)} %fusion), kind=kLoop, calls=%fused_computation.78 | loop fusion | bytes 884736 | tf_op jit(solution)/shard_map/slice | solution.py:285
  106.9 1.5 %collective-permute-start.11 = (f16[64,1152]{1,0:T(8,128)(2,1)}, f16[64,1152]{1,0:T(8,128)(2,1)S(1)}, u32[]{:S(2)}, u32[]{:S(2)}) collective-permute-start(f16[64,1152]{1,0:T(8,128)(2,1)} %get-tuple-element.30), channel_id=1, source_target_pairs={{0,2},{1,65},{2,4},{3,67},{4,6},{5,69},{6,0},{7,71},{8,10},{9,73},... | collective-permute-start | bytes 442376 | tf_op jit(solution)/shard_map/ppermute | solution.py:28
  108.4 1.8 %collective-permute-start.13 = (f16[64,1152]{1,0:T(8,128)(2,1)}, f16[64,1152]{1,0:T(8,128)(2,1)S(1)}, u32[]{:S(2)}, u32[]{:S(2)}) collective-permute-start(f16[64,1152]{1,0:T(8,128)(2,1)} %get-tuple-element.31), channel_id=1, source_target_pairs={{0,6},{1,73},{2,0},{3,75},{4,2},{5,77},{6,4},{7,79},{8,14},{9,65},... | collective-permute-start | bytes 442376 | tf_op jit(solution)/shard_map/ppermute | solution.py:28
  110.2 5.2 %collective-permute-start.12 = (f16[64,1152]{1,0:T(8,128)(2,1)}, f16[64,1152]{1,0:T(8,128)(2,1)}, u32[]{:S(2)}, u32[]{:S(2)}) collective-permute-start(f16[64,1152]{1,0:T(8,128)(2,1)} %get-tuple-element.32), channel_id=1, source_target_pairs={{0,4},{1,9},{2,6},{3,11},{4,0},{5,13},{6,2},{7,15},{8,12},{9,1},{1... | collective-permute-start | bytes 442376 | tf_op jit(solution)/shard_map/ppermute | solution.py:28
  115.4 2.5 %multiply_reduce_fusion = f32[256]{0:T(256)S(1)} fusion(f32[256,1152]{1,0:T(8,128)S(1)} %copy-done.2, f32[256]{0:T(256)S(1)} %reduce.1, f16[256,1152]{1,0:T(8,128)(2,1)} %collective-permute-done.16, f16[256,1152]{1,0:T(8,128)(2,1)} %collective-permute-done.15, f16[256,1152]{1,0:T(8,128)(2,1)S(1)} %collective-permute-done.14, f16[1024,1152]{1,0:T(8,128)(2,1)} %copy-done.4, ...), kind=kLoop, calls=%fused_computation.3 | loop fusion | flops 4423424 | bytes 4720640 | tf_op jit(solution)/shard_map/reduce_sum | solution.py:48
  117.9 3.5 %subtract_multiply_fusion = f32[256,1152]{1,0:T(8,128)} fusion(f32[256,1152]{1,0:T(8,128)S(1)} %copy-done.2, f32[256]{0:T(256)S(1)} %multiply_reduce_fusion, f32[256]{0:T(256)S(1)} %reduce.1, f16[256,1152]{1,0:T(8,128)(2,1)} %collective-permute-done.16, f16[256,1152]{1,0:T(8,128)(2,1)} %collective-permute-done.15, ...), kind=kLoop, calls=%fused_computation.2 | loop fusion | flops 4718592 | bytes 5900288 | tf_op jit(solution)/shard_map/mul | solution.py:48
  121.4 1.5 %reduce_sum.39 = f32[]{:T(128)} reduce(f32[128,1,128]{2,0,1:T(8,128)} %bitcast.3, f32[]{:T(128)} %constant.207.clone.1), dimensions={0,1,2}, to_apply=%region_3.4 | reduce | flops 16383 | bytes 65544 | tf_op jit(solution)/shard_map/reduce_sum | solution.py:216
  123.6 1.1 multiply_reduce_fusion.1
  124.7 1.8 %subtract_multiply_fusion.1 = f32[64,1152]{1,0:T(8,128)} fusion(f32[64,1152]{1,0:T(8,128)S(1)} %copy-done.5, f32[64]{0:T(128)S(1)} %multiply_reduce_fusion.1, f32[64]{0:T(128)S(1)} %reduce, f16[64,1152]{1,0:T(8,128)(2,1)S(1)} %collective-permute-done.13, f16[64,1152]{1,0:T(8,128)(2,1)} %collective-permute-done.12, ...), kind=kLoop, calls=%fused_computation.17 | loop fusion | flops 958464 | bytes 1327616 | tf_op jit(solution)/shard_map/mul | solution.py:48
  (77 shorter events, 10.8 us)
Async XLA Ops:
  3.8 5.2 %copy-start.9 = (bf16[64,1152]{1,0:T(8,128)(2,1)S(1)}, bf16[64,1152]{1,0:T(8,128)(2,1)}, u32[]{:S(2)}) copy-start(bf16[64,1152]{1,0:T(8,128)(2,1)} %get-tuple-element.16) | copy-start | bytes 442372
  3.8 33.4 %all-to-all-start = ((bf16[4,256,1152]{2,1,0:T(8,128)(2,1)}), bf16[4,256,1152]{2,1,0:T(8,128)(2,1)S(1)}, u32[]{:S(2)}, u32[]{:S(2)}) async-start(bf16[4,256,1152]{2,1,0:T(8,128)(2,1)} %get-tuple-element.15), calls=%async_computation | async-start | bytes 4718592 | tf_op jit(solution)/shard_map/all_to_all | solution.py:242
  8.9 9.4 %collective-permute-start.2 = (bf16[64,1152]{1,0:T(8,128)(2,1)S(1)}, bf16[64,1152]{1,0:T(8,128)(2,1)S(1)}, u32[]{:S(2)}, u32[]{:S(2)}) collective-permute-start(bf16[64,1152]{1,0:T(8,128)(2,1)S(1)} %copy-done.9), channel_id=1, source_target_pairs={{0,2},{1,65},{2,4},{3,67},{4,6},{5,69},{6,0},{7,71},{8,10},{9,73},... | collective-permute-start | bytes 442376 | tf_op jit(solution)/shard_map/ppermute | solution.py:28
  10.6 7.7 %collective-permute-start.1 = (bf16[64,1152]{1,0:T(8,128)(2,1)S(1)}, bf16[64,1152]{1,0:T(8,128)(2,1)S(1)}, u32[]{:S(2)}, u32[]{:S(2)}) collective-permute-start(bf16[64,1152]{1,0:T(8,128)(2,1)S(1)} %copy-done.9), channel_id=1, source_target_pairs={{0,4},{1,9},{2,6},{3,11},{4,0},{5,13},{6,2},{7,15},{8,12},{9,1},{1... | collective-permute-start | bytes 442376 | tf_op jit(solution)/shard_map/ppermute | solution.py:28
  13.9 4.3 %collective-permute-start = (bf16[64,1152]{1,0:T(8,128)(2,1)S(1)}, bf16[64,1152]{1,0:T(8,128)(2,1)S(1)}, u32[]{:S(2)}, u32[]{:S(2)}) collective-permute-start(bf16[64,1152]{1,0:T(8,128)(2,1)S(1)} %copy-done.9), channel_id=1, source_target_pairs={{0,6},{1,73},{2,0},{3,75},{4,2},{5,77},{6,4},{7,79},{8,14},{9,65},... | collective-permute-start | bytes 442376 | tf_op jit(solution)/shard_map/ppermute | solution.py:28
  18.3 18.8 %copy-start.6 = (bf16[256,1152]{1,0:T(8,128)(2,1)}, bf16[256,1152]{1,0:T(8,128)(2,1)S(1)}, u32[]{:S(2)}) copy-start(bf16[256,1152]{1,0:T(8,128)(2,1)S(1)} %constant_dynamic-update-slice_fusion.refs_1_.refs_6_) | copy-start | bytes 1769476
  18.4 10.7 %collective-permute-start.5 = (bf16[256,1152]{1,0:T(8,128)(2,1)S(1)}, bf16[256,1152]{1,0:T(8,128)(2,1)S(1)}, u32[]{:S(2)}, u32[]{:S(2)}) collective-permute-start(bf16[256,1152]{1,0:T(8,128)(2,1)S(1)} %constant_dynamic-update-slice_fusion.refs_1_.refs_6_), channel_id=1, source_target_pairs={{0,8},{1,5},{2,10},{3,7},{4,12},{5,1},{6,14},{7,3},{8,0},{9,13},{1... | collective-permute-start | bytes 1769480 | tf_op jit(solution)/shard_map/ppermute | solution.py:28
  21.1 14.2 %collective-permute-start.4 = (bf16[256,1152]{1,0:T(8,128)(2,1)S(1)}, bf16[256,1152]{1,0:T(8,128)(2,1)S(1)}, u32[]{:S(2)}, u32[]{:S(2)}) collective-permute-start(bf16[256,1152]{1,0:T(8,128)(2,1)S(1)} %constant_dynamic-update-slice_fusion.refs_1_.refs_6_), channel_id=1, source_target_pairs={{0,64},{1,3},{2,66},{3,5},{4,68},{5,7},{6,70},{7,1},{8,72},{9,11},... | collective-permute-start | bytes 1769480 | tf_op jit(solution)/shard_map/ppermute | solution.py:28
  21.4 14.7 %collective-permute-start.3 = (bf16[256,1152]{1,0:T(8,128)(2,1)S(1)}, bf16[256,1152]{1,0:T(8,128)(2,1)}, u32[]{:S(2)}, u32[]{:S(2)}) collective-permute-start(bf16[256,1152]{1,0:T(8,128)(2,1)S(1)} %constant_dynamic-update-slice_fusion.refs_1_.refs_6_), channel_id=1, source_target_pairs={{0,72},{1,7},{2,74},{3,1},{4,76},{5,3},{6,78},{7,5},{8,64},{9,15},... | collective-permute-start | bytes 1769480 | tf_op jit(solution)/shard_map/ppermute | solution.py:28
  29.0 8.2 %copy-start.7 = (bf16[256,1152]{1,0:T(8,128)(2,1)}, bf16[256,1152]{1,0:T(8,128)(2,1)S(1)}, u32[]{:S(2)}) copy-start(bf16[256,1152]{1,0:T(8,128)(2,1)S(1)} %collective-permute-done.5.refs_4_.refs_9_) | copy-start | bytes 1769476
  35.3 0.8 copy-start.8
  37.2 1.4 %copy-start.3 = (bf16[4,256,1152]{2,1,0:T(8,128)(2,1)}, bf16[4,256,1152]{2,1,0:T(8,128)(2,1)S(1)}, u32[]{:S(2)}) copy-start(bf16[4,256,1152]{2,1,0:T(8,128)(2,1)S(1)} %all-to-all-done) | copy-start | bytes 7077892
  38.6 1.9 %copy-start.12 = (s32[4]{0:T(128)S(1)}, s32[4]{0:T(128)}, u32[]{:S(2)}) copy-start(s32[4]{0:T(128)} %constant.209.clone) | copy-start | bytes 52
  38.6 6.4 %collective-permute-start.6 = (bf16[1024,1152]{1,0:T(8,128)(2,1)}, bf16[1024,1152]{1,0:T(8,128)(2,1)}, u32[]{:S(2)}, u32[]{:S(2)}) collective-permute-start(bf16[1024,1152]{1,0:T(8,128)(2,1)} %shard_map.86.refs_4_), channel_id=1, source_target_pairs={{0,1},{1,0},{2,3},{3,2},{4,5},{5,4},{6,7},{7,6},{8,9},{9,8},{10,11... | collective-permute-start | bytes 7077896 | tf_op jit(solution)/shard_map/ppermute | solution.py:28
  69.8 1.0 copy-start.1
  69.8 5.5 %copy-start = (f32[1024,1152]{1,0:T(8,128)}, f32[1024,1152]{1,0:T(8,128)S(1)}, u32[]{:S(2)}) copy-start(f32[1024,1152]{1,0:T(8,128)S(1)} %get-tuple-element.21) | copy-start | bytes 14155780
  70.8 4.5 %collective-permute-start.9 = (f16[1024,1152]{1,0:T(8,128)(2,1)S(1)}, f16[1024,1152]{1,0:T(8,128)(2,1)S(1)}, u32[]{:S(2)}, u32[]{:S(2)}) collective-permute-start(f16[1024,1152]{1,0:T(8,128)(2,1)S(1)} %multiply_convert_fusion), channel_id=1, source_target_pairs={{0,1},{1,0},{2,3},{3,2},{4,5},{5,4},{6,7},{7,6},{8,9},{9,8},{10,11... | collective-permute-start | bytes 7077896 | tf_op jit(solution)/shard_map/ppermute | solution.py:28
  71.3 15.3 %collective-permute-start.8 = (f16[256,1152]{1,0:T(8,128)(2,1)S(1)}, f16[256,1152]{1,0:T(8,128)(2,1)}, u32[]{:S(2)}, u32[]{:S(2)}) collective-permute-start(f16[256,1152]{1,0:T(8,128)(2,1)S(1)} %multiply_convert_fusion.5), channel_id=1, source_target_pairs={{0,72},{1,7},{2,74},{3,1},{4,76},{5,3},{6,78},{7,5},{8,64},{9,15},... | collective-permute-start | bytes 1769480 | tf_op jit(solution)/shard_map/ppermute | solution.py:28
  74.0 13.8 %collective-permute-start.7 = (f16[256,1152]{1,0:T(8,128)(2,1)S(1)}, f16[256,1152]{1,0:T(8,128)(2,1)}, u32[]{:S(2)}, u32[]{:S(2)}) collective-permute-start(f16[256,1152]{1,0:T(8,128)(2,1)S(1)} %multiply_convert_fusion.6), channel_id=1, source_target_pairs={{0,64},{1,3},{2,66},{3,5},{4,68},{5,7},{6,70},{7,1},{8,72},{9,11},... | collective-permute-start | bytes 1769480 | tf_op jit(solution)/shard_map/ppermute | solution.py:28
  75.4 2.0 %copy-start.4 = (f16[1024,1152]{1,0:T(8,128)(2,1)}, f16[1024,1152]{1,0:T(8,128)(2,1)S(1)}, u32[]{:S(2)}) copy-start(f16[1024,1152]{1,0:T(8,128)(2,1)S(1)} %collective-permute-done.9) | copy-start | bytes 7077892
  78.6 5.0 %copy-start.11 = (f32[64,1]{1,0:T(8,128)S(1)}, f32[64,1]{1,0:T(8,128)}, u32[]{:S(2)}) copy-start(f32[64,1]{1,0:T(8,128)} %get-tuple-element.14) | copy-start | bytes 772
  78.6 5.1 %copy-start.10 = (f32[256,1]{1,0:T(8,128)S(1)}, f32[256,1]{1,0:T(8,128)}, u32[]{:S(2)}) copy-start(f32[256,1]{1,0:T(8,128)} %get-tuple-element.23) | copy-start | bytes 3076
  80.9 10.8 %collective-permute-start.10 = (f16[256,1152]{1,0:T(8,128)(2,1)}, f16[256,1152]{1,0:T(8,128)(2,1)}, u32[]{:S(2)}, u32[]{:S(2)}) collective-permute-start(f16[256,1152]{1,0:T(8,128)(2,1)} %multiply_convert_fusion.3), channel_id=1, source_target_pairs={{0,8},{1,5},{2,10},{3,7},{4,12},{5,1},{6,14},{7,3},{8,0},{9,13},{1... | collective-permute-start | bytes 1769480 | tf_op jit(solution)/shard_map/ppermute | solution.py:28
  83.8 31.5 %collective-permute-start.14 = (f16[256,1152]{1,0:T(8,128)(2,1)}, f16[256,1152]{1,0:T(8,128)(2,1)S(1)}, u32[]{:S(2)}, u32[]{:S(2)}) collective-permute-start(f16[256,1152]{1,0:T(8,128)(2,1)} %get-tuple-element.29), channel_id=1, source_target_pairs={{0,16},{1,17},{2,18},{3,19},{4,20},{5,21},{6,22},{7,23},{8,24},{9,... | collective-permute-start | bytes 1769480 | tf_op jit(solution)/shard_map/ppermute | solution.py:28
  84.8 25.4 %collective-permute-start.15 = (f16[256,1152]{1,0:T(8,128)(2,1)}, f16[256,1152]{1,0:T(8,128)(2,1)}, u32[]{:S(2)}, u32[]{:S(2)}) collective-permute-start(f16[256,1152]{1,0:T(8,128)(2,1)} %get-tuple-element.27), channel_id=1, source_target_pairs={{0,48},{1,49},{2,50},{3,51},{4,52},{5,53},{6,54},{7,55},{8,56},{9,... | collective-permute-start | bytes 1769480 | tf_op jit(solution)/shard_map/ppermute | solution.py:28
  86.6 28.8 %collective-permute-start.16 = (f16[256,1152]{1,0:T(8,128)(2,1)}, f16[256,1152]{1,0:T(8,128)(2,1)}, u32[]{:S(2)}, u32[]{:S(2)}) collective-permute-start(f16[256,1152]{1,0:T(8,128)(2,1)} %get-tuple-element.28), channel_id=1, source_target_pairs={{0,32},{1,33},{2,34},{3,35},{4,36},{5,37},{6,38},{7,39},{8,40},{9,... | collective-permute-start | bytes 1769480 | tf_op jit(solution)/shard_map/ppermute | solution.py:28
  93.5 21.8 %copy-start.2 = (f32[256,1152]{1,0:T(8,128)S(1)}, f32[256,1152]{1,0:T(8,128)}, u32[]{:S(2)}) copy-start(f32[256,1152]{1,0:T(8,128)} %text_ref.1) | copy-start | bytes 3538948
  95.1 26.3 %all-to-all-start.1 = ((f32[128,1,128]{2,1,0:T(1,128)}), f32[128,1,128]{2,1,0:T(1,128)}, u32[]{:S(2)}, u32[]{:S(2)}) async-start(f32[128,1,128]{2,1,0:T(1,128)} %broadcast_in_dim.22), calls=%async_computation.1 | async-start | bytes 131072 | tf_op jit(solution)/shard_map/all_to_all | solution.py:216
  106.9 16.6 %collective-permute-start.11 = (f16[64,1152]{1,0:T(8,128)(2,1)}, f16[64,1152]{1,0:T(8,128)(2,1)S(1)}, u32[]{:S(2)}, u32[]{:S(2)}) collective-permute-start(f16[64,1152]{1,0:T(8,128)(2,1)} %get-tuple-element.30), channel_id=1, source_target_pairs={{0,2},{1,65},{2,4},{3,67},{4,6},{5,69},{6,0},{7,71},{8,10},{9,73},... | collective-permute-start | bytes 442376 | tf_op jit(solution)/shard_map/ppermute | solution.py:28
  108.4 15.1 %collective-permute-start.13 = (f16[64,1152]{1,0:T(8,128)(2,1)}, f16[64,1152]{1,0:T(8,128)(2,1)S(1)}, u32[]{:S(2)}, u32[]{:S(2)}) collective-permute-start(f16[64,1152]{1,0:T(8,128)(2,1)} %get-tuple-element.31), channel_id=1, source_target_pairs={{0,6},{1,73},{2,0},{3,75},{4,2},{5,77},{6,4},{7,79},{8,14},{9,65},... | collective-permute-start | bytes 442376 | tf_op jit(solution)/shard_map/ppermute | solution.py:28
  110.2 13.4 %collective-permute-start.12 = (f16[64,1152]{1,0:T(8,128)(2,1)}, f16[64,1152]{1,0:T(8,128)(2,1)}, u32[]{:S(2)}, u32[]{:S(2)}) collective-permute-start(f16[64,1152]{1,0:T(8,128)(2,1)} %get-tuple-element.32), channel_id=1, source_target_pairs={{0,4},{1,9},{2,6},{3,11},{4,0},{5,13},{6,2},{7,15},{8,12},{9,1},{1... | collective-permute-start | bytes 442376 | tf_op jit(solution)/shard_map/ppermute | solution.py:28
  117.9 5.7 %copy-start.5 = (f32[64,1152]{1,0:T(8,128)S(1)}, f32[64,1152]{1,0:T(8,128)}, u32[]{:S(2)}) copy-start(f32[64,1152]{1,0:T(8,128)} %image_ref.1) | copy-start | bytes 884740

commit v3 on v2

--- a/solution.py
+++ b/solution.py
@@ -42,10 +42,6 @@
 
 def swap(x, y, z, c):
     return x, y, z, 1 - c
-
-
-def finish(unit_vals, inverse, direction):
-    return inverse * (direction - unit_vals * jnp.sum(unit_vals * direction, axis=1, keepdims=True))
 
 
 CHUNK = 256
@@ -99,8 +95,31 @@
 
 def after(value, others):
     for other in others:
-        value = value + 0 * other[:1, : value.shape[1]].astype(value.dtype)
+        value = value + 0 * other[:1, :1].astype(value.dtype)
     return value
+
+
+def finish_kernel(*refs):
+    loss_parts, (image_out, text_out, loss_out) = refs[6], refs[7:]
+    for (vectors, inverse, direction), out in ((refs[:3], image_out), (refs[3:6], text_out)):
+        unit = vectors[...] * inverse[...]
+        along = jnp.sum(unit * direction[...], axis=1, keepdims=True)
+        out[...] = inverse[...] * (direction[...] - unit * along)
+    total = jnp.sum(jnp.sum(loss_parts[...], axis=0), axis=1, keepdims=True)
+    loss_out[...] = total * (1.0 / (128 * image_out.shape[0]))
+
+
+def finish(images, texts, loss_parts):
+    return pl.pallas_call(
+        finish_kernel,
+        out_shape=(
+            jax.ShapeDtypeStruct(images[2].shape, jnp.float32),
+            jax.ShapeDtypeStruct(texts[2].shape, jnp.float32),
+            jax.ShapeDtypeStruct((1, 1), jnp.float32),
+        ),
+        in_specs=[VMEM] * 7,
+        out_specs=[VMEM] * 3,
+    )(*images, *texts, loss_parts)
 
 
 def pair_kernel(n_image, *refs):
@@ -129,14 +148,13 @@
     loss_out[...] = jnp.zeros_like(loss_out)
     row_index = lax.broadcasted_iota(jnp.int32, (CHUNK, CHUNK), 0)
 
-    for copy in image_copies:
-        copy.wait()
-
-    def weigh(t, carry):
+    def weigh(t, carry, arriving=()):
         base = base_ref[t]
         pltpu.make_async_copy(text_buf.at[tile(t)], text_buf.at[tile(t)], sems.at[t]).wait()
         for i in range(n_cols):
             cols = pl.ds(i * CHUNK, CHUNK)
+            if arriving:
+                arriving[i].wait()
             scores = lax.dot_general(
                 text_buf[tile(t), :],
                 image_buf[cols, :],
@@ -159,7 +177,8 @@
             loss_out[...] += jnp.sum(jnp.log1p(joined).reshape(8, 8, CHUNK), axis=0)
         return carry
 
-    lax.fori_loop(0, n_text, weigh, 0)
+    weigh(0, 0, image_copies)
+    lax.fori_loop(1, n_text, weigh, 0)
 
     for half, out in enumerate(text_outs):
         rows = pl.ds(half * RING * CHUNK, RING * CHUNK)
@@ -189,7 +208,7 @@
     out = pl.pallas_call(
         functools.partial(pair_kernel, n_image),
         out_shape=out_shape,
-        in_specs=[SMEM, SMEM, SMEM, VMEM] + [HBM] * (2 + n_image),
+        in_specs=[SMEM, SMEM, SMEM, VMEM, HBM, ANY] + [HBM] * n_image,
         out_specs=[VMEM] * len(out_shape),
         scratch_shapes=[
             pltpu.VMEM((n_rows, dim), jnp.bfloat16),
@@ -203,17 +222,17 @@
             bytes_accessed=2 * (n_rows + n_cols) * dim,
             transcendentals=2 * n_rows * n_cols,
         ),
-    )(scale, base, pick, match, *slow(mine, other, *images))
+    )(scale, base, pick, match, *slow(mine), other, *slow(*images))
     return out[0], out[1], out[2:-1], out[-1]
 
 
 VMEM_LIMIT = 32 * 2**20
 
 
-def total_loss(part):
+def loss_parts(part):
     part = jnp.sum(part.reshape(-1, 128), axis=0)[None, None]
     parts = jnp.broadcast_to(part, (128, 1, 128))
-    return jnp.sum(lax.all_to_all(parts, AXES, 0, 0, tiled=True))
+    return lax.all_to_all(parts, AXES, 0, 0, tiled=True)
 
 
 def narrow(part):
@@ -274,19 +293,20 @@
         text_dir = text_dir + wide(send(wire, along_y(s)))
 
     line_dir, up_part, down_part, far_part = parts
-    far_part = held(far_part, [wide(wires[0][:8, :128])])
+    far_part = after(far_part, [wide(other[:8, :128])])
     for s, part in ((1, up_part), (3, down_part), (2, far_part)):
         line_dir = line_dir + wide(send(narrow(part), along_second(s)))
-    loss = total_loss(after(loss, [line_dir]))
+    loss = loss_parts(after(loss, [line_dir]))
     n = image_rows
     wire = narrow(line_dir[n:])
     image_dir = line_dir[:n]
     for r in (1, 2, 3):
         image_dir = image_dir + wide(send(wire[(r - 1) * n : r * n], along_first(r)))
 
-    grad_images = finish(picture_vectors * image_inv, image_inv, image_dir)
-    grad_texts = finish(caption_vectors * text_inv, text_inv, text_dir)
-    loss = loss / matching_captions.shape[0]
+    grad_images, grad_texts, loss = finish(
+        (picture_vectors, image_inv, image_dir), (caption_vectors, text_inv, text_dir), loss
+    )
+    loss = loss[0, 0]
     return (grad_images, grad_texts, loss)
 
 

time: 128 us -> 121 us (0.945); the launches traced: 128 us -> 119 us
  other arithmetic: 19.8 us -> 7.4 us
  waiting for transfers between devices: 22.4 us -> 27.2 us
  Pallas kernels: 28 us -> 31.9 us
  starting transfers between devices: 46.4 us -> 42.5 us
    mul x3 -> x0, other arithmetic: 5.29 us -> none  [the longest x2 5.28 us: finish(): inverse * (direction - unit_vals * jnp.sum(unit_vals * direction, axis=1,...]
    reduce_sum x4 -> x1, other arithmetic: 5.14 us -> 0.02 us  [loss_parts(): part = jnp.sum(part.reshape(-1, 128), axis=0)[None, None]]
    ppermute x17, waiting for transfers between devices: 21.3 us -> 26.1 us  [send(): return lax.ppermute(value, AXES, pairs)]
    add x1 -> x3, other arithmetic: 0.01 us -> 3.98 us  [the longest x1 3.18 us: body(): text_dir = text_dir + wide(send(wire, along_y(s)))]
    pallas_call x0 -> x1, Pallas kernels: none -> 3.29 us  [finish(): pl.pallas_call(finish_kernel, out_shape=(jax.ShapeDtypeStruct(images[2].s...]
    convert_element_type x6, other arithmetic: 5.74 us -> 2.63 us  [narrow(): return (part * 0.25).astype(WIRE)]
    all_to_all x1, starting transfers between devices: 9.99 us -> 7.77 us  [loss_parts(): return lax.all_to_all(parts, AXES, 0, 0, tiled=True)]
    slice x1, local copies, waits for them, and re-layouts: 1.85 us -> 0.08 us  [body(): image_dir = image_dir + wide(send(wire[(r - 1) * n:r * n], along_first(r)))]
  transfers between devices with their start and end apart: 19 -> 19, of which waited for: 8 -> 11; matrix products, arithmetic and copies ran while one was open for 16% -> 9% of each run, Pallas kernels for 0% -> 0%
where the time goes in v3:
time: 121 us; the launch traced here: 119 us
  starting transfers between devices  42.5 us (35%)
  Pallas kernels  31.9 us (26%)
  waiting for transfers between devices  27.2 us (22%)
  other arithmetic  7.4 us (6%)
  local copies, waits for them, and re-layouts  6.41 us (5%)
  between operations  3.48 us (3%)
    ppermute x17, starting transfers between devices, send(): return lax.ppermute(value, AXES, pairs)  29.6 us
    ppermute x17, waiting for transfers between devices, send(): return lax.ppermute(value, AXES, pairs)  26.1 us
    pallas_call x1, Pallas kernels, pair_block(): pl.pallas_call(functools.partial(pair_kernel, n_image), out_shape=out_sha...  25.4 us
    all_to_all x1, starting transfers between devices, loss_parts(): return lax.all_to_all(parts, AXES, 0, 0, tiled=True)  7.77 us
    all_to_all x1, starting transfers between devices, body(): lax.all_to_all(own, AXES, 0, 0, axis_index_groups=list(rings.values()), t...  5.15 us
    pallas_call x1, Pallas kernels, finish(): pl.pallas_call(finish_kernel, out_shape=(jax.ShapeDtypeStruct(images[2].s...  3.29 us
    add x1, other arithmetic, body(): text_dir = text_dir + wide(send(wire, along_y(s)))  3.18 us
    pallas_call x1, Pallas kernels, prepare(): pl.pallas_call(prepare_kernel, out_shape=(jax.ShapeDtypeStruct((RING,) +...  3.15 us
  transfers between devices with their start and end apart: 19, of which 11 were waited for; matrix products, arithmetic and copies ran while one was open for 9% of the time, Pallas kernels for 0%

profile of v3, /device:TPU:1, one launch (start us, length us, event | category | flops | bytes accessed | tf_op | source)
XLA Modules:
  0.0 118.9 jit_solution(13958562381569988755)
XLA Ops:
  0.6 3.1 %shard_map.85 = (bf16[4,256,1152]{2,1,0:T(8,128)(2,1)}, f32[256,1]{1,0:T(8,128)}, bf16[64,1152]{1,0:T(8,128)(2,1)}, f32[64,1]{1,0:T(8,128)}) custom-call(f32[256,1152]{1,0:T(8,128)} %refs_3_.1, f32[64,1152]{1,0:T(8,128)} %refs_0_.1), custom_call_target="tpu_custom_call" | custom-call | tf_op jit(solution)/shard_map/pallas_call | solution.py:69
  3.8 5.1 %all-to-all-start = ((bf16[4,256,1152]{2,1,0:T(8,128)(2,1)}), bf16[4,256,1152]{2,1,0:T(8,128)(2,1)S(1)}, u32[]{:S(2)}, u32[]{:S(2)}) async-start(bf16[4,256,1152]{2,1,0:T(8,128)(2,1)} %get-tuple-element.18), calls=%async_computation | async-start | bytes 4718592 | tf_op jit(solution)/shard_map/all_to_all | solution.py:261
  8.9 1.6 %collective-permute-start.2 = (bf16[64,1152]{1,0:T(8,128)(2,1)S(1)}, bf16[64,1152]{1,0:T(8,128)(2,1)S(1)}, u32[]{:S(2)}, u32[]{:S(2)}) collective-permute-start(bf16[64,1152]{1,0:T(8,128)(2,1)S(1)} %copy-done.7), channel_id=1, source_target_pairs={{0,2},{1,65},{2,4},{3,67},{4,6},{5,69},{6,0},{7,71},{8,10},{9,73},... | collective-permute-start | bytes 442376 | tf_op jit(solution)/shard_map/ppermute | solution.py:28
  10.6 3.3 %collective-permute-start.1 = (bf16[64,1152]{1,0:T(8,128)(2,1)S(1)}, bf16[64,1152]{1,0:T(8,128)(2,1)S(1)}, u32[]{:S(2)}, u32[]{:S(2)}) collective-permute-start(bf16[64,1152]{1,0:T(8,128)(2,1)S(1)} %copy-done.7), channel_id=1, source_target_pairs={{0,4},{1,9},{2,6},{3,11},{4,0},{5,13},{6,2},{7,15},{8,12},{9,1},{1... | collective-permute-start | bytes 442376 | tf_op jit(solution)/shard_map/ppermute | solution.py:28
  14.6 3.5 %collective-permute-done = bf16[64,1152]{1,0:T(8,128)(2,1)S(1)} collective-permute-done((bf16[64,1152]{1,0:T(8,128)(2,1)S(1)}, bf16[64,1152]{1,0:T(8,128)(2,1)S(1)}, u32[]{:S(2)}, u32[]{:S(2)}) %collective-permute-start) | collective-permute-done | bytes 147488 | tf_op jit(solution)/shard_map/ppermute | solution.py:28
  18.3 2.7 %collective-permute-start.5 = (bf16[256,1152]{1,0:T(8,128)(2,1)S(1)}, bf16[256,1152]{1,0:T(8,128)(2,1)S(1)}, u32[]{:S(2)}, u32[]{:S(2)}) collective-permute-start(bf16[256,1152]{1,0:T(8,128)(2,1)S(1)} %constant_dynamic-update-slice_fusion.refs_1_.refs_6_), channel_id=1, source_target_pairs={{0,8},{1,5},{2,10},{3,7},{4,12},{5,1},{6,14},{7,3},{8,0},{9,13},{1... | collective-permute-start | bytes 1769480 | tf_op jit(solution)/shard_map/ppermute | solution.py:28
  21.4 2.4 %collective-permute-start.3 = (bf16[256,1152]{1,0:T(8,128)(2,1)S(1)}, bf16[256,1152]{1,0:T(8,128)(2,1)}, u32[]{:S(2)}, u32[]{:S(2)}) collective-permute-start(bf16[256,1152]{1,0:T(8,128)(2,1)S(1)} %constant_dynamic-update-slice_fusion.refs_1_.refs_6_), channel_id=1, source_target_pairs={{0,72},{1,7},{2,74},{3,1},{4,76},{5,3},{6,78},{7,5},{8,64},{9,15},... | collective-permute-start | bytes 1769480 | tf_op jit(solution)/shard_map/ppermute | solution.py:28
  23.8 5.2 %collective-permute-done.5.refs_4_.refs_9_ = bf16[256,1152]{1,0:T(8,128)(2,1)S(1)} collective-permute-done((bf16[256,1152]{1,0:T(8,128)(2,1)S(1)}, bf16[256,1152]{1,0:T(8,128)(2,1)S(1)}, u32[]{:S(2)}, u32[]{:S(2)}) %collective-permute-start.5) | collective-permute-done | bytes 589856 | tf_op jit(solution)/shard_map/ppermute | solution.py:28
  29.0 6.3 %collective-permute-done.4.refs_3_.refs_8_ = bf16[256,1152]{1,0:T(8,128)(2,1)S(1)} collective-permute-done((bf16[256,1152]{1,0:T(8,128)(2,1)S(1)}, bf16[256,1152]{1,0:T(8,128)(2,1)S(1)}, u32[]{:S(2)}, u32[]{:S(2)}) %collective-permute-start.4) | collective-permute-done | bytes 589856 | tf_op jit(solution)/shard_map/ppermute | solution.py:28
  35.3 0.8 copy-done.5
  36.1 1.1 all-to-all-done
  37.2 1.4 %copy-done.1 = bf16[4,256,1152]{2,1,0:T(8,128)(2,1)} copy-done((bf16[4,256,1152]{2,1,0:T(8,128)(2,1)}, bf16[4,256,1152]{2,1,0:T(8,128)(2,1)S(1)}, u32[]{:S(2)}) %copy-start.1) | copy-done | bytes 2359320
  38.6 1.9 %collective-permute-start.6 = (bf16[1024,1152]{1,0:T(8,128)(2,1)}, bf16[1024,1152]{1,0:T(8,128)(2,1)S(1)}, u32[]{:S(2)}, u32[]{:S(2)}) collective-permute-start(bf16[1024,1152]{1,0:T(8,128)(2,1)} %shard_map.86.refs_4_), channel_id=1, source_target_pairs={{0,1},{1,0},{2,3},{3,2},{4,5},{5,4},{6,7},{7,6},{8,9},{9,8},{10,11... | collective-permute-start | bytes 7077896 | tf_op jit(solution)/shard_map/ppermute | solution.py:28
  42.1 0.8 reshape.285
  43.9 1.0 collective-permute-done.6.refs_5_
  44.8 25.4 %shard_map.87 = (f32[1024,1152]{1,0:T(8,128)S(1)}, f32[1024,1152]{1,0:T(8,128)S(1)}, f32[256,1152]{1,0:T(8,128)S(1)}, f32[256,1152]{1,0:T(8,128)S(1)}, f32[256,1...) custom-call(f32[3]{0:T(128)S(1)} %pad_maximum_fusion.refs_0_, s32[8]{0:T(128)S(1)} %pad_add_fusion.refs_1_, ...), custom_call_target="tpu_custom_call" | custom-call | flops 14495514624 | bytes 7077888 | tf_op jit(solution)/shard_map/pallas_call | solution.py:208
  71.5 2.5 %collective-permute-start.8 = (f16[256,1152]{1,0:T(8,128)(2,1)S(1)}, f16[256,1152]{1,0:T(8,128)(2,1)S(1)}, u32[]{:S(2)}, u32[]{:S(2)}) collective-permute-start(f16[256,1152]{1,0:T(8,128)(2,1)S(1)} %multiply_convert_fusion.5), channel_id=1, source_target_pairs={{0,72},{1,7},{2,74},{3,1},{4,76},{5,3},{6,78},{7,5},{8,64},{9,15},... | collective-permute-start | bytes 1769480 | tf_op jit(solution)/shard_map/ppermute | solution.py:28
  74.2 1.3 %collective-permute-done.9 = f16[1024,1152]{1,0:T(8,128)(2,1)S(1)} collective-permute-done((f16[1024,1152]{1,0:T(8,128)(2,1)S(1)}, f16[1024,1152]{1,0:T(8,128)(2,1)S(1)}, u32[]{:S(2)}, u32[]{:S(2)}) %collective-permute-start.9) | collective-permute-done | bytes 2359328 | tf_op jit(solution)/shard_map/ppermute | solution.py:28
  77.0 2.8 %collective-permute-start.10 = (f16[256,1152]{1,0:T(8,128)(2,1)S(1)}, f16[256,1152]{1,0:T(8,128)(2,1)S(1)}, u32[]{:S(2)}, u32[]{:S(2)}) collective-permute-start(f16[256,1152]{1,0:T(8,128)(2,1)S(1)} %multiply_convert_fusion.4), channel_id=1, source_target_pairs={{0,8},{1,5},{2,10},{3,7},{4,12},{5,1},{6,14},{7,3},{8,0},{9,13},{1... | collective-permute-start | bytes 1769480 | tf_op jit(solution)/shard_map/ppermute | solution.py:28
  79.8 1.8 %multiply_convert_fusion.3 = (f16[256,1152]{1,0:T(8,128)(2,1)}, f16[256,1152]{1,0:T(8,128)(2,1)}, f16[256,1152]{1,0:T(8,128)(2,1)S(1)}) fusion(f32[1024,1152]{1,0:T(8,128)S(1)} %get-tuple-element.26, f16[1024,1152]{1,0:T(8,128)(2,1)S(1)} %collective-permute-done.9), kind=kLoop, calls=%fused_computation.5 | loop fusion | flops 4423680 | bytes 7077888 | tf_op jit(solution)/shard_map/convert_element_type | solution.py:239
  81.6 0.9 collective-permute-start.14
  82.4 2.4 %collective-permute-start.16 = (f16[256,1152]{1,0:T(8,128)(2,1)}, f16[256,1152]{1,0:T(8,128)(2,1)S(1)}, u32[]{:S(2)}, u32[]{:S(2)}) collective-permute-start(f16[256,1152]{1,0:T(8,128)(2,1)} %get-tuple-element.34), channel_id=1, source_target_pairs={{0,32},{1,33},{2,34},{3,35},{4,36},{5,37},{6,38},{7,39},{8,40},{9,... | collective-permute-start | bytes 1769480 | tf_op jit(solution)/shard_map/ppermute | solution.py:28
  84.8 2.4 %collective-permute-done.8 = f16[256,1152]{1,0:T(8,128)(2,1)S(1)} collective-permute-done((f16[256,1152]{1,0:T(8,128)(2,1)S(1)}, f16[256,1152]{1,0:T(8,128)(2,1)S(1)}, u32[]{:S(2)}, u32[]{:S(2)}) %collective-permute-start.8) | collective-permute-done | bytes 589856 | tf_op jit(solution)/shard_map/ppermute | solution.py:28
  87.2 2.5 %collective-permute-start.15 = (f16[256,1152]{1,0:T(8,128)(2,1)S(1)}, f16[256,1152]{1,0:T(8,128)(2,1)}, u32[]{:S(2)}, u32[]{:S(2)}) collective-permute-start(f16[256,1152]{1,0:T(8,128)(2,1)S(1)} %get-tuple-element.35), channel_id=1, source_target_pairs={{0,48},{1,49},{2,50},{3,51},{4,52},{5,53},{6,54},{7,55},{8,56},{9,... | collective-permute-start | bytes 1769480 | tf_op jit(solution)/shard_map/ppermute | solution.py:28
  89.7 1.1 collective-permute-done.7
  93.1 7.8 %all-to-all-start.1 = ((f32[128,1,128]{2,1,0:T(1,128)}), f32[128,1,128]{2,1,0:T(1,128)S(1)}, u32[]{:S(2)}, u32[]{:S(2)}) async-start(f32[128,1,128]{2,1,0:T(1,128)} %broadcast_in_dim.20), calls=%async_computation.1 | async-start | bytes 131072 | tf_op jit(solution)/shard_map/all_to_all | solution.py:235
  101.0 1.6 %collective-permute-start.11 = (f16[64,1152]{1,0:T(8,128)(2,1)S(1)}, f16[64,1152]{1,0:T(8,128)(2,1)S(1)}, u32[]{:S(2)}, u32[]{:S(2)}) collective-permute-start(f16[64,1152]{1,0:T(8,128)(2,1)S(1)} %get-tuple-element.36), channel_id=1, source_target_pairs={{0,2},{1,65},{2,4},{3,67},{4,6},{5,69},{6,0},{7,71},{8,10},{9,73},... | collective-permute-start | bytes 442376 | tf_op jit(solution)/shard_map/ppermute | solution.py:28
  102.6 1.8 %collective-permute-start.13 = (f16[64,1152]{1,0:T(8,128)(2,1)S(1)}, f16[64,1152]{1,0:T(8,128)(2,1)S(1)}, u32[]{:S(2)}, u32[]{:S(2)}) collective-permute-start(f16[64,1152]{1,0:T(8,128)(2,1)S(1)} %get-tuple-element.37), channel_id=1, source_target_pairs={{0,6},{1,73},{2,0},{3,75},{4,2},{5,77},{6,4},{7,79},{8,14},{9,65},... | collective-permute-start | bytes 442376 | tf_op jit(solution)/shard_map/ppermute | solution.py:28
  104.4 1.4 %collective-permute-start.12 = (f16[64,1152]{1,0:T(8,128)(2,1)S(1)}, f16[64,1152]{1,0:T(8,128)(2,1)S(1)}, u32[]{:S(2)}, u32[]{:S(2)}) collective-permute-start(f16[64,1152]{1,0:T(8,128)(2,1)S(1)} %get-tuple-element.38), channel_id=1, source_target_pairs={{0,4},{1,9},{2,6},{3,11},{4,0},{5,13},{6,2},{7,15},{8,12},{9,1},{1... | collective-permute-start | bytes 442376 | tf_op jit(solution)/shard_map/ppermute | solution.py:28
  105.8 4.9 %collective-permute-done.16 = f16[256,1152]{1,0:T(8,128)(2,1)S(1)} collective-permute-done((f16[256,1152]{1,0:T(8,128)(2,1)}, f16[256,1152]{1,0:T(8,128)(2,1)S(1)}, u32[]{:S(2)}, u32[]{:S(2)}) %collective-permute-start.16) | collective-permute-done | bytes 589856 | tf_op jit(solution)/shard_map/ppermute | solution.py:28
  111.0 3.2 %multiply_add_fusion.refs_5_ = f32[256,1152]{1,0:T(8,128)} fusion(f16[256,1152]{1,0:T(8,128)(2,1)S(1)} %collective-permute-done.16, f16[256,1152]{1,0:T(8,128)(2,1)} %collective-permute-done.15, f16[256,1152]{1,0:T(8,128)(2,1)S(1)} %collective-permute-done.14, f32[1024,1152]{1,0:T(8,128)} %copy-done, f16[1024,1152]{1,0:T(8,128)(2,1)} %copy-done.2), kind=kLoop, calls=%fused_computation.2 | loop fusion | flops 3538944 | bytes 4718592 | tf_op jit(solution)/shard_map/add | solution.py:293
  115.6 3.3 %shard_map.88 = (f32[64,1152]{1,0:T(8,128)}, f32[256,1152]{1,0:T(8,128)}, f32[1,1]{1,0:T(1,128)}) custom-call(f32[64,1152]{1,0:T(8,128)} %refs_0_.1, f32[64,1]{1,0:T(8,128)} %get-tuple-element.17.refs_1_, f32[64,1152]{1,0:T(8,128)} %fusion.2.refs_2_, f32[256,1152]{1,0:T(8,128)} %refs_3_.1, f32[256,1]{1,0:T(8,128)} %get-tuple-element.25.refs_4_, ...), custom_call_target="tpu_custom_call" | custom-call | tf_op jit(solution)/shard_map/pallas_call | solution.py:113
  (65 shorter events, 8.0 us)
Async XLA Ops:
  3.8 5.2 %copy-start.7 = (bf16[64,1152]{1,0:T(8,128)(2,1)S(1)}, bf16[64,1152]{1,0:T(8,128)(2,1)}, u32[]{:S(2)}) copy-start(bf16[64,1152]{1,0:T(8,128)(2,1)} %get-tuple-element.19) | copy-start | bytes 442372
  3.8 33.4 %all-to-all-start = ((bf16[4,256,1152]{2,1,0:T(8,128)(2,1)}), bf16[4,256,1152]{2,1,0:T(8,128)(2,1)S(1)}, u32[]{:S(2)}, u32[]{:S(2)}) async-start(bf16[4,256,1152]{2,1,0:T(8,128)(2,1)} %get-tuple-element.18), calls=%async_computation | async-start | bytes 4718592 | tf_op jit(solution)/shard_map/all_to_all | solution.py:261
  8.9 9.4 %collective-permute-start.2 = (bf16[64,1152]{1,0:T(8,128)(2,1)S(1)}, bf16[64,1152]{1,0:T(8,128)(2,1)S(1)}, u32[]{:S(2)}, u32[]{:S(2)}) collective-permute-start(bf16[64,1152]{1,0:T(8,128)(2,1)S(1)} %copy-done.7), channel_id=1, source_target_pairs={{0,2},{1,65},{2,4},{3,67},{4,6},{5,69},{6,0},{7,71},{8,10},{9,73},... | collective-permute-start | bytes 442376 | tf_op jit(solution)/shard_map/ppermute | solution.py:28
  10.6 7.7 %collective-permute-start.1 = (bf16[64,1152]{1,0:T(8,128)(2,1)S(1)}, bf16[64,1152]{1,0:T(8,128)(2,1)S(1)}, u32[]{:S(2)}, u32[]{:S(2)}) collective-permute-start(bf16[64,1152]{1,0:T(8,128)(2,1)S(1)} %copy-done.7), channel_id=1, source_target_pairs={{0,4},{1,9},{2,6},{3,11},{4,0},{5,13},{6,2},{7,15},{8,12},{9,1},{1... | collective-permute-start | bytes 442376 | tf_op jit(solution)/shard_map/ppermute | solution.py:28
  13.9 4.3 %collective-permute-start = (bf16[64,1152]{1,0:T(8,128)(2,1)S(1)}, bf16[64,1152]{1,0:T(8,128)(2,1)S(1)}, u32[]{:S(2)}, u32[]{:S(2)}) collective-permute-start(bf16[64,1152]{1,0:T(8,128)(2,1)S(1)} %copy-done.7), channel_id=1, source_target_pairs={{0,6},{1,73},{2,0},{3,75},{4,2},{5,77},{6,4},{7,79},{8,14},{9,65},... | collective-permute-start | bytes 442376 | tf_op jit(solution)/shard_map/ppermute | solution.py:28
  18.3 18.8 %copy-start.3 = (bf16[256,1152]{1,0:T(8,128)(2,1)}, bf16[256,1152]{1,0:T(8,128)(2,1)S(1)}, u32[]{:S(2)}) copy-start(bf16[256,1152]{1,0:T(8,128)(2,1)S(1)} %constant_dynamic-update-slice_fusion.refs_1_.refs_6_) | copy-start | bytes 1769476
  18.3 10.7 %collective-permute-start.5 = (bf16[256,1152]{1,0:T(8,128)(2,1)S(1)}, bf16[256,1152]{1,0:T(8,128)(2,1)S(1)}, u32[]{:S(2)}, u32[]{:S(2)}) collective-permute-start(bf16[256,1152]{1,0:T(8,128)(2,1)S(1)} %constant_dynamic-update-slice_fusion.refs_1_.refs_6_), channel_id=1, source_target_pairs={{0,8},{1,5},{2,10},{3,7},{4,12},{5,1},{6,14},{7,3},{8,0},{9,13},{1... | collective-permute-start | bytes 1769480 | tf_op jit(solution)/shard_map/ppermute | solution.py:28
  21.1 14.2 %collective-permute-start.4 = (bf16[256,1152]{1,0:T(8,128)(2,1)S(1)}, bf16[256,1152]{1,0:T(8,128)(2,1)S(1)}, u32[]{:S(2)}, u32[]{:S(2)}) collective-permute-start(bf16[256,1152]{1,0:T(8,128)(2,1)S(1)} %constant_dynamic-update-slice_fusion.refs_1_.refs_6_), channel_id=1, source_target_pairs={{0,64},{1,3},{2,66},{3,5},{4,68},{5,7},{6,70},{7,1},{8,72},{9,11},... | collective-permute-start | bytes 1769480 | tf_op jit(solution)/shard_map/ppermute | solution.py:28
  21.4 14.7 %collective-permute-start.3 = (bf16[256,1152]{1,0:T(8,128)(2,1)S(1)}, bf16[256,1152]{1,0:T(8,128)(2,1)}, u32[]{:S(2)}, u32[]{:S(2)}) collective-permute-start(bf16[256,1152]{1,0:T(8,128)(2,1)S(1)} %constant_dynamic-update-slice_fusion.refs_1_.refs_6_), channel_id=1, source_target_pairs={{0,72},{1,7},{2,74},{3,1},{4,76},{5,3},{6,78},{7,5},{8,64},{9,15},... | collective-permute-start | bytes 1769480 | tf_op jit(solution)/shard_map/ppermute | solution.py:28
  29.0 8.2 %copy-start.4 = (bf16[256,1152]{1,0:T(8,128)(2,1)}, bf16[256,1152]{1,0:T(8,128)(2,1)S(1)}, u32[]{:S(2)}) copy-start(bf16[256,1152]{1,0:T(8,128)(2,1)S(1)} %collective-permute-done.5.refs_4_.refs_9_) | copy-start | bytes 1769476
  35.3 0.8 copy-start.5
  37.2 1.4 %copy-start.1 = (bf16[4,256,1152]{2,1,0:T(8,128)(2,1)}, bf16[4,256,1152]{2,1,0:T(8,128)(2,1)S(1)}, u32[]{:S(2)}) copy-start(bf16[4,256,1152]{2,1,0:T(8,128)(2,1)S(1)} %all-to-all-done) | copy-start | bytes 7077892
  38.6 1.9 %copy-start.8 = (s32[4]{0:T(128)S(1)}, s32[4]{0:T(128)}, u32[]{:S(2)}) copy-start(s32[4]{0:T(128)} %constant.207.clone) | copy-start | bytes 52
  38.6 6.2 %collective-permute-start.6 = (bf16[1024,1152]{1,0:T(8,128)(2,1)}, bf16[1024,1152]{1,0:T(8,128)(2,1)S(1)}, u32[]{:S(2)}, u32[]{:S(2)}) collective-permute-start(bf16[1024,1152]{1,0:T(8,128)(2,1)} %shard_map.86.refs_4_), channel_id=1, source_target_pairs={{0,1},{1,0},{2,3},{3,2},{4,5},{5,4},{6,7},{7,6},{8,9},{9,8},{10,11... | collective-permute-start | bytes 7077896 | tf_op jit(solution)/shard_map/ppermute | solution.py:28
  70.3 9.5 %copy-start = (f32[1024,1152]{1,0:T(8,128)}, f32[1024,1152]{1,0:T(8,128)S(1)}, u32[]{:S(2)}) copy-start(f32[1024,1152]{1,0:T(8,128)S(1)} %get-tuple-element.26) | copy-start | bytes 14155780
  70.7 4.8 %collective-permute-start.9 = (f16[1024,1152]{1,0:T(8,128)(2,1)S(1)}, f16[1024,1152]{1,0:T(8,128)(2,1)S(1)}, u32[]{:S(2)}, u32[]{:S(2)}) collective-permute-start(f16[1024,1152]{1,0:T(8,128)(2,1)S(1)} %multiply_convert_fusion), channel_id=1, source_target_pairs={{0,1},{1,0},{2,3},{3,2},{4,5},{5,4},{6,7},{7,6},{8,9},{9,8},{10,11... | collective-permute-start | bytes 7077896 | tf_op jit(solution)/shard_map/ppermute | solution.py:28
  71.5 15.7 %collective-permute-start.8 = (f16[256,1152]{1,0:T(8,128)(2,1)S(1)}, f16[256,1152]{1,0:T(8,128)(2,1)S(1)}, u32[]{:S(2)}, u32[]{:S(2)}) collective-permute-start(f16[256,1152]{1,0:T(8,128)(2,1)S(1)} %multiply_convert_fusion.5), channel_id=1, source_target_pairs={{0,72},{1,7},{2,74},{3,1},{4,76},{5,3},{6,78},{7,5},{8,64},{9,15},... | collective-permute-start | bytes 1769480 | tf_op jit(solution)/shard_map/ppermute | solution.py:28
  74.2 16.6 %collective-permute-start.7 = (f16[256,1152]{1,0:T(8,128)(2,1)S(1)}, f16[256,1152]{1,0:T(8,128)(2,1)S(1)}, u32[]{:S(2)}, u32[]{:S(2)}) collective-permute-start(f16[256,1152]{1,0:T(8,128)(2,1)S(1)} %multiply_convert_fusion.6), channel_id=1, source_target_pairs={{0,64},{1,3},{2,66},{3,5},{4,68},{5,7},{6,70},{7,1},{8,72},{9,11},... | collective-permute-start | bytes 1769480 | tf_op jit(solution)/shard_map/ppermute | solution.py:28
  75.6 6.0 %copy-start.2 = (f16[1024,1152]{1,0:T(8,128)(2,1)}, f16[1024,1152]{1,0:T(8,128)(2,1)S(1)}, u32[]{:S(2)}) copy-start(f16[1024,1152]{1,0:T(8,128)(2,1)S(1)} %collective-permute-done.9) | copy-start | bytes 7077892
  77.0 13.8 %collective-permute-start.10 = (f16[256,1152]{1,0:T(8,128)(2,1)S(1)}, f16[256,1152]{1,0:T(8,128)(2,1)S(1)}, u32[]{:S(2)}, u32[]{:S(2)}) collective-permute-start(f16[256,1152]{1,0:T(8,128)(2,1)S(1)} %multiply_convert_fusion.4), channel_id=1, source_target_pairs={{0,8},{1,5},{2,10},{3,7},{4,12},{5,1},{6,14},{7,3},{8,0},{9,13},{1... | collective-permute-start | bytes 1769480 | tf_op jit(solution)/shard_map/ppermute | solution.py:28
  81.6 22.9 %collective-permute-start.14 = (f16[256,1152]{1,0:T(8,128)(2,1)}, f16[256,1152]{1,0:T(8,128)(2,1)S(1)}, u32[]{:S(2)}, u32[]{:S(2)}) collective-permute-start(f16[256,1152]{1,0:T(8,128)(2,1)} %get-tuple-element.33), channel_id=1, source_target_pairs={{0,16},{1,17},{2,18},{3,19},{4,20},{5,21},{6,22},{7,23},{8,24},{9,... | collective-permute-start | bytes 1769480 | tf_op jit(solution)/shard_map/ppermute | solution.py:28
  82.4 28.3 %collective-permute-start.16 = (f16[256,1152]{1,0:T(8,128)(2,1)}, f16[256,1152]{1,0:T(8,128)(2,1)S(1)}, u32[]{:S(2)}, u32[]{:S(2)}) collective-permute-start(f16[256,1152]{1,0:T(8,128)(2,1)} %get-tuple-element.34), channel_id=1, source_target_pairs={{0,32},{1,33},{2,34},{3,35},{4,36},{5,37},{6,38},{7,39},{8,40},{9,... | collective-permute-start | bytes 1769480 | tf_op jit(solution)/shard_map/ppermute | solution.py:28
  87.2 23.8 %collective-permute-start.15 = (f16[256,1152]{1,0:T(8,128)(2,1)S(1)}, f16[256,1152]{1,0:T(8,128)(2,1)}, u32[]{:S(2)}, u32[]{:S(2)}) collective-permute-start(f16[256,1152]{1,0:T(8,128)(2,1)S(1)} %get-tuple-element.35), channel_id=1, source_target_pairs={{0,48},{1,49},{2,50},{3,51},{4,52},{5,53},{6,54},{7,55},{8,56},{9,... | collective-permute-start | bytes 1769480 | tf_op jit(solution)/shard_map/ppermute | solution.py:28
  93.1 21.8 %all-to-all-start.1 = ((f32[128,1,128]{2,1,0:T(1,128)}), f32[128,1,128]{2,1,0:T(1,128)S(1)}, u32[]{:S(2)}, u32[]{:S(2)}) async-start(f32[128,1,128]{2,1,0:T(1,128)} %broadcast_in_dim.20), calls=%async_computation.1 | async-start | bytes 131072 | tf_op jit(solution)/shard_map/all_to_all | solution.py:235
  101.0 13.2 %collective-permute-start.11 = (f16[64,1152]{1,0:T(8,128)(2,1)S(1)}, f16[64,1152]{1,0:T(8,128)(2,1)S(1)}, u32[]{:S(2)}, u32[]{:S(2)}) collective-permute-start(f16[64,1152]{1,0:T(8,128)(2,1)S(1)} %get-tuple-element.36), channel_id=1, source_target_pairs={{0,2},{1,65},{2,4},{3,67},{4,6},{5,69},{6,0},{7,71},{8,10},{9,73},... | collective-permute-start | bytes 442376 | tf_op jit(solution)/shard_map/ppermute | solution.py:28
  102.6 11.6 %collective-permute-start.13 = (f16[64,1152]{1,0:T(8,128)(2,1)S(1)}, f16[64,1152]{1,0:T(8,128)(2,1)S(1)}, u32[]{:S(2)}, u32[]{:S(2)}) collective-permute-start(f16[64,1152]{1,0:T(8,128)(2,1)S(1)} %get-tuple-element.37), channel_id=1, source_target_pairs={{0,6},{1,73},{2,0},{3,75},{4,2},{5,77},{6,4},{7,79},{8,14},{9,65},... | collective-permute-start | bytes 442376 | tf_op jit(solution)/shard_map/ppermute | solution.py:28
  104.4 9.8 %collective-permute-start.12 = (f16[64,1152]{1,0:T(8,128)(2,1)S(1)}, f16[64,1152]{1,0:T(8,128)(2,1)S(1)}, u32[]{:S(2)}, u32[]{:S(2)}) collective-permute-start(f16[64,1152]{1,0:T(8,128)(2,1)S(1)} %get-tuple-element.38), channel_id=1, source_target_pairs={{0,4},{1,9},{2,6},{3,11},{4,0},{5,13},{6,2},{7,15},{8,12},{9,1},{1... | collective-permute-start | bytes 442376 | tf_op jit(solution)/shard_map/ppermute | solution.py:28
  115.0 0.6 copy-start.6

commit v4 on v3

--- a/solution.py
+++ b/solution.py
@@ -95,7 +95,7 @@
 
 def after(value, others):
     for other in others:
-        value = value + 0 * other[:1, :1].astype(value.dtype)
+        value = value + 0 * other[:1, : value.shape[1]].astype(value.dtype)
     return value
 
 
@@ -148,13 +148,11 @@
     loss_out[...] = jnp.zeros_like(loss_out)
     row_index = lax.broadcasted_iota(jnp.int32, (CHUNK, CHUNK), 0)
 
-    def weigh(t, carry, arriving=()):
+    def weigh(t, carry):
         base = base_ref[t]
         pltpu.make_async_copy(text_buf.at[tile(t)], text_buf.at[tile(t)], sems.at[t]).wait()
         for i in range(n_cols):
             cols = pl.ds(i * CHUNK, CHUNK)
-            if arriving:
-                arriving[i].wait()
             scores = lax.dot_general(
                 text_buf[tile(t), :],
                 image_buf[cols, :],
@@ -177,8 +175,9 @@
             loss_out[...] += jnp.sum(jnp.log1p(joined).reshape(8, 8, CHUNK), axis=0)
         return carry
 
-    weigh(0, 0, image_copies)
-    lax.fori_loop(1, n_text, weigh, 0)
+    for copy in image_copies:
+        copy.wait()
+    lax.fori_loop(0, n_text, weigh, 0)
 
     for half, out in enumerate(text_outs):
         rows = pl.ds(half * RING * CHUNK, RING * CHUNK)
@@ -288,12 +287,12 @@
     wires = [
         narrow(mine[s * n : (s + 1) * n] + wide(other[s * n : (s + 1) * n])) for s in (1, 3, 2)
     ]
-    text_dir = mine[:n] + wide(other[:n])
+    text_dir = lax.optimization_barrier(mine[:n] + wide(other[:n]))
     for s, wire in zip((1, 3, 2), wires):
         text_dir = text_dir + wide(send(wire, along_y(s)))
 
     line_dir, up_part, down_part, far_part = parts
-    far_part = after(far_part, [wide(other[:8, :128])])
+    far_part = after(far_part, [other])
     for s, part in ((1, up_part), (3, down_part), (2, far_part)):
         line_dir = line_dir + wide(send(narrow(part), along_second(s)))
     loss = loss_parts(after(loss, [line_dir]))
@@ -303,6 +302,9 @@
     for r in (1, 2, 3):
         image_dir = image_dir + wide(send(wire[(r - 1) * n : r * n], along_first(r)))
 
+    image_dir, text_dir = [
+        pltpu.with_memory_space_constraint(a, pltpu.VMEM) for a in (image_dir, text_dir)
+    ]
     grad_images, grad_texts, loss = finish(
         (picture_vectors, image_inv, image_dir), (caption_vectors, text_inv, text_dir), loss
     )

time: 121 us -> 117 us (0.967)
  waiting for transfers between devices: 27.2 us -> 29.6 us
  other arithmetic: 7.4 us -> 5.48 us
  local copies, waits for them, and re-layouts: 6.41 us -> 4.72 us
  between operations: 3.48 us -> 2.18 us
    all_to_all x1, waiting for transfers between devices: 0.01 us -> 1.56 us  [loss_parts(): return lax.all_to_all(parts, AXES, 0, 0, tiled=True)]
    add x1, other arithmetic: 3.18 us -> 1.76 us  [body(): text_dir = text_dir + wide(send(wire, along_y(s)))]
    unnamed x21 -> x15, local copies, waits for them, and re-layouts: 2.93 us -> 2.31 us
  transfers between devices with their start and end apart: 19 -> 19, of which waited for: 11 -> 12; matrix products, arithmetic and copies ran while one was open for 9% -> 6% of each run, Pallas kernels for 0% -> 0%
where the time goes in v4:
time: 117 us; the launch traced here: 116 us
  starting transfers between devices  42.7 us (36%)
  Pallas kernels  30.9 us (26%)
  waiting for transfers between devices  29.6 us (25%)
  other arithmetic  5.48 us (5%)
  local copies, waits for them, and re-layouts  4.72 us (4%)
  between operations  2.18 us (2%)
    ppermute x17, starting transfers between devices, send(): return lax.ppermute(value, AXES, pairs)  29.6 us
    ppermute x17, waiting for transfers between devices, send(): return lax.ppermute(value, AXES, pairs)  27 us
    pallas_call x1, Pallas kernels, pair_block(): pl.pallas_call(functools.partial(pair_kernel, n_image), out_shape=out_sha...  24.8 us
    all_to_all x1, starting transfers between devices, loss_parts(): return lax.all_to_all(parts, AXES, 0, 0, tiled=True)  7.9 us
    all_to_all x1, starting transfers between devices, body(): lax.all_to_all(own, AXES, 0, 0, axis_index_groups=list(rings.values()), t...  5.15 us
    pallas_call x1, Pallas kernels, prepare(): pl.pallas_call(prepare_kernel, out_shape=(jax.ShapeDtypeStruct((RING,) +...  3.16 us
    pallas_call x1, Pallas kernels, finish(): pl.pallas_call(finish_kernel, out_shape=(jax.ShapeDtypeStruct(images[2].s...  2.93 us
    convert_element_type x6, other arithmetic, narrow(): return (part * 0.25).astype(WIRE)  2.83 us
  transfers between devices with their start and end apart: 19, of which 12 were waited for; matrix products, arithmetic and copies ran while one was open for 6% of the time, Pallas kernels for 0%

profile of v4, /device:TPU:1, one launch (start us, length us, event | category | flops | bytes accessed | tf_op | source)
XLA Modules:
  0.0 115.5 jit_solution(12395902087265680276)
XLA Ops:
  0.6 3.2 %shard_map.85 = (bf16[4,256,1152]{2,1,0:T(8,128)(2,1)}, f32[256,1]{1,0:T(8,128)}, bf16[64,1152]{1,0:T(8,128)(2,1)}, f32[64,1]{1,0:T(8,128)}) custom-call(f32[256,1152]{1,0:T(8,128)} %refs_3_.1, f32[64,1152]{1,0:T(8,128)} %refs_0_.1), custom_call_target="tpu_custom_call" | custom-call | tf_op jit(solution)/shard_map/pallas_call | solution.py:69
  3.8 5.1 %all-to-all-start = ((bf16[4,256,1152]{2,1,0:T(8,128)(2,1)}), bf16[4,256,1152]{2,1,0:T(8,128)(2,1)S(1)}, u32[]{:S(2)}, u32[]{:S(2)}) async-start(bf16[4,256,1152]{2,1,0:T(8,128)(2,1)} %get-tuple-element.18), calls=%async_computation | async-start | bytes 4718592 | tf_op jit(solution)/shard_map/all_to_all | solution.py:260
  8.9 1.6 %collective-permute-start.2 = (bf16[64,1152]{1,0:T(8,128)(2,1)S(1)}, bf16[64,1152]{1,0:T(8,128)(2,1)S(1)}, u32[]{:S(2)}, u32[]{:S(2)}) collective-permute-start(bf16[64,1152]{1,0:T(8,128)(2,1)S(1)} %copy-done.4), channel_id=1, source_target_pairs={{0,2},{1,65},{2,4},{3,67},{4,6},{5,69},{6,0},{7,71},{8,10},{9,73},... | collective-permute-start | bytes 442376 | tf_op jit(solution)/shard_map/ppermute | solution.py:28
  10.6 3.3 %collective-permute-start.1 = (bf16[64,1152]{1,0:T(8,128)(2,1)S(1)}, bf16[64,1152]{1,0:T(8,128)(2,1)S(1)}, u32[]{:S(2)}, u32[]{:S(2)}) collective-permute-start(bf16[64,1152]{1,0:T(8,128)(2,1)S(1)} %copy-done.4), channel_id=1, source_target_pairs={{0,4},{1,9},{2,6},{3,11},{4,0},{5,13},{6,2},{7,15},{8,12},{9,1},{1... | collective-permute-start | bytes 442376 | tf_op jit(solution)/shard_map/ppermute | solution.py:28
  14.6 3.5 %collective-permute-done = bf16[64,1152]{1,0:T(8,128)(2,1)S(1)} collective-permute-done((bf16[64,1152]{1,0:T(8,128)(2,1)S(1)}, bf16[64,1152]{1,0:T(8,128)(2,1)S(1)}, u32[]{:S(2)}, u32[]{:S(2)}) %collective-permute-start) | collective-permute-done | bytes 147488 | tf_op jit(solution)/shard_map/ppermute | solution.py:28
  18.3 2.7 %collective-permute-start.5 = (bf16[256,1152]{1,0:T(8,128)(2,1)S(1)}, bf16[256,1152]{1,0:T(8,128)(2,1)S(1)}, u32[]{:S(2)}, u32[]{:S(2)}) collective-permute-start(bf16[256,1152]{1,0:T(8,128)(2,1)S(1)} %constant_dynamic-update-slice_fusion.refs_1_.refs_6_), channel_id=1, source_target_pairs={{0,8},{1,5},{2,10},{3,7},{4,12},{5,1},{6,14},{7,3},{8,0},{9,13},{1... | collective-permute-start | bytes 1769480 | tf_op jit(solution)/shard_map/ppermute | solution.py:28
  21.4 2.4 %collective-permute-start.3 = (bf16[256,1152]{1,0:T(8,128)(2,1)S(1)}, bf16[256,1152]{1,0:T(8,128)(2,1)}, u32[]{:S(2)}, u32[]{:S(2)}) collective-permute-start(bf16[256,1152]{1,0:T(8,128)(2,1)S(1)} %constant_dynamic-update-slice_fusion.refs_1_.refs_6_), channel_id=1, source_target_pairs={{0,72},{1,7},{2,74},{3,1},{4,76},{5,3},{6,78},{7,5},{8,64},{9,15},... | collective-permute-start | bytes 1769480 | tf_op jit(solution)/shard_map/ppermute | solution.py:28
  23.8 5.2 %collective-permute-done.5.refs_4_.refs_9_ = bf16[256,1152]{1,0:T(8,128)(2,1)S(1)} collective-permute-done((bf16[256,1152]{1,0:T(8,128)(2,1)S(1)}, bf16[256,1152]{1,0:T(8,128)(2,1)S(1)}, u32[]{:S(2)}, u32[]{:S(2)}) %collective-permute-start.5) | collective-permute-done | bytes 589856 | tf_op jit(solution)/shard_map/ppermute | solution.py:28
  29.0 6.3 %collective-permute-done.4.refs_3_.refs_8_ = bf16[256,1152]{1,0:T(8,128)(2,1)S(1)} collective-permute-done((bf16[256,1152]{1,0:T(8,128)(2,1)S(1)}, bf16[256,1152]{1,0:T(8,128)(2,1)S(1)}, u32[]{:S(2)}, u32[]{:S(2)}) %collective-permute-start.4) | collective-permute-done | bytes 589856 | tf_op jit(solution)/shard_map/ppermute | solution.py:28
  36.1 1.1 all-to-all-done
  37.2 1.4 %copy-done = bf16[4,256,1152]{2,1,0:T(8,128)(2,1)} copy-done((bf16[4,256,1152]{2,1,0:T(8,128)(2,1)}, bf16[4,256,1152]{2,1,0:T(8,128)(2,1)S(1)}, u32[]{:S(2)}) %copy-start) | copy-done | bytes 2359320
  38.6 1.9 %collective-permute-start.6 = (bf16[1024,1152]{1,0:T(8,128)(2,1)}, bf16[1024,1152]{1,0:T(8,128)(2,1)S(1)}, u32[]{:S(2)}, u32[]{:S(2)}) collective-permute-start(bf16[1024,1152]{1,0:T(8,128)(2,1)} %shard_map.86.refs_4_), channel_id=1, source_target_pairs={{0,1},{1,0},{2,3},{3,2},{4,5},{5,4},{6,7},{7,6},{8,9},{9,8},{10,11... | collective-permute-start | bytes 7077896 | tf_op jit(solution)/shard_map/ppermute | solution.py:28
  42.1 0.8 reshape.285
  43.9 1.0 collective-permute-done.6.refs_5_
  44.8 24.8 %shard_map.87 = (f32[1024,1152]{1,0:T(8,128)S(1)}, f32[1024,1152]{1,0:T(8,128)S(1)}, f32[256,1152]{1,0:T(8,128)S(1)}, f32[256,1152]{1,0:T(8,128)S(1)}, f32[256,1...) custom-call(f32[3]{0:T(128)S(1)} %pad_maximum_fusion.refs_0_, s32[8]{0:T(128)S(1)} %pad_add_fusion.refs_1_, ...), custom_call_target="tpu_custom_call" | custom-call | flops 14495514624 | bytes 7077888 | tf_op jit(solution)/shard_map/pallas_call | solution.py:207
  70.7 2.6 %collective-permute-start.8 = (f16[256,1152]{1,0:T(8,128)(2,1)S(1)}, f16[256,1152]{1,0:T(8,128)(2,1)S(1)}, u32[]{:S(2)}, u32[]{:S(2)}) collective-permute-start(f16[256,1152]{1,0:T(8,128)(2,1)S(1)} %multiply_convert_fusion.5), channel_id=1, source_target_pairs={{0,72},{1,7},{2,74},{3,1},{4,76},{5,3},{6,78},{7,5},{8,64},{9,15},... | collective-permute-start | bytes 1769480 | tf_op jit(solution)/shard_map/ppermute | solution.py:28
  73.6 1.1 collective-permute-done.9
  74.9 2.8 %collective-permute-start.10 = (f16[256,1152]{1,0:T(8,128)(2,1)S(1)}, f16[256,1152]{1,0:T(8,128)(2,1)S(1)}, u32[]{:S(2)}, u32[]{:S(2)}) collective-permute-start(f16[256,1152]{1,0:T(8,128)(2,1)S(1)} %multiply_convert_fusion.4), channel_id=1, source_target_pairs={{0,8},{1,5},{2,10},{3,7},{4,12},{5,1},{6,14},{7,3},{8,0},{9,13},{1... | collective-permute-start | bytes 1769480 | tf_op jit(solution)/shard_map/ppermute | solution.py:28
  77.7 2.0 %multiply_convert_fusion.3 = (f16[256,1152]{1,0:T(8,128)(2,1)}, f16[256,1152]{1,0:T(8,128)(2,1)}, f16[256,1152]{1,0:T(8,128)(2,1)S(1)}, f32[256,1152]{1,0:T(8,128)S(1)}) fusion(f32[1024,1152]{1,0:T(8,128)S(1)} %get-tuple-element.26, f16[1024,1152]{1,0:T(8,128)(2,1)S(1)} %collective-permute-done.9), kind=kLoop, calls=%fused_computation.5 | loop fusion | flops 5308416 | bytes 10027008 | tf_op jit(solution)/shard_map/convert_element_type | solution.py:238
  79.7 0.9 collective-permute-start.14
  80.5 2.4 %collective-permute-start.16 = (f16[256,1152]{1,0:T(8,128)(2,1)}, f16[256,1152]{1,0:T(8,128)(2,1)}, u32[]{:S(2)}, u32[]{:S(2)}) collective-permute-start(f16[256,1152]{1,0:T(8,128)(2,1)} %get-tuple-element.34), channel_id=1, source_target_pairs={{0,32},{1,33},{2,34},{3,35},{4,36},{5,37},{6,38},{7,39},{8,40},{9,... | collective-permute-start | bytes 1769480 | tf_op jit(solution)/shard_map/ppermute | solution.py:28
  82.9 3.4 %collective-permute-done.8 = f16[256,1152]{1,0:T(8,128)(2,1)S(1)} collective-permute-done((f16[256,1152]{1,0:T(8,128)(2,1)S(1)}, f16[256,1152]{1,0:T(8,128)(2,1)S(1)}, u32[]{:S(2)}, u32[]{:S(2)}) %collective-permute-start.8) | collective-permute-done | bytes 589856 | tf_op jit(solution)/shard_map/ppermute | solution.py:28
  86.4 2.5 %collective-permute-start.15 = (f16[256,1152]{1,0:T(8,128)(2,1)S(1)}, f16[256,1152]{1,0:T(8,128)(2,1)}, u32[]{:S(2)}, u32[]{:S(2)}) collective-permute-start(f16[256,1152]{1,0:T(8,128)(2,1)S(1)} %get-tuple-element.35), channel_id=1, source_target_pairs={{0,48},{1,49},{2,50},{3,51},{4,52},{5,53},{6,54},{7,55},{8,56},{9,... | collective-permute-start | bytes 1769480 | tf_op jit(solution)/shard_map/ppermute | solution.py:28
  88.8 1.4 %collective-permute-done.7 = f16[256,1152]{1,0:T(8,128)(2,1)S(1)} collective-permute-done((f16[256,1152]{1,0:T(8,128)(2,1)S(1)}, f16[256,1152]{1,0:T(8,128)(2,1)S(1)}, u32[]{:S(2)}, u32[]{:S(2)}) %collective-permute-start.7) | collective-permute-done | bytes 589856 | tf_op jit(solution)/shard_map/ppermute | solution.py:28
  91.4 7.9 %all-to-all-start.1 = ((f32[128,1,128]{2,1,0:T(1,128)}), f32[128,1,128]{2,1,0:T(1,128)}, u32[]{:S(2)}, u32[]{:S(2)}) async-start(f32[128,1,128]{2,1,0:T(1,128)} %broadcast_in_dim.20), calls=%async_computation.1 | async-start | bytes 131072 | tf_op jit(solution)/shard_map/all_to_all | solution.py:234
  99.4 1.6 %collective-permute-start.11 = (f16[64,1152]{1,0:T(8,128)(2,1)S(1)}, f16[64,1152]{1,0:T(8,128)(2,1)S(1)}, u32[]{:S(2)}, u32[]{:S(2)}) collective-permute-start(f16[64,1152]{1,0:T(8,128)(2,1)S(1)} %get-tuple-element.37), channel_id=1, source_target_pairs={{0,2},{1,65},{2,4},{3,67},{4,6},{5,69},{6,0},{7,71},{8,10},{9,73},... | collective-permute-start | bytes 442376 | tf_op jit(solution)/shard_map/ppermute | solution.py:28
  101.0 1.8 %collective-permute-start.13 = (f16[64,1152]{1,0:T(8,128)(2,1)S(1)}, f16[64,1152]{1,0:T(8,128)(2,1)S(1)}, u32[]{:S(2)}, u32[]{:S(2)}) collective-permute-start(f16[64,1152]{1,0:T(8,128)(2,1)S(1)} %get-tuple-element.38), channel_id=1, source_target_pairs={{0,6},{1,73},{2,0},{3,75},{4,2},{5,77},{6,4},{7,79},{8,14},{9,65},... | collective-permute-start | bytes 442376 | tf_op jit(solution)/shard_map/ppermute | solution.py:28
  102.8 1.4 %collective-permute-start.12 = (f16[64,1152]{1,0:T(8,128)(2,1)S(1)}, f16[64,1152]{1,0:T(8,128)(2,1)S(1)}, u32[]{:S(2)}, u32[]{:S(2)}) collective-permute-start(f16[64,1152]{1,0:T(8,128)(2,1)S(1)} %get-tuple-element.39), channel_id=1, source_target_pairs={{0,4},{1,9},{2,6},{3,11},{4,0},{5,13},{6,2},{7,15},{8,12},{9,1},{1... | collective-permute-start | bytes 442376 | tf_op jit(solution)/shard_map/ppermute | solution.py:28
  104.3 4.7 %collective-permute-done.16 = f16[256,1152]{1,0:T(8,128)(2,1)} collective-permute-done((f16[256,1152]{1,0:T(8,128)(2,1)}, f16[256,1152]{1,0:T(8,128)(2,1)}, u32[]{:S(2)}, u32[]{:S(2)}) %collective-permute-start.16) | collective-permute-done | bytes 589856 | tf_op jit(solution)/shard_map/ppermute | solution.py:28
  109.1 1.8 %multiply_add_fusion.refs_5_ = f32[256,1152]{1,0:T(8,128)S(1)} fusion(f16[256,1152]{1,0:T(8,128)(2,1)} %collective-permute-done.16, f16[256,1152]{1,0:T(8,128)(2,1)} %collective-permute-done.15, f32[256,1152]{1,0:T(8,128)S(1)} %get-tuple-element.36, f16[256,1152]{1,0:T(8,128)(2,1)} %collective-permute-done.14), kind=kLoop, calls=%fused_computation.2 | loop fusion | flops 2654208 | bytes 4128768 | tf_op jit(solution)/shard_map/add | solution.py:292
  111.0 1.6 %all-to-all-done.1.refs_6_ = f32[128,1,128]{2,1,0:T(1,128)} async-done(((f32[128,1,128]{2,1,0:T(1,128)}), f32[128,1,128]{2,1,0:T(1,128)}, u32[]{:S(2)}, u32[]{:S(2)}) %all-to-all-start.1) | async-done | bytes 65568 | tf_op jit(solution)/shard_map/all_to_all | solution.py:234
  112.6 2.9 %shard_map.88 = (f32[64,1152]{1,0:T(8,128)}, f32[256,1152]{1,0:T(8,128)}, f32[1,1]{1,0:T(1,128)}) custom-call(f32[64,1152]{1,0:T(8,128)} %refs_0_.1, f32[64,1]{1,0:T(8,128)} %get-tuple-element.17.refs_1_, f32[64,1152]{1,0:T(8,128)S(1)} %fusion.2.refs_2_, f32[256,1152]{1,0:T(8,128)} %refs_3_.1, f32[256,1]{1,0:T(8,128)} %get-tuple-element.25.refs_4_, ...), custom_call_target="tpu_custom_call" | custom-call | tf_op jit(solution)/shard_map/pallas_call | solution.py:113
  (58 shorter events, 6.3 us)
Async XLA Ops:
  3.8 5.2 %copy-start.4 = (bf16[64,1152]{1,0:T(8,128)(2,1)S(1)}, bf16[64,1152]{1,0:T(8,128)(2,1)}, u32[]{:S(2)}) copy-start(bf16[64,1152]{1,0:T(8,128)(2,1)} %get-tuple-element.19) | copy-start | bytes 442372
  3.8 33.4 %all-to-all-start = ((bf16[4,256,1152]{2,1,0:T(8,128)(2,1)}), bf16[4,256,1152]{2,1,0:T(8,128)(2,1)S(1)}, u32[]{:S(2)}, u32[]{:S(2)}) async-start(bf16[4,256,1152]{2,1,0:T(8,128)(2,1)} %get-tuple-element.18), calls=%async_computation | async-start | bytes 4718592 | tf_op jit(solution)/shard_map/all_to_all | solution.py:260
  8.9 9.4 %collective-permute-start.2 = (bf16[64,1152]{1,0:T(8,128)(2,1)S(1)}, bf16[64,1152]{1,0:T(8,128)(2,1)S(1)}, u32[]{:S(2)}, u32[]{:S(2)}) collective-permute-start(bf16[64,1152]{1,0:T(8,128)(2,1)S(1)} %copy-done.4), channel_id=1, source_target_pairs={{0,2},{1,65},{2,4},{3,67},{4,6},{5,69},{6,0},{7,71},{8,10},{9,73},... | collective-permute-start | bytes 442376 | tf_op jit(solution)/shard_map/ppermute | solution.py:28
  10.6 7.7 %collective-permute-start.1 = (bf16[64,1152]{1,0:T(8,128)(2,1)S(1)}, bf16[64,1152]{1,0:T(8,128)(2,1)S(1)}, u32[]{:S(2)}, u32[]{:S(2)}) collective-permute-start(bf16[64,1152]{1,0:T(8,128)(2,1)S(1)} %copy-done.4), channel_id=1, source_target_pairs={{0,4},{1,9},{2,6},{3,11},{4,0},{5,13},{6,2},{7,15},{8,12},{9,1},{1... | collective-permute-start | bytes 442376 | tf_op jit(solution)/shard_map/ppermute | solution.py:28
  13.9 4.3 %collective-permute-start = (bf16[64,1152]{1,0:T(8,128)(2,1)S(1)}, bf16[64,1152]{1,0:T(8,128)(2,1)S(1)}, u32[]{:S(2)}, u32[]{:S(2)}) collective-permute-start(bf16[64,1152]{1,0:T(8,128)(2,1)S(1)} %copy-done.4), channel_id=1, source_target_pairs={{0,6},{1,73},{2,0},{3,75},{4,2},{5,77},{6,4},{7,79},{8,14},{9,65},... | collective-permute-start | bytes 442376 | tf_op jit(solution)/shard_map/ppermute | solution.py:28
  18.3 18.8 %copy-start.1 = (bf16[256,1152]{1,0:T(8,128)(2,1)}, bf16[256,1152]{1,0:T(8,128)(2,1)S(1)}, u32[]{:S(2)}) copy-start(bf16[256,1152]{1,0:T(8,128)(2,1)S(1)} %constant_dynamic-update-slice_fusion.refs_1_.refs_6_) | copy-start | bytes 1769476
  18.3 10.7 %collective-permute-start.5 = (bf16[256,1152]{1,0:T(8,128)(2,1)S(1)}, bf16[256,1152]{1,0:T(8,128)(2,1)S(1)}, u32[]{:S(2)}, u32[]{:S(2)}) collective-permute-start(bf16[256,1152]{1,0:T(8,128)(2,1)S(1)} %constant_dynamic-update-slice_fusion.refs_1_.refs_6_), channel_id=1, source_target_pairs={{0,8},{1,5},{2,10},{3,7},{4,12},{5,1},{6,14},{7,3},{8,0},{9,13},{1... | collective-permute-start | bytes 1769480 | tf_op jit(solution)/shard_map/ppermute | solution.py:28
  21.1 14.2 %collective-permute-start.4 = (bf16[256,1152]{1,0:T(8,128)(2,1)S(1)}, bf16[256,1152]{1,0:T(8,128)(2,1)S(1)}, u32[]{:S(2)}, u32[]{:S(2)}) collective-permute-start(bf16[256,1152]{1,0:T(8,128)(2,1)S(1)} %constant_dynamic-update-slice_fusion.refs_1_.refs_6_), channel_id=1, source_target_pairs={{0,64},{1,3},{2,66},{3,5},{4,68},{5,7},{6,70},{7,1},{8,72},{9,11},... | collective-permute-start | bytes 1769480 | tf_op jit(solution)/shard_map/ppermute | solution.py:28
  21.4 14.7 %collective-permute-start.3 = (bf16[256,1152]{1,0:T(8,128)(2,1)S(1)}, bf16[256,1152]{1,0:T(8,128)(2,1)}, u32[]{:S(2)}, u32[]{:S(2)}) collective-permute-start(bf16[256,1152]{1,0:T(8,128)(2,1)S(1)} %constant_dynamic-update-slice_fusion.refs_1_.refs_6_), channel_id=1, source_target_pairs={{0,72},{1,7},{2,74},{3,1},{4,76},{5,3},{6,78},{7,5},{8,64},{9,15},... | collective-permute-start | bytes 1769480 | tf_op jit(solution)/shard_map/ppermute | solution.py:28
  29.0 8.2 %copy-start.2 = (bf16[256,1152]{1,0:T(8,128)(2,1)}, bf16[256,1152]{1,0:T(8,128)(2,1)S(1)}, u32[]{:S(2)}) copy-start(bf16[256,1152]{1,0:T(8,128)(2,1)S(1)} %collective-permute-done.5.refs_4_.refs_9_) | copy-start | bytes 1769476
  35.3 0.8 copy-start.3
  37.2 1.4 %copy-start = (bf16[4,256,1152]{2,1,0:T(8,128)(2,1)}, bf16[4,256,1152]{2,1,0:T(8,128)(2,1)S(1)}, u32[]{:S(2)}) copy-start(bf16[4,256,1152]{2,1,0:T(8,128)(2,1)S(1)} %all-to-all-done) | copy-start | bytes 7077892
  38.6 1.9 %copy-start.5 = (s32[4]{0:T(128)S(1)}, s32[4]{0:T(128)}, u32[]{:S(2)}) copy-start(s32[4]{0:T(128)} %constant.206.clone) | copy-start | bytes 52
  38.6 6.2 %collective-permute-start.6 = (bf16[1024,1152]{1,0:T(8,128)(2,1)}, bf16[1024,1152]{1,0:T(8,128)(2,1)S(1)}, u32[]{:S(2)}, u32[]{:S(2)}) collective-permute-start(bf16[1024,1152]{1,0:T(8,128)(2,1)} %shard_map.86.refs_4_), channel_id=1, source_target_pairs={{0,1},{1,0},{2,3},{3,2},{4,5},{5,4},{6,7},{7,6},{8,9},{9,8},{10,11... | collective-permute-start | bytes 7077896 | tf_op jit(solution)/shard_map/ppermute | solution.py:28
  70.1 4.6 %collective-permute-start.9 = (f16[1024,1152]{1,0:T(8,128)(2,1)S(1)}, f16[1024,1152]{1,0:T(8,128)(2,1)S(1)}, u32[]{:S(2)}, u32[]{:S(2)}) collective-permute-start(f16[1024,1152]{1,0:T(8,128)(2,1)S(1)} %multiply_convert_fusion), channel_id=1, source_target_pairs={{0,1},{1,0},{2,3},{3,2},{4,5},{5,4},{6,7},{7,6},{8,9},{9,8},{10,11... | collective-permute-start | bytes 7077896 | tf_op jit(solution)/shard_map/ppermute | solution.py:28
  70.7 15.7 %collective-permute-start.8 = (f16[256,1152]{1,0:T(8,128)(2,1)S(1)}, f16[256,1152]{1,0:T(8,128)(2,1)S(1)}, u32[]{:S(2)}, u32[]{:S(2)}) collective-permute-start(f16[256,1152]{1,0:T(8,128)(2,1)S(1)} %multiply_convert_fusion.5), channel_id=1, source_target_pairs={{0,72},{1,7},{2,74},{3,1},{4,76},{5,3},{6,78},{7,5},{8,64},{9,15},... | collective-permute-start | bytes 1769480 | tf_op jit(solution)/shard_map/ppermute | solution.py:28
  73.3 17.0 %collective-permute-start.7 = (f16[256,1152]{1,0:T(8,128)(2,1)S(1)}, f16[256,1152]{1,0:T(8,128)(2,1)S(1)}, u32[]{:S(2)}, u32[]{:S(2)}) collective-permute-start(f16[256,1152]{1,0:T(8,128)(2,1)S(1)} %multiply_convert_fusion.6), channel_id=1, source_target_pairs={{0,64},{1,3},{2,66},{3,5},{4,68},{5,7},{6,70},{7,1},{8,72},{9,11},... | collective-permute-start | bytes 1769480 | tf_op jit(solution)/shard_map/ppermute | solution.py:28
  74.9 15.4 %collective-permute-start.10 = (f16[256,1152]{1,0:T(8,128)(2,1)S(1)}, f16[256,1152]{1,0:T(8,128)(2,1)S(1)}, u32[]{:S(2)}, u32[]{:S(2)}) collective-permute-start(f16[256,1152]{1,0:T(8,128)(2,1)S(1)} %multiply_convert_fusion.4), channel_id=1, source_target_pairs={{0,8},{1,5},{2,10},{3,7},{4,12},{5,1},{6,14},{7,3},{8,0},{9,13},{1... | collective-permute-start | bytes 1769480 | tf_op jit(solution)/shard_map/ppermute | solution.py:28
  79.7 23.2 %collective-permute-start.14 = (f16[256,1152]{1,0:T(8,128)(2,1)}, f16[256,1152]{1,0:T(8,128)(2,1)}, u32[]{:S(2)}, u32[]{:S(2)}) collective-permute-start(f16[256,1152]{1,0:T(8,128)(2,1)} %get-tuple-element.33), channel_id=1, source_target_pairs={{0,16},{1,17},{2,18},{3,19},{4,20},{5,21},{6,22},{7,23},{8,24},{9,... | collective-permute-start | bytes 1769480 | tf_op jit(solution)/shard_map/ppermute | solution.py:28
  80.5 28.4 %collective-permute-start.16 = (f16[256,1152]{1,0:T(8,128)(2,1)}, f16[256,1152]{1,0:T(8,128)(2,1)}, u32[]{:S(2)}, u32[]{:S(2)}) collective-permute-start(f16[256,1152]{1,0:T(8,128)(2,1)} %get-tuple-element.34), channel_id=1, source_target_pairs={{0,32},{1,33},{2,34},{3,35},{4,36},{5,37},{6,38},{7,39},{8,40},{9,... | collective-permute-start | bytes 1769480 | tf_op jit(solution)/shard_map/ppermute | solution.py:28
  86.4 22.8 %collective-permute-start.15 = (f16[256,1152]{1,0:T(8,128)(2,1)S(1)}, f16[256,1152]{1,0:T(8,128)(2,1)}, u32[]{:S(2)}, u32[]{:S(2)}) collective-permute-start(f16[256,1152]{1,0:T(8,128)(2,1)S(1)} %get-tuple-element.35), channel_id=1, source_target_pairs={{0,48},{1,49},{2,50},{3,51},{4,52},{5,53},{6,54},{7,55},{8,56},{9,... | collective-permute-start | bytes 1769480 | tf_op jit(solution)/shard_map/ppermute | solution.py:28
  91.4 21.2 %all-to-all-start.1 = ((f32[128,1,128]{2,1,0:T(1,128)}), f32[128,1,128]{2,1,0:T(1,128)}, u32[]{:S(2)}, u32[]{:S(2)}) async-start(f32[128,1,128]{2,1,0:T(1,128)} %broadcast_in_dim.20), calls=%async_computation.1 | async-start | bytes 131072 | tf_op jit(solution)/shard_map/all_to_all | solution.py:234
  99.4 11.5 %collective-permute-start.11 = (f16[64,1152]{1,0:T(8,128)(2,1)S(1)}, f16[64,1152]{1,0:T(8,128)(2,1)S(1)}, u32[]{:S(2)}, u32[]{:S(2)}) collective-permute-start(f16[64,1152]{1,0:T(8,128)(2,1)S(1)} %get-tuple-element.37), channel_id=1, source_target_pairs={{0,2},{1,65},{2,4},{3,67},{4,6},{5,69},{6,0},{7,71},{8,10},{9,73},... | collective-permute-start | bytes 442376 | tf_op jit(solution)/shard_map/ppermute | solution.py:28
  101.0 9.9 %collective-permute-start.13 = (f16[64,1152]{1,0:T(8,128)(2,1)S(1)}, f16[64,1152]{1,0:T(8,128)(2,1)S(1)}, u32[]{:S(2)}, u32[]{:S(2)}) collective-permute-start(f16[64,1152]{1,0:T(8,128)(2,1)S(1)} %get-tuple-element.38), channel_id=1, source_target_pairs={{0,6},{1,73},{2,0},{3,75},{4,2},{5,77},{6,4},{7,79},{8,14},{9,65},... | collective-permute-start | bytes 442376 | tf_op jit(solution)/shard_map/ppermute | solution.py:28
  102.8 8.1 %collective-permute-start.12 = (f16[64,1152]{1,0:T(8,128)(2,1)S(1)}, f16[64,1152]{1,0:T(8,128)(2,1)S(1)}, u32[]{:S(2)}, u32[]{:S(2)}) collective-permute-start(f16[64,1152]{1,0:T(8,128)(2,1)S(1)} %get-tuple-element.39), channel_id=1, source_target_pairs={{0,4},{1,9},{2,6},{3,11},{4,0},{5,13},{6,2},{7,15},{8,12},{9,1},{1... | collective-permute-start | bytes 442376 | tf_op jit(solution)/shard_map/ppermute | solution.py:28

commit v5 on v4

--- a/solution.py
+++ b/solution.py
@@ -285,7 +285,10 @@
     n = text_rows
     other = send(narrow(other), swap)
     wires = [
-        narrow(mine[s * n : (s + 1) * n] + wide(other[s * n : (s + 1) * n])) for s in (1, 3, 2)
+        lax.optimization_barrier(
+            narrow(mine[s * n : (s + 1) * n] + wide(other[s * n : (s + 1) * n]))
+        )
+        for s in (1, 3, 2)
     ]
     text_dir = lax.optimization_barrier(mine[:n] + wide(other[:n]))
     for s, wire in zip((1, 3, 2), wires):
@@ -297,7 +300,7 @@
         line_dir = line_dir + wide(send(narrow(part), along_second(s)))
     loss = loss_parts(after(loss, [line_dir]))
     n = image_rows
-    wire = narrow(line_dir[n:])
+    wire = lax.optimization_barrier(narrow(line_dir[n:]))
     image_dir = line_dir[:n]
     for r in (1, 2, 3):
         image_dir = image_dir + wide(send(wire[(r - 1) * n : r * n], along_first(r)))

time: 117 us -> 115 us (0.983); the launches traced: 116 us -> 115 us
    all_to_all x1, waiting for transfers between devices: 1.56 us -> 0.05 us  [loss_parts(): return lax.all_to_all(parts, AXES, 0, 0, tiled=True)]
    ppermute x17, waiting for transfers between devices: 27 us -> 28.4 us  [send(): return lax.ppermute(value, AXES, pairs)]
  transfers between devices with their start and end apart: 19 -> 19, of which waited for: 12 -> 11; matrix products, arithmetic and copies ran while one was open for 6% -> 7% of each run, Pallas kernels for 0% -> 0%
where the time goes in v5:
time: 115 us
  starting transfers between devices  42.1 us (37%)
  Pallas kernels  30.9 us (27%)
  waiting for transfers between devices  29.5 us (26%)
  other arithmetic  5.48 us (5%)
  local copies, waits for them, and re-layouts  4.72 us (4%)
  between operations  2.18 us (2%)
    ppermute x17, starting transfers between devices, send(): return lax.ppermute(value, AXES, pairs)  29 us
    ppermute x17, waiting for transfers between devices, send(): return lax.ppermute(value, AXES, pairs)  28.4 us
    pallas_call x1, Pallas kernels, pair_block(): pl.pallas_call(functools.partial(pair_kernel, n_image), out_shape=out_sha...  24.8 us
    all_to_all x1, starting transfers between devices, loss_parts(): return lax.all_to_all(parts, AXES, 0, 0, tiled=True)  7.9 us
    all_to_all x1, starting transfers between devices, body(): lax.all_to_all(own, AXES, 0, 0, axis_index_groups=list(rings.values()), t...  5.15 us
    pallas_call x1, Pallas kernels, prepare(): pl.pallas_call(prepare_kernel, out_shape=(jax.ShapeDtypeStruct((RING,) +...  3.16 us
    pallas_call x1, Pallas kernels, finish(): pl.pallas_call(finish_kernel, out_shape=(jax.ShapeDtypeStruct(images[2].s...  2.93 us
    convert_element_type x6, other arithmetic, narrow(): return (part * 0.25).astype(WIRE)  2.83 us
  transfers between devices with their start and end apart: 19, of which 11 were waited for; matrix products, arithmetic and copies ran while one was open for 7% of the time, Pallas kernels for 0%

profile of v5, /device:TPU:1, one launch (start us, length us, event | category | flops | bytes accessed | tf_op | source)
XLA Modules:
  0.0 114.9 jit_solution(186724352027226012)
XLA Ops:
  0.6 3.2 %shard_map.85 = (bf16[4,256,1152]{2,1,0:T(8,128)(2,1)}, f32[256,1]{1,0:T(8,128)}, bf16[64,1152]{1,0:T(8,128)(2,1)}, f32[64,1]{1,0:T(8,128)}) custom-call(f32[256,1152]{1,0:T(8,128)} %refs_3_.1, f32[64,1152]{1,0:T(8,128)} %refs_0_.1), custom_call_target="tpu_custom_call" | custom-call | tf_op jit(solution)/shard_map/pallas_call | solution.py:69
  3.8 5.1 %all-to-all-start = ((bf16[4,256,1152]{2,1,0:T(8,128)(2,1)}), bf16[4,256,1152]{2,1,0:T(8,128)(2,1)S(1)}, u32[]{:S(2)}, u32[]{:S(2)}) async-start(bf16[4,256,1152]{2,1,0:T(8,128)(2,1)} %get-tuple-element.18), calls=%async_computation | async-start | bytes 4718592 | tf_op jit(solution)/shard_map/all_to_all | solution.py:260
  8.9 1.6 %collective-permute-start.2 = (bf16[64,1152]{1,0:T(8,128)(2,1)S(1)}, bf16[64,1152]{1,0:T(8,128)(2,1)S(1)}, u32[]{:S(2)}, u32[]{:S(2)}) collective-permute-start(bf16[64,1152]{1,0:T(8,128)(2,1)S(1)} %copy-done.4), channel_id=1, source_target_pairs={{0,2},{1,65},{2,4},{3,67},{4,6},{5,69},{6,0},{7,71},{8,10},{9,73},... | collective-permute-start | bytes 442376 | tf_op jit(solution)/shard_map/ppermute | solution.py:28
  10.6 3.3 %collective-permute-start.1 = (bf16[64,1152]{1,0:T(8,128)(2,1)S(1)}, bf16[64,1152]{1,0:T(8,128)(2,1)S(1)}, u32[]{:S(2)}, u32[]{:S(2)}) collective-permute-start(bf16[64,1152]{1,0:T(8,128)(2,1)S(1)} %copy-done.4), channel_id=1, source_target_pairs={{0,4},{1,9},{2,6},{3,11},{4,0},{5,13},{6,2},{7,15},{8,12},{9,1},{1... | collective-permute-start | bytes 442376 | tf_op jit(solution)/shard_map/ppermute | solution.py:28
  13.9 0.7 collective-permute-start
  14.6 3.5 %collective-permute-done = bf16[64,1152]{1,0:T(8,128)(2,1)S(1)} collective-permute-done((bf16[64,1152]{1,0:T(8,128)(2,1)S(1)}, bf16[64,1152]{1,0:T(8,128)(2,1)S(1)}, u32[]{:S(2)}, u32[]{:S(2)}) %collective-permute-start) | collective-permute-done | bytes 147488 | tf_op jit(solution)/shard_map/ppermute | solution.py:28
  18.3 2.7 %collective-permute-start.5 = (bf16[256,1152]{1,0:T(8,128)(2,1)S(1)}, bf16[256,1152]{1,0:T(8,128)(2,1)S(1)}, u32[]{:S(2)}, u32[]{:S(2)}) collective-permute-start(bf16[256,1152]{1,0:T(8,128)(2,1)S(1)} %constant_dynamic-update-slice_fusion.refs_1_.refs_6_), channel_id=1, source_target_pairs={{0,8},{1,5},{2,10},{3,7},{4,12},{5,1},{6,14},{7,3},{8,0},{9,13},{1... | collective-permute-start | bytes 1769480 | tf_op jit(solution)/shard_map/ppermute | solution.py:28
  21.4 2.4 %collective-permute-start.3 = (bf16[256,1152]{1,0:T(8,128)(2,1)S(1)}, bf16[256,1152]{1,0:T(8,128)(2,1)}, u32[]{:S(2)}, u32[]{:S(2)}) collective-permute-start(bf16[256,1152]{1,0:T(8,128)(2,1)S(1)} %constant_dynamic-update-slice_fusion.refs_1_.refs_6_), channel_id=1, source_target_pairs={{0,72},{1,7},{2,74},{3,1},{4,76},{5,3},{6,78},{7,5},{8,64},{9,15},... | collective-permute-start | bytes 1769480 | tf_op jit(solution)/shard_map/ppermute | solution.py:28
  23.8 5.2 %collective-permute-done.5.refs_4_.refs_9_ = bf16[256,1152]{1,0:T(8,128)(2,1)S(1)} collective-permute-done((bf16[256,1152]{1,0:T(8,128)(2,1)S(1)}, bf16[256,1152]{1,0:T(8,128)(2,1)S(1)}, u32[]{:S(2)}, u32[]{:S(2)}) %collective-permute-start.5) | collective-permute-done | bytes 589856 | tf_op jit(solution)/shard_map/ppermute | solution.py:28
  29.0 6.3 %collective-permute-done.4.refs_3_.refs_8_ = bf16[256,1152]{1,0:T(8,128)(2,1)S(1)} collective-permute-done((bf16[256,1152]{1,0:T(8,128)(2,1)S(1)}, bf16[256,1152]{1,0:T(8,128)(2,1)S(1)}, u32[]{:S(2)}, u32[]{:S(2)}) %collective-permute-start.4) | collective-permute-done | bytes 589856 | tf_op jit(solution)/shard_map/ppermute | solution.py:28
  35.3 0.8 copy-done.3
  36.1 1.1 all-to-all-done
  37.2 1.4 %copy-done = bf16[4,256,1152]{2,1,0:T(8,128)(2,1)} copy-done((bf16[4,256,1152]{2,1,0:T(8,128)(2,1)}, bf16[4,256,1152]{2,1,0:T(8,128)(2,1)S(1)}, u32[]{:S(2)}) %copy-start) | copy-done | bytes 2359320
  38.6 1.9 %collective-permute-start.6 = (bf16[1024,1152]{1,0:T(8,128)(2,1)}, bf16[1024,1152]{1,0:T(8,128)(2,1)S(1)}, u32[]{:S(2)}, u32[]{:S(2)}) collective-permute-start(bf16[1024,1152]{1,0:T(8,128)(2,1)} %shard_map.86.refs_4_), channel_id=1, source_target_pairs={{0,1},{1,0},{2,3},{3,2},{4,5},{5,4},{6,7},{7,6},{8,9},{9,8},{10,11... | collective-permute-start | bytes 7077896 | tf_op jit(solution)/shard_map/ppermute | solution.py:28
  42.1 0.8 reshape.285
  43.9 1.0 collective-permute-done.6.refs_5_
  44.8 24.8 %shard_map.87 = (f32[1024,1152]{1,0:T(8,128)S(1)}, f32[1024,1152]{1,0:T(8,128)S(1)}, f32[256,1152]{1,0:T(8,128)S(1)}, f32[256,1152]{1,0:T(8,128)S(1)}, f32[256,1...) custom-call(f32[3]{0:T(128)S(1)} %pad_maximum_fusion.refs_0_, s32[8]{0:T(128)S(1)} %pad_add_fusion.refs_1_, ...), custom_call_target="tpu_custom_call" | custom-call | flops 14495514624 | bytes 7077888 | tf_op jit(solution)/shard_map/pallas_call | solution.py:207
  70.7 2.6 %collective-permute-start.8 = (f16[256,1152]{1,0:T(8,128)(2,1)S(1)}, f16[256,1152]{1,0:T(8,128)(2,1)S(1)}, u32[]{:S(2)}, u32[]{:S(2)}) collective-permute-start(f16[256,1152]{1,0:T(8,128)(2,1)S(1)} %multiply_convert_fusion.5), channel_id=1, source_target_pairs={{0,72},{1,7},{2,74},{3,1},{4,76},{5,3},{6,78},{7,5},{8,64},{9,15},... | collective-permute-start | bytes 1769480 | tf_op jit(solution)/shard_map/ppermute | solution.py:28
  73.6 1.1 collective-permute-done.9
  74.9 2.8 %collective-permute-start.10 = (f16[256,1152]{1,0:T(8,128)(2,1)S(1)}, f16[256,1152]{1,0:T(8,128)(2,1)S(1)}, u32[]{:S(2)}, u32[]{:S(2)}) collective-permute-start(f16[256,1152]{1,0:T(8,128)(2,1)S(1)} %multiply_convert_fusion.4), channel_id=1, source_target_pairs={{0,8},{1,5},{2,10},{3,7},{4,12},{5,1},{6,14},{7,3},{8,0},{9,13},{1... | collective-permute-start | bytes 1769480 | tf_op jit(solution)/shard_map/ppermute | solution.py:28
  77.7 2.0 %multiply_convert_fusion.3 = (f16[256,1152]{1,0:T(8,128)(2,1)}, f16[256,1152]{1,0:T(8,128)(2,1)}, f16[256,1152]{1,0:T(8,128)(2,1)S(1)}, f32[256,1152]{1,0:T(8,128)S(1)}) fusion(f32[1024,1152]{1,0:T(8,128)S(1)} %get-tuple-element.26, f16[1024,1152]{1,0:T(8,128)(2,1)S(1)} %collective-permute-done.9), kind=kLoop, calls=%fused_computation.5 | loop fusion | flops 5308416 | bytes 10027008 | tf_op jit(solution)/shard_map/convert_element_type | solution.py:238
  79.7 2.4 %collective-permute-start.16 = (f16[256,1152]{1,0:T(8,128)(2,1)}, f16[256,1152]{1,0:T(8,128)(2,1)}, u32[]{:S(2)}, u32[]{:S(2)}) collective-permute-start(f16[256,1152]{1,0:T(8,128)(2,1)} %get-tuple-element.34), channel_id=1, source_target_pairs={{0,32},{1,33},{2,34},{3,35},{4,36},{5,37},{6,38},{7,39},{8,40},{9,... | collective-permute-start | bytes 1769480 | tf_op jit(solution)/shard_map/ppermute | solution.py:28
  82.3 4.0 %collective-permute-done.8 = f16[256,1152]{1,0:T(8,128)(2,1)S(1)} collective-permute-done((f16[256,1152]{1,0:T(8,128)(2,1)S(1)}, f16[256,1152]{1,0:T(8,128)(2,1)S(1)}, u32[]{:S(2)}, u32[]{:S(2)}) %collective-permute-start.8) | collective-permute-done | bytes 589856 | tf_op jit(solution)/shard_map/ppermute | solution.py:28
  86.4 2.5 %collective-permute-start.15 = (f16[256,1152]{1,0:T(8,128)(2,1)S(1)}, f16[256,1152]{1,0:T(8,128)(2,1)}, u32[]{:S(2)}, u32[]{:S(2)}) collective-permute-start(f16[256,1152]{1,0:T(8,128)(2,1)S(1)} %get-tuple-element.35), channel_id=1, source_target_pairs={{0,48},{1,49},{2,50},{3,51},{4,52},{5,53},{6,54},{7,55},{8,56},{9,... | collective-permute-start | bytes 1769480 | tf_op jit(solution)/shard_map/ppermute | solution.py:28
  88.8 1.4 %collective-permute-done.7 = f16[256,1152]{1,0:T(8,128)(2,1)S(1)} collective-permute-done((f16[256,1152]{1,0:T(8,128)(2,1)S(1)}, f16[256,1152]{1,0:T(8,128)(2,1)S(1)}, u32[]{:S(2)}, u32[]{:S(2)}) %collective-permute-start.7) | collective-permute-done | bytes 589856 | tf_op jit(solution)/shard_map/ppermute | solution.py:28
  91.4 7.9 %all-to-all-start.1 = ((f32[128,1,128]{2,1,0:T(1,128)}), f32[128,1,128]{2,1,0:T(1,128)}, u32[]{:S(2)}, u32[]{:S(2)}) async-start(f32[128,1,128]{2,1,0:T(1,128)} %broadcast_in_dim.20), calls=%async_computation.1 | async-start | bytes 131072 | tf_op jit(solution)/shard_map/all_to_all | solution.py:234
  99.4 1.6 %collective-permute-start.11 = (f16[64,1152]{1,0:T(8,128)(2,1)S(1)}, f16[64,1152]{1,0:T(8,128)(2,1)S(1)}, u32[]{:S(2)}, u32[]{:S(2)}) collective-permute-start(f16[64,1152]{1,0:T(8,128)(2,1)S(1)} %get-tuple-element.37), channel_id=1, source_target_pairs={{0,2},{1,65},{2,4},{3,67},{4,6},{5,69},{6,0},{7,71},{8,10},{9,73},... | collective-permute-start | bytes 442376 | tf_op jit(solution)/shard_map/ppermute | solution.py:28
  101.0 1.8 %collective-permute-start.13 = (f16[64,1152]{1,0:T(8,128)(2,1)S(1)}, f16[64,1152]{1,0:T(8,128)(2,1)S(1)}, u32[]{:S(2)}, u32[]{:S(2)}) collective-permute-start(f16[64,1152]{1,0:T(8,128)(2,1)S(1)} %get-tuple-element.38), channel_id=1, source_target_pairs={{0,6},{1,73},{2,0},{3,75},{4,2},{5,77},{6,4},{7,79},{8,14},{9,65},... | collective-permute-start | bytes 442376 | tf_op jit(solution)/shard_map/ppermute | solution.py:28
  102.8 1.4 %collective-permute-start.12 = (f16[64,1152]{1,0:T(8,128)(2,1)S(1)}, f16[64,1152]{1,0:T(8,128)(2,1)S(1)}, u32[]{:S(2)}, u32[]{:S(2)}) collective-permute-start(f16[64,1152]{1,0:T(8,128)(2,1)S(1)} %get-tuple-element.39), channel_id=1, source_target_pairs={{0,4},{1,9},{2,6},{3,11},{4,0},{5,13},{6,2},{7,15},{8,12},{9,1},{1... | collective-permute-start | bytes 442376 | tf_op jit(solution)/shard_map/ppermute | solution.py:28
  104.3 5.7 %collective-permute-done.14 = f16[256,1152]{1,0:T(8,128)(2,1)} collective-permute-done((f16[256,1152]{1,0:T(8,128)(2,1)}, f16[256,1152]{1,0:T(8,128)(2,1)}, u32[]{:S(2)}, u32[]{:S(2)}) %collective-permute-start.14) | collective-permute-done | bytes 589856 | tf_op jit(solution)/shard_map/ppermute | solution.py:28
  110.0 1.8 %multiply_add_fusion.refs_5_ = f32[256,1152]{1,0:T(8,128)S(1)} fusion(f16[256,1152]{1,0:T(8,128)(2,1)} %collective-permute-done.16, f16[256,1152]{1,0:T(8,128)(2,1)} %collective-permute-done.15, f32[256,1152]{1,0:T(8,128)S(1)} %get-tuple-element.36, f16[256,1152]{1,0:T(8,128)(2,1)} %collective-permute-done.14), kind=kLoop, calls=%fused_computation.2 | loop fusion | flops 2654208 | bytes 4128768 | tf_op jit(solution)/shard_map/add | solution.py:295
  111.9 2.9 %shard_map.88 = (f32[64,1152]{1,0:T(8,128)}, f32[256,1152]{1,0:T(8,128)}, f32[1,1]{1,0:T(1,128)}) custom-call(f32[64,1152]{1,0:T(8,128)} %refs_0_.1, f32[64,1]{1,0:T(8,128)} %get-tuple-element.17.refs_1_, f32[64,1152]{1,0:T(8,128)S(1)} %fusion.2.refs_2_, f32[256,1152]{1,0:T(8,128)} %refs_3_.1, f32[256,1]{1,0:T(8,128)} %get-tuple-element.25.refs_4_, ...), custom_call_target="tpu_custom_call" | custom-call | tf_op jit(solution)/shard_map/pallas_call | solution.py:113
  (58 shorter events, 4.9 us)
Async XLA Ops:
  3.8 5.2 %copy-start.4 = (bf16[64,1152]{1,0:T(8,128)(2,1)S(1)}, bf16[64,1152]{1,0:T(8,128)(2,1)}, u32[]{:S(2)}) copy-start(bf16[64,1152]{1,0:T(8,128)(2,1)} %get-tuple-element.19) | copy-start | bytes 442372
  3.8 33.4 %all-to-all-start = ((bf16[4,256,1152]{2,1,0:T(8,128)(2,1)}), bf16[4,256,1152]{2,1,0:T(8,128)(2,1)S(1)}, u32[]{:S(2)}, u32[]{:S(2)}) async-start(bf16[4,256,1152]{2,1,0:T(8,128)(2,1)} %get-tuple-element.18), calls=%async_computation | async-start | bytes 4718592 | tf_op jit(solution)/shard_map/all_to_all | solution.py:260
  8.9 9.4 %collective-permute-start.2 = (bf16[64,1152]{1,0:T(8,128)(2,1)S(1)}, bf16[64,1152]{1,0:T(8,128)(2,1)S(1)}, u32[]{:S(2)}, u32[]{:S(2)}) collective-permute-start(bf16[64,1152]{1,0:T(8,128)(2,1)S(1)} %copy-done.4), channel_id=1, source_target_pairs={{0,2},{1,65},{2,4},{3,67},{4,6},{5,69},{6,0},{7,71},{8,10},{9,73},... | collective-permute-start | bytes 442376 | tf_op jit(solution)/shard_map/ppermute | solution.py:28
  10.6 7.7 %collective-permute-start.1 = (bf16[64,1152]{1,0:T(8,128)(2,1)S(1)}, bf16[64,1152]{1,0:T(8,128)(2,1)S(1)}, u32[]{:S(2)}, u32[]{:S(2)}) collective-permute-start(bf16[64,1152]{1,0:T(8,128)(2,1)S(1)} %copy-done.4), channel_id=1, source_target_pairs={{0,4},{1,9},{2,6},{3,11},{4,0},{5,13},{6,2},{7,15},{8,12},{9,1},{1... | collective-permute-start | bytes 442376 | tf_op jit(solution)/shard_map/ppermute | solution.py:28
  13.9 4.3 %collective-permute-start = (bf16[64,1152]{1,0:T(8,128)(2,1)S(1)}, bf16[64,1152]{1,0:T(8,128)(2,1)S(1)}, u32[]{:S(2)}, u32[]{:S(2)}) collective-permute-start(bf16[64,1152]{1,0:T(8,128)(2,1)S(1)} %copy-done.4), channel_id=1, source_target_pairs={{0,6},{1,73},{2,0},{3,75},{4,2},{5,77},{6,4},{7,79},{8,14},{9,65},... | collective-permute-start | bytes 442376 | tf_op jit(solution)/shard_map/ppermute | solution.py:28
  18.3 18.8 %copy-start.1 = (bf16[256,1152]{1,0:T(8,128)(2,1)}, bf16[256,1152]{1,0:T(8,128)(2,1)S(1)}, u32[]{:S(2)}) copy-start(bf16[256,1152]{1,0:T(8,128)(2,1)S(1)} %constant_dynamic-update-slice_fusion.refs_1_.refs_6_) | copy-start | bytes 1769476
  18.3 10.7 %collective-permute-start.5 = (bf16[256,1152]{1,0:T(8,128)(2,1)S(1)}, bf16[256,1152]{1,0:T(8,128)(2,1)S(1)}, u32[]{:S(2)}, u32[]{:S(2)}) collective-permute-start(bf16[256,1152]{1,0:T(8,128)(2,1)S(1)} %constant_dynamic-update-slice_fusion.refs_1_.refs_6_), channel_id=1, source_target_pairs={{0,8},{1,5},{2,10},{3,7},{4,12},{5,1},{6,14},{7,3},{8,0},{9,13},{1... | collective-permute-start | bytes 1769480 | tf_op jit(solution)/shard_map/ppermute | solution.py:28
  21.1 14.2 %collective-permute-start.4 = (bf16[256,1152]{1,0:T(8,128)(2,1)S(1)}, bf16[256,1152]{1,0:T(8,128)(2,1)S(1)}, u32[]{:S(2)}, u32[]{:S(2)}) collective-permute-start(bf16[256,1152]{1,0:T(8,128)(2,1)S(1)} %constant_dynamic-update-slice_fusion.refs_1_.refs_6_), channel_id=1, source_target_pairs={{0,64},{1,3},{2,66},{3,5},{4,68},{5,7},{6,70},{7,1},{8,72},{9,11},... | collective-permute-start | bytes 1769480 | tf_op jit(solution)/shard_map/ppermute | solution.py:28
  21.4 14.7 %collective-permute-start.3 = (bf16[256,1152]{1,0:T(8,128)(2,1)S(1)}, bf16[256,1152]{1,0:T(8,128)(2,1)}, u32[]{:S(2)}, u32[]{:S(2)}) collective-permute-start(bf16[256,1152]{1,0:T(8,128)(2,1)S(1)} %constant_dynamic-update-slice_fusion.refs_1_.refs_6_), channel_id=1, source_target_pairs={{0,72},{1,7},{2,74},{3,1},{4,76},{5,3},{6,78},{7,5},{8,64},{9,15},... | collective-permute-start | bytes 1769480 | tf_op jit(solution)/shard_map/ppermute | solution.py:28
  29.0 8.2 %copy-start.2 = (bf16[256,1152]{1,0:T(8,128)(2,1)}, bf16[256,1152]{1,0:T(8,128)(2,1)S(1)}, u32[]{:S(2)}) copy-start(bf16[256,1152]{1,0:T(8,128)(2,1)S(1)} %collective-permute-done.5.refs_4_.refs_9_) | copy-start | bytes 1769476
  35.3 0.8 copy-start.3
  37.2 1.4 %copy-start = (bf16[4,256,1152]{2,1,0:T(8,128)(2,1)}, bf16[4,256,1152]{2,1,0:T(8,128)(2,1)S(1)}, u32[]{:S(2)}) copy-start(bf16[4,256,1152]{2,1,0:T(8,128)(2,1)S(1)} %all-to-all-done) | copy-start | bytes 7077892
  38.6 1.9 %copy-start.5 = (s32[4]{0:T(128)S(1)}, s32[4]{0:T(128)}, u32[]{:S(2)}) copy-start(s32[4]{0:T(128)} %constant.206.clone) | copy-start | bytes 52
  38.6 6.2 %collective-permute-start.6 = (bf16[1024,1152]{1,0:T(8,128)(2,1)}, bf16[1024,1152]{1,0:T(8,128)(2,1)S(1)}, u32[]{:S(2)}, u32[]{:S(2)}) collective-permute-start(bf16[1024,1152]{1,0:T(8,128)(2,1)} %shard_map.86.refs_4_), channel_id=1, source_target_pairs={{0,1},{1,0},{2,3},{3,2},{4,5},{5,4},{6,7},{7,6},{8,9},{9,8},{10,11... | collective-permute-start | bytes 7077896 | tf_op jit(solution)/shard_map/ppermute | solution.py:28
  70.1 4.6 %collective-permute-start.9 = (f16[1024,1152]{1,0:T(8,128)(2,1)S(1)}, f16[1024,1152]{1,0:T(8,128)(2,1)S(1)}, u32[]{:S(2)}, u32[]{:S(2)}) collective-permute-start(f16[1024,1152]{1,0:T(8,128)(2,1)S(1)} %multiply_convert_fusion), channel_id=1, source_target_pairs={{0,1},{1,0},{2,3},{3,2},{4,5},{5,4},{6,7},{7,6},{8,9},{9,8},{10,11... | collective-permute-start | bytes 7077896 | tf_op jit(solution)/shard_map/ppermute | solution.py:28
  70.7 15.7 %collective-permute-start.8 = (f16[256,1152]{1,0:T(8,128)(2,1)S(1)}, f16[256,1152]{1,0:T(8,128)(2,1)S(1)}, u32[]{:S(2)}, u32[]{:S(2)}) collective-permute-start(f16[256,1152]{1,0:T(8,128)(2,1)S(1)} %multiply_convert_fusion.5), channel_id=1, source_target_pairs={{0,72},{1,7},{2,74},{3,1},{4,76},{5,3},{6,78},{7,5},{8,64},{9,15},... | collective-permute-start | bytes 1769480 | tf_op jit(solution)/shard_map/ppermute | solution.py:28
  73.3 17.0 %collective-permute-start.7 = (f16[256,1152]{1,0:T(8,128)(2,1)S(1)}, f16[256,1152]{1,0:T(8,128)(2,1)S(1)}, u32[]{:S(2)}, u32[]{:S(2)}) collective-permute-start(f16[256,1152]{1,0:T(8,128)(2,1)S(1)} %multiply_convert_fusion.6), channel_id=1, source_target_pairs={{0,64},{1,3},{2,66},{3,5},{4,68},{5,7},{6,70},{7,1},{8,72},{9,11},... | collective-permute-start | bytes 1769480 | tf_op jit(solution)/shard_map/ppermute | solution.py:28
  74.9 15.4 %collective-permute-start.10 = (f16[256,1152]{1,0:T(8,128)(2,1)S(1)}, f16[256,1152]{1,0:T(8,128)(2,1)S(1)}, u32[]{:S(2)}, u32[]{:S(2)}) collective-permute-start(f16[256,1152]{1,0:T(8,128)(2,1)S(1)} %multiply_convert_fusion.4), channel_id=1, source_target_pairs={{0,8},{1,5},{2,10},{3,7},{4,12},{5,1},{6,14},{7,3},{8,0},{9,13},{1... | collective-permute-start | bytes 1769480 | tf_op jit(solution)/shard_map/ppermute | solution.py:28
  79.7 23.2 %collective-permute-start.16 = (f16[256,1152]{1,0:T(8,128)(2,1)}, f16[256,1152]{1,0:T(8,128)(2,1)}, u32[]{:S(2)}, u32[]{:S(2)}) collective-permute-start(f16[256,1152]{1,0:T(8,128)(2,1)} %get-tuple-element.34), channel_id=1, source_target_pairs={{0,32},{1,33},{2,34},{3,35},{4,36},{5,37},{6,38},{7,39},{8,40},{9,... | collective-permute-start | bytes 1769480 | tf_op jit(solution)/shard_map/ppermute | solution.py:28
  82.0 27.9 %collective-permute-start.14 = (f16[256,1152]{1,0:T(8,128)(2,1)}, f16[256,1152]{1,0:T(8,128)(2,1)}, u32[]{:S(2)}, u32[]{:S(2)}) collective-permute-start(f16[256,1152]{1,0:T(8,128)(2,1)} %get-tuple-element.33), channel_id=1, source_target_pairs={{0,16},{1,17},{2,18},{3,19},{4,20},{5,21},{6,22},{7,23},{8,24},{9,... | collective-permute-start | bytes 1769480 | tf_op jit(solution)/shard_map/ppermute | solution.py:28
  86.4 23.6 %collective-permute-start.15 = (f16[256,1152]{1,0:T(8,128)(2,1)S(1)}, f16[256,1152]{1,0:T(8,128)(2,1)}, u32[]{:S(2)}, u32[]{:S(2)}) collective-permute-start(f16[256,1152]{1,0:T(8,128)(2,1)S(1)} %get-tuple-element.35), channel_id=1, source_target_pairs={{0,48},{1,49},{2,50},{3,51},{4,52},{5,53},{6,54},{7,55},{8,56},{9,... | collective-permute-start | bytes 1769480 | tf_op jit(solution)/shard_map/ppermute | solution.py:28
  91.4 20.5 %all-to-all-start.1 = ((f32[128,1,128]{2,1,0:T(1,128)}), f32[128,1,128]{2,1,0:T(1,128)}, u32[]{:S(2)}, u32[]{:S(2)}) async-start(f32[128,1,128]{2,1,0:T(1,128)} %broadcast_in_dim.20), calls=%async_computation.1 | async-start | bytes 131072 | tf_op jit(solution)/shard_map/all_to_all | solution.py:234
  99.4 12.3 %collective-permute-start.11 = (f16[64,1152]{1,0:T(8,128)(2,1)S(1)}, f16[64,1152]{1,0:T(8,128)(2,1)S(1)}, u32[]{:S(2)}, u32[]{:S(2)}) collective-permute-start(f16[64,1152]{1,0:T(8,128)(2,1)S(1)} %get-tuple-element.37), channel_id=1, source_target_pairs={{0,2},{1,65},{2,4},{3,67},{4,6},{5,69},{6,0},{7,71},{8,10},{9,73},... | collective-permute-start | bytes 442376 | tf_op jit(solution)/shard_map/ppermute | solution.py:28
  101.0 10.7 %collective-permute-start.13 = (f16[64,1152]{1,0:T(8,128)(2,1)S(1)}, f16[64,1152]{1,0:T(8,128)(2,1)S(1)}, u32[]{:S(2)}, u32[]{:S(2)}) collective-permute-start(f16[64,1152]{1,0:T(8,128)(2,1)S(1)} %get-tuple-element.38), channel_id=1, source_target_pairs={{0,6},{1,73},{2,0},{3,75},{4,2},{5,77},{6,4},{7,79},{8,14},{9,65},... | collective-permute-start | bytes 442376 | tf_op jit(solution)/shard_map/ppermute | solution.py:28
  102.8 8.9 %collective-permute-start.12 = (f16[64,1152]{1,0:T(8,128)(2,1)S(1)}, f16[64,1152]{1,0:T(8,128)(2,1)S(1)}, u32[]{:S(2)}, u32[]{:S(2)}) collective-permute-start(f16[64,1152]{1,0:T(8,128)(2,1)S(1)} %get-tuple-element.39), channel_id=1, source_target_pairs={{0,4},{1,9},{2,6},{3,11},{4,0},{5,13},{6,2},{7,15},{8,12},{9,1},{1... | collective-permute-start | bytes 442376 | tf_op jit(solution)/shard_map/ppermute | solution.py:28

commit v6 on v5

--- a/solution.py
+++ b/solution.py
@@ -295,7 +295,7 @@
         text_dir = text_dir + wide(send(wire, along_y(s)))
 
     line_dir, up_part, down_part, far_part = parts
-    far_part = after(far_part, [other])
+    down_part, far_part = after(down_part, [other]), after(far_part, [other])
     for s, part in ((1, up_part), (3, down_part), (2, far_part)):
         line_dir = line_dir + wide(send(narrow(part), along_second(s)))
     loss = loss_parts(after(loss, [line_dir]))

time: 115 us -> 117 us (1.017)
  starting transfers between devices: 42.1 us -> 44.2 us
    all_to_all x1, starting transfers between devices: 7.9 us -> 10.8 us  [loss_parts(): return lax.all_to_all(parts, AXES, 0, 0, tiled=True)]
    ppermute x17, waiting for transfers between devices: 28.4 us -> 27 us  [send(): return lax.ppermute(value, AXES, pairs)]
    convert_element_type x6 -> x5, other arithmetic: 2.83 us -> 2.85 us  [narrow(): return (part * 0.25).astype(WIRE)]
  transfers between devices with their start and end apart: 19 -> 19, of which waited for: 11 -> 11; matrix products, arithmetic and copies ran while one was open for 7% -> 6% of each run, Pallas kernels for 0% -> 0%
where the time goes in v6:
time: 117 us
  starting transfers between devices  44.2 us (38%)
  Pallas kernels  30.9 us (26%)
  waiting for transfers between devices  29.2 us (25%)
  other arithmetic  5.5 us (5%)
  local copies, waits for them, and re-layouts  4.71 us (4%)
  between operations  2.16 us (2%)
    ppermute x17, starting transfers between devices, send(): return lax.ppermute(value, AXES, pairs)  28.3 us
    ppermute x17, waiting for transfers between devices, send(): return lax.ppermute(value, AXES, pairs)  27 us
    pallas_call x1, Pallas kernels, pair_block(): pl.pallas_call(functools.partial(pair_kernel, n_image), out_shape=out_sha...  24.8 us
    all_to_all x1, starting transfers between devices, loss_parts(): return lax.all_to_all(parts, AXES, 0, 0, tiled=True)  10.8 us
    all_to_all x1, starting transfers between devices, body(): lax.all_to_all(own, AXES, 0, 0, axis_index_groups=list(rings.values()), t...  5.15 us
    pallas_call x1, Pallas kernels, prepare(): pl.pallas_call(prepare_kernel, out_shape=(jax.ShapeDtypeStruct((RING,) +...  3.15 us
    pallas_call x1, Pallas kernels, finish(): pl.pallas_call(finish_kernel, out_shape=(jax.ShapeDtypeStruct(images[2].s...  2.93 us
    convert_element_type x5, other arithmetic, narrow(): return (part * 0.25).astype(WIRE)  2.85 us
  transfers between devices with their start and end apart: 19, of which 11 were waited for; matrix products, arithmetic and copies ran while one was open for 6% of the time, Pallas kernels for 0%

profile of v6, /device:TPU:1, one launch (start us, length us, event | category | flops | bytes accessed | tf_op | source)
XLA Modules:
  0.0 116.7 jit_solution(17249022349539847973)
XLA Ops:
  0.6 3.2 %shard_map.85 = (bf16[4,256,1152]{2,1,0:T(8,128)(2,1)}, f32[256,1]{1,0:T(8,128)}, bf16[64,1152]{1,0:T(8,128)(2,1)}, f32[64,1]{1,0:T(8,128)}) custom-call(f32[256,1152]{1,0:T(8,128)} %refs_3_.1, f32[64,1152]{1,0:T(8,128)} %refs_0_.1), custom_call_target="tpu_custom_call" | custom-call | tf_op jit(solution)/shard_map/pallas_call | solution.py:69
  3.8 5.1 %all-to-all-start = ((bf16[4,256,1152]{2,1,0:T(8,128)(2,1)}), bf16[4,256,1152]{2,1,0:T(8,128)(2,1)S(1)}, u32[]{:S(2)}, u32[]{:S(2)}) async-start(bf16[4,256,1152]{2,1,0:T(8,128)(2,1)} %get-tuple-element.18), calls=%async_computation | async-start | bytes 4718592 | tf_op jit(solution)/shard_map/all_to_all | solution.py:260
  8.9 1.6 %collective-permute-start.2 = (bf16[64,1152]{1,0:T(8,128)(2,1)S(1)}, bf16[64,1152]{1,0:T(8,128)(2,1)S(1)}, u32[]{:S(2)}, u32[]{:S(2)}) collective-permute-start(bf16[64,1152]{1,0:T(8,128)(2,1)S(1)} %copy-done.4), channel_id=1, source_target_pairs={{0,2},{1,65},{2,4},{3,67},{4,6},{5,69},{6,0},{7,71},{8,10},{9,73},... | collective-permute-start | bytes 442376 | tf_op jit(solution)/shard_map/ppermute | solution.py:28
  10.6 3.3 %collective-permute-start.1 = (bf16[64,1152]{1,0:T(8,128)(2,1)S(1)}, bf16[64,1152]{1,0:T(8,128)(2,1)S(1)}, u32[]{:S(2)}, u32[]{:S(2)}) collective-permute-start(bf16[64,1152]{1,0:T(8,128)(2,1)S(1)} %copy-done.4), channel_id=1, source_target_pairs={{0,4},{1,9},{2,6},{3,11},{4,0},{5,13},{6,2},{7,15},{8,12},{9,1},{1... | collective-permute-start | bytes 442376 | tf_op jit(solution)/shard_map/ppermute | solution.py:28
  13.9 0.7 collective-permute-start
  14.6 3.5 %collective-permute-done = bf16[64,1152]{1,0:T(8,128)(2,1)S(1)} collective-permute-done((bf16[64,1152]{1,0:T(8,128)(2,1)S(1)}, bf16[64,1152]{1,0:T(8,128)(2,1)S(1)}, u32[]{:S(2)}, u32[]{:S(2)}) %collective-permute-start) | collective-permute-done | bytes 147488 | tf_op jit(solution)/shard_map/ppermute | solution.py:28
  18.3 2.7 %collective-permute-start.5 = (bf16[256,1152]{1,0:T(8,128)(2,1)S(1)}, bf16[256,1152]{1,0:T(8,128)(2,1)S(1)}, u32[]{:S(2)}, u32[]{:S(2)}) collective-permute-start(bf16[256,1152]{1,0:T(8,128)(2,1)S(1)} %constant_dynamic-update-slice_fusion.refs_1_.refs_6_), channel_id=1, source_target_pairs={{0,8},{1,5},{2,10},{3,7},{4,12},{5,1},{6,14},{7,3},{8,0},{9,13},{1... | collective-permute-start | bytes 1769480 | tf_op jit(solution)/shard_map/ppermute | solution.py:28
  21.4 2.4 %collective-permute-start.3 = (bf16[256,1152]{1,0:T(8,128)(2,1)S(1)}, bf16[256,1152]{1,0:T(8,128)(2,1)}, u32[]{:S(2)}, u32[]{:S(2)}) collective-permute-start(bf16[256,1152]{1,0:T(8,128)(2,1)S(1)} %constant_dynamic-update-slice_fusion.refs_1_.refs_6_), channel_id=1, source_target_pairs={{0,72},{1,7},{2,74},{3,1},{4,76},{5,3},{6,78},{7,5},{8,64},{9,15},... | collective-permute-start | bytes 1769480 | tf_op jit(solution)/shard_map/ppermute | solution.py:28
  23.8 5.2 %collective-permute-done.5.refs_4_.refs_9_ = bf16[256,1152]{1,0:T(8,128)(2,1)S(1)} collective-permute-done((bf16[256,1152]{1,0:T(8,128)(2,1)S(1)}, bf16[256,1152]{1,0:T(8,128)(2,1)S(1)}, u32[]{:S(2)}, u32[]{:S(2)}) %collective-permute-start.5) | collective-permute-done | bytes 589856 | tf_op jit(solution)/shard_map/ppermute | solution.py:28
  29.0 6.3 %collective-permute-done.4.refs_3_.refs_8_ = bf16[256,1152]{1,0:T(8,128)(2,1)S(1)} collective-permute-done((bf16[256,1152]{1,0:T(8,128)(2,1)S(1)}, bf16[256,1152]{1,0:T(8,128)(2,1)S(1)}, u32[]{:S(2)}, u32[]{:S(2)}) %collective-permute-start.4) | collective-permute-done | bytes 589856 | tf_op jit(solution)/shard_map/ppermute | solution.py:28
  35.3 0.8 copy-done.3
  36.1 1.1 all-to-all-done
  37.2 1.4 %copy-done = bf16[4,256,1152]{2,1,0:T(8,128)(2,1)} copy-done((bf16[4,256,1152]{2,1,0:T(8,128)(2,1)}, bf16[4,256,1152]{2,1,0:T(8,128)(2,1)S(1)}, u32[]{:S(2)}) %copy-start) | copy-done | bytes 2359320
  38.6 1.9 %collective-permute-start.6 = (bf16[1024,1152]{1,0:T(8,128)(2,1)}, bf16[1024,1152]{1,0:T(8,128)(2,1)S(1)}, u32[]{:S(2)}, u32[]{:S(2)}) collective-permute-start(bf16[1024,1152]{1,0:T(8,128)(2,1)} %shard_map.86.refs_4_), channel_id=1, source_target_pairs={{0,1},{1,0},{2,3},{3,2},{4,5},{5,4},{6,7},{7,6},{8,9},{9,8},{10,11... | collective-permute-start | bytes 7077896 | tf_op jit(solution)/shard_map/ppermute | solution.py:28
  42.1 0.8 reshape.285
  43.9 1.0 collective-permute-done.6.refs_5_
  44.8 24.8 %shard_map.87 = (f32[1024,1152]{1,0:T(8,128)S(1)}, f32[1024,1152]{1,0:T(8,128)S(1)}, f32[256,1152]{1,0:T(8,128)S(1)}, f32[256,1152]{1,0:T(8,128)S(1)}, f32[256,1...) custom-call(f32[3]{0:T(128)S(1)} %pad_maximum_fusion.refs_0_, s32[8]{0:T(128)S(1)} %pad_add_fusion.refs_1_, ...), custom_call_target="tpu_custom_call" | custom-call | flops 14495514624 | bytes 7077888 | tf_op jit(solution)/shard_map/pallas_call | solution.py:207
  70.7 1.3 %collective-permute-start.7 = (f16[256,1152]{1,0:T(8,128)(2,1)S(1)}, f16[256,1152]{1,0:T(8,128)(2,1)S(1)}, u32[]{:S(2)}, u32[]{:S(2)}) collective-permute-start(f16[256,1152]{1,0:T(8,128)(2,1)S(1)} %multiply_convert_fusion.6), channel_id=1, source_target_pairs={{0,64},{1,3},{2,66},{3,5},{4,68},{5,7},{6,70},{7,1},{8,72},{9,11},... | collective-permute-start | bytes 1769480 | tf_op jit(solution)/shard_map/ppermute | solution.py:28
  71.9 2.8 %collective-permute-done.8 = f16[1024,1152]{1,0:T(8,128)(2,1)S(1)} collective-permute-done((f16[1024,1152]{1,0:T(8,128)(2,1)S(1)}, f16[1024,1152]{1,0:T(8,128)(2,1)S(1)}, u32[]{:S(2)}, u32[]{:S(2)}) %collective-permute-start.8) | collective-permute-done | bytes 2359328 | tf_op jit(solution)/shard_map/ppermute | solution.py:28
  75.0 2.8 %collective-permute-start.9 = (f16[256,1152]{1,0:T(8,128)(2,1)S(1)}, f16[256,1152]{1,0:T(8,128)(2,1)S(1)}, u32[]{:S(2)}, u32[]{:S(2)}) collective-permute-start(f16[256,1152]{1,0:T(8,128)(2,1)S(1)} %get-tuple-element.40), channel_id=1, source_target_pairs={{0,72},{1,7},{2,74},{3,1},{4,76},{5,3},{6,78},{7,5},{8,64},{9,15},... | collective-permute-start | bytes 1769480 | tf_op jit(solution)/shard_map/ppermute | solution.py:28
  78.3 1.9 %multiply_convert_fusion.3 = (f16[256,1152]{1,0:T(8,128)(2,1)}, f16[256,1152]{1,0:T(8,128)(2,1)}, f16[256,1152]{1,0:T(8,128)(2,1)S(1)}, f32[256,1152]{1,0:T(8,128)S(1)}) fusion(f32[1024,1152]{1,0:T(8,128)S(1)} %get-tuple-element.26, f16[1024,1152]{1,0:T(8,128)(2,1)S(1)} %collective-permute-done.8), kind=kLoop, calls=%fused_computation.5 | loop fusion | flops 5308416 | bytes 10027008 | tf_op jit(solution)/shard_map/convert_element_type | solution.py:238
  80.3 2.8 %collective-permute-start.16 = (f16[256,1152]{1,0:T(8,128)(2,1)}, f16[256,1152]{1,0:T(8,128)(2,1)}, u32[]{:S(2)}, u32[]{:S(2)}) collective-permute-start(f16[256,1152]{1,0:T(8,128)(2,1)} %get-tuple-element.34), channel_id=1, source_target_pairs={{0,32},{1,33},{2,34},{3,35},{4,36},{5,37},{6,38},{7,39},{8,40},{9,... | collective-permute-start | bytes 1769480 | tf_op jit(solution)/shard_map/ppermute | solution.py:28
  83.4 2.4 %collective-permute-start.15 = (f16[256,1152]{1,0:T(8,128)(2,1)S(1)}, f16[256,1152]{1,0:T(8,128)(2,1)}, u32[]{:S(2)}, u32[]{:S(2)}) collective-permute-start(f16[256,1152]{1,0:T(8,128)(2,1)S(1)} %get-tuple-element.35), channel_id=1, source_target_pairs={{0,48},{1,49},{2,50},{3,51},{4,52},{5,53},{6,54},{7,55},{8,56},{9,... | collective-permute-start | bytes 1769480 | tf_op jit(solution)/shard_map/ppermute | solution.py:28
  85.8 5.2 %collective-permute-done.9 = f16[256,1152]{1,0:T(8,128)(2,1)S(1)} collective-permute-done((f16[256,1152]{1,0:T(8,128)(2,1)S(1)}, f16[256,1152]{1,0:T(8,128)(2,1)S(1)}, u32[]{:S(2)}, u32[]{:S(2)}) %collective-permute-start.9) | collective-permute-done | bytes 589856 | tf_op jit(solution)/shard_map/ppermute | solution.py:28
  92.1 10.8 %all-to-all-start.1 = ((f32[128,1,128]{2,1,0:T(1,128)}), f32[128,1,128]{2,1,0:T(1,128)}, u32[]{:S(2)}, u32[]{:S(2)}) async-start(f32[128,1,128]{2,1,0:T(1,128)} %broadcast_in_dim.20), calls=%async_computation.1 | async-start | bytes 131072 | tf_op jit(solution)/shard_map/all_to_all | solution.py:234
  103.0 1.6 %collective-permute-start.11 = (f16[64,1152]{1,0:T(8,128)(2,1)S(1)}, f16[64,1152]{1,0:T(8,128)(2,1)S(1)}, u32[]{:S(2)}, u32[]{:S(2)}) collective-permute-start(f16[64,1152]{1,0:T(8,128)(2,1)S(1)} %get-tuple-element.37), channel_id=1, source_target_pairs={{0,2},{1,65},{2,4},{3,67},{4,6},{5,69},{6,0},{7,71},{8,10},{9,73},... | collective-permute-start | bytes 442376 | tf_op jit(solution)/shard_map/ppermute | solution.py:28
  104.6 1.8 %collective-permute-start.13 = (f16[64,1152]{1,0:T(8,128)(2,1)S(1)}, f16[64,1152]{1,0:T(8,128)(2,1)S(1)}, u32[]{:S(2)}, u32[]{:S(2)}) collective-permute-start(f16[64,1152]{1,0:T(8,128)(2,1)S(1)} %get-tuple-element.38), channel_id=1, source_target_pairs={{0,6},{1,73},{2,0},{3,75},{4,2},{5,77},{6,4},{7,79},{8,14},{9,65},... | collective-permute-start | bytes 442376 | tf_op jit(solution)/shard_map/ppermute | solution.py:28
  106.4 1.4 %collective-permute-start.12 = (f16[64,1152]{1,0:T(8,128)(2,1)S(1)}, f16[64,1152]{1,0:T(8,128)(2,1)S(1)}, u32[]{:S(2)}, u32[]{:S(2)}) collective-permute-start(f16[64,1152]{1,0:T(8,128)(2,1)S(1)} %get-tuple-element.39), channel_id=1, source_target_pairs={{0,4},{1,9},{2,6},{3,11},{4,0},{5,13},{6,2},{7,15},{8,12},{9,1},{1... | collective-permute-start | bytes 442376 | tf_op jit(solution)/shard_map/ppermute | solution.py:28
  107.8 2.7 %collective-permute-done.14 = f16[256,1152]{1,0:T(8,128)(2,1)} collective-permute-done((f16[256,1152]{1,0:T(8,128)(2,1)}, f16[256,1152]{1,0:T(8,128)(2,1)}, u32[]{:S(2)}, u32[]{:S(2)}) %collective-permute-start.14) | collective-permute-done | bytes 589856 | tf_op jit(solution)/shard_map/ppermute | solution.py:28
  110.5 1.8 %multiply_add_fusion.refs_5_ = f32[256,1152]{1,0:T(8,128)S(1)} fusion(f16[256,1152]{1,0:T(8,128)(2,1)} %collective-permute-done.16, f16[256,1152]{1,0:T(8,128)(2,1)} %collective-permute-done.15, f32[256,1152]{1,0:T(8,128)S(1)} %get-tuple-element.36, f16[256,1152]{1,0:T(8,128)(2,1)} %collective-permute-done.14), kind=kLoop, calls=%fused_computation.2 | loop fusion | flops 2654208 | bytes 4128768 | tf_op jit(solution)/shard_map/add | solution.py:295
  112.7 1.1 all-to-all-done.1.refs_6_
  113.8 2.9 %shard_map.88 = (f32[64,1152]{1,0:T(8,128)}, f32[256,1152]{1,0:T(8,128)}, f32[1,1]{1,0:T(1,128)}) custom-call(f32[64,1152]{1,0:T(8,128)} %refs_0_.1, f32[64,1]{1,0:T(8,128)} %get-tuple-element.17.refs_1_, f32[64,1152]{1,0:T(8,128)S(1)} %fusion.2.refs_2_, f32[256,1152]{1,0:T(8,128)} %refs_3_.1, f32[256,1]{1,0:T(8,128)} %get-tuple-element.25.refs_4_, ...), custom_call_target="tpu_custom_call" | custom-call | tf_op jit(solution)/shard_map/pallas_call | solution.py:113
  (57 shorter events, 5.3 us)
Async XLA Ops:
  3.8 5.2 %copy-start.4 = (bf16[64,1152]{1,0:T(8,128)(2,1)S(1)}, bf16[64,1152]{1,0:T(8,128)(2,1)}, u32[]{:S(2)}) copy-start(bf16[64,1152]{1,0:T(8,128)(2,1)} %get-tuple-element.19) | copy-start | bytes 442372
  3.8 33.4 %all-to-all-start = ((bf16[4,256,1152]{2,1,0:T(8,128)(2,1)}), bf16[4,256,1152]{2,1,0:T(8,128)(2,1)S(1)}, u32[]{:S(2)}, u32[]{:S(2)}) async-start(bf16[4,256,1152]{2,1,0:T(8,128)(2,1)} %get-tuple-element.18), calls=%async_computation | async-start | bytes 4718592 | tf_op jit(solution)/shard_map/all_to_all | solution.py:260
  8.9 9.4 %collective-permute-start.2 = (bf16[64,1152]{1,0:T(8,128)(2,1)S(1)}, bf16[64,1152]{1,0:T(8,128)(2,1)S(1)}, u32[]{:S(2)}, u32[]{:S(2)}) collective-permute-start(bf16[64,1152]{1,0:T(8,128)(2,1)S(1)} %copy-done.4), channel_id=1, source_target_pairs={{0,2},{1,65},{2,4},{3,67},{4,6},{5,69},{6,0},{7,71},{8,10},{9,73},... | collective-permute-start | bytes 442376 | tf_op jit(solution)/shard_map/ppermute | solution.py:28
  10.6 7.7 %collective-permute-start.1 = (bf16[64,1152]{1,0:T(8,128)(2,1)S(1)}, bf16[64,1152]{1,0:T(8,128)(2,1)S(1)}, u32[]{:S(2)}, u32[]{:S(2)}) collective-permute-start(bf16[64,1152]{1,0:T(8,128)(2,1)S(1)} %copy-done.4), channel_id=1, source_target_pairs={{0,4},{1,9},{2,6},{3,11},{4,0},{5,13},{6,2},{7,15},{8,12},{9,1},{1... | collective-permute-start | bytes 442376 | tf_op jit(solution)/shard_map/ppermute | solution.py:28
  13.9 4.3 %collective-permute-start = (bf16[64,1152]{1,0:T(8,128)(2,1)S(1)}, bf16[64,1152]{1,0:T(8,128)(2,1)S(1)}, u32[]{:S(2)}, u32[]{:S(2)}) collective-permute-start(bf16[64,1152]{1,0:T(8,128)(2,1)S(1)} %copy-done.4), channel_id=1, source_target_pairs={{0,6},{1,73},{2,0},{3,75},{4,2},{5,77},{6,4},{7,79},{8,14},{9,65},... | collective-permute-start | bytes 442376 | tf_op jit(solution)/shard_map/ppermute | solution.py:28
  18.3 18.8 %copy-start.1 = (bf16[256,1152]{1,0:T(8,128)(2,1)}, bf16[256,1152]{1,0:T(8,128)(2,1)S(1)}, u32[]{:S(2)}) copy-start(bf16[256,1152]{1,0:T(8,128)(2,1)S(1)} %constant_dynamic-update-slice_fusion.refs_1_.refs_6_) | copy-start | bytes 1769476
  18.3 10.7 %collective-permute-start.5 = (bf16[256,1152]{1,0:T(8,128)(2,1)S(1)}, bf16[256,1152]{1,0:T(8,128)(2,1)S(1)}, u32[]{:S(2)}, u32[]{:S(2)}) collective-permute-start(bf16[256,1152]{1,0:T(8,128)(2,1)S(1)} %constant_dynamic-update-slice_fusion.refs_1_.refs_6_), channel_id=1, source_target_pairs={{0,8},{1,5},{2,10},{3,7},{4,12},{5,1},{6,14},{7,3},{8,0},{9,13},{1... | collective-permute-start | bytes 1769480 | tf_op jit(solution)/shard_map/ppermute | solution.py:28
  21.1 14.2 %collective-permute-start.4 = (bf16[256,1152]{1,0:T(8,128)(2,1)S(1)}, bf16[256,1152]{1,0:T(8,128)(2,1)S(1)}, u32[]{:S(2)}, u32[]{:S(2)}) collective-permute-start(bf16[256,1152]{1,0:T(8,128)(2,1)S(1)} %constant_dynamic-update-slice_fusion.refs_1_.refs_6_), channel_id=1, source_target_pairs={{0,64},{1,3},{2,66},{3,5},{4,68},{5,7},{6,70},{7,1},{8,72},{9,11},... | collective-permute-start | bytes 1769480 | tf_op jit(solution)/shard_map/ppermute | solution.py:28
  21.4 14.7 %collective-permute-start.3 = (bf16[256,1152]{1,0:T(8,128)(2,1)S(1)}, bf16[256,1152]{1,0:T(8,128)(2,1)}, u32[]{:S(2)}, u32[]{:S(2)}) collective-permute-start(bf16[256,1152]{1,0:T(8,128)(2,1)S(1)} %constant_dynamic-update-slice_fusion.refs_1_.refs_6_), channel_id=1, source_target_pairs={{0,72},{1,7},{2,74},{3,1},{4,76},{5,3},{6,78},{7,5},{8,64},{9,15},... | collective-permute-start | bytes 1769480 | tf_op jit(solution)/shard_map/ppermute | solution.py:28
  29.0 8.2 %copy-start.2 = (bf16[256,1152]{1,0:T(8,128)(2,1)}, bf16[256,1152]{1,0:T(8,128)(2,1)S(1)}, u32[]{:S(2)}) copy-start(bf16[256,1152]{1,0:T(8,128)(2,1)S(1)} %collective-permute-done.5.refs_4_.refs_9_) | copy-start | bytes 1769476
  35.3 0.8 copy-start.3
  37.2 1.4 %copy-start = (bf16[4,256,1152]{2,1,0:T(8,128)(2,1)}, bf16[4,256,1152]{2,1,0:T(8,128)(2,1)S(1)}, u32[]{:S(2)}) copy-start(bf16[4,256,1152]{2,1,0:T(8,128)(2,1)S(1)} %all-to-all-done) | copy-start | bytes 7077892
  38.6 1.9 %copy-start.5 = (s32[4]{0:T(128)S(1)}, s32[4]{0:T(128)}, u32[]{:S(2)}) copy-start(s32[4]{0:T(128)} %constant.206.clone) | copy-start | bytes 52
  38.6 6.2 %collective-permute-start.6 = (bf16[1024,1152]{1,0:T(8,128)(2,1)}, bf16[1024,1152]{1,0:T(8,128)(2,1)S(1)}, u32[]{:S(2)}, u32[]{:S(2)}) collective-permute-start(bf16[1024,1152]{1,0:T(8,128)(2,1)} %shard_map.86.refs_4_), channel_id=1, source_target_pairs={{0,1},{1,0},{2,3},{3,2},{4,5},{5,4},{6,7},{7,6},{8,9},{9,8},{10,11... | collective-permute-start | bytes 7077896 | tf_op jit(solution)/shard_map/ppermute | solution.py:28
  70.1 4.6 %collective-permute-start.8 = (f16[1024,1152]{1,0:T(8,128)(2,1)S(1)}, f16[1024,1152]{1,0:T(8,128)(2,1)S(1)}, u32[]{:S(2)}, u32[]{:S(2)}) collective-permute-start(f16[1024,1152]{1,0:T(8,128)(2,1)S(1)} %multiply_convert_fusion), channel_id=1, source_target_pairs={{0,1},{1,0},{2,3},{3,2},{4,5},{5,4},{6,7},{7,6},{8,9},{9,8},{10,11... | collective-permute-start | bytes 7077896 | tf_op jit(solution)/shard_map/ppermute | solution.py:28
  70.7 12.7 %collective-permute-start.7 = (f16[256,1152]{1,0:T(8,128)(2,1)S(1)}, f16[256,1152]{1,0:T(8,128)(2,1)S(1)}, u32[]{:S(2)}, u32[]{:S(2)}) collective-permute-start(f16[256,1152]{1,0:T(8,128)(2,1)S(1)} %multiply_convert_fusion.6), channel_id=1, source_target_pairs={{0,64},{1,3},{2,66},{3,5},{4,68},{5,7},{6,70},{7,1},{8,72},{9,11},... | collective-permute-start | bytes 1769480 | tf_op jit(solution)/shard_map/ppermute | solution.py:28
  75.0 15.9 %collective-permute-start.9 = (f16[256,1152]{1,0:T(8,128)(2,1)S(1)}, f16[256,1152]{1,0:T(8,128)(2,1)S(1)}, u32[]{:S(2)}, u32[]{:S(2)}) collective-permute-start(f16[256,1152]{1,0:T(8,128)(2,1)S(1)} %get-tuple-element.40), channel_id=1, source_target_pairs={{0,72},{1,7},{2,74},{3,1},{4,76},{5,3},{6,78},{7,5},{8,64},{9,15},... | collective-permute-start | bytes 1769480 | tf_op jit(solution)/shard_map/ppermute | solution.py:28
  77.8 13.2 %collective-permute-start.10 = (f16[256,1152]{1,0:T(8,128)(2,1)S(1)}, f16[256,1152]{1,0:T(8,128)(2,1)S(1)}, u32[]{:S(2)}, u32[]{:S(2)}) collective-permute-start(f16[256,1152]{1,0:T(8,128)(2,1)S(1)} %get-tuple-element.41), channel_id=1, source_target_pairs={{0,8},{1,5},{2,10},{3,7},{4,12},{5,1},{6,14},{7,3},{8,0},{9,13},{1... | collective-permute-start | bytes 1769480 | tf_op jit(solution)/shard_map/ppermute | solution.py:28
  80.3 26.1 %collective-permute-start.16 = (f16[256,1152]{1,0:T(8,128)(2,1)}, f16[256,1152]{1,0:T(8,128)(2,1)}, u32[]{:S(2)}, u32[]{:S(2)}) collective-permute-start(f16[256,1152]{1,0:T(8,128)(2,1)} %get-tuple-element.34), channel_id=1, source_target_pairs={{0,32},{1,33},{2,34},{3,35},{4,36},{5,37},{6,38},{7,39},{8,40},{9,... | collective-permute-start | bytes 1769480 | tf_op jit(solution)/shard_map/ppermute | solution.py:28
  83.1 27.4 %collective-permute-start.14 = (f16[256,1152]{1,0:T(8,128)(2,1)}, f16[256,1152]{1,0:T(8,128)(2,1)}, u32[]{:S(2)}, u32[]{:S(2)}) collective-permute-start(f16[256,1152]{1,0:T(8,128)(2,1)} %get-tuple-element.33), channel_id=1, source_target_pairs={{0,16},{1,17},{2,18},{3,19},{4,20},{5,21},{6,22},{7,23},{8,24},{9,... | collective-permute-start | bytes 1769480 | tf_op jit(solution)/shard_map/ppermute | solution.py:28
  83.4 27.2 %collective-permute-start.15 = (f16[256,1152]{1,0:T(8,128)(2,1)S(1)}, f16[256,1152]{1,0:T(8,128)(2,1)}, u32[]{:S(2)}, u32[]{:S(2)}) collective-permute-start(f16[256,1152]{1,0:T(8,128)(2,1)S(1)} %get-tuple-element.35), channel_id=1, source_target_pairs={{0,48},{1,49},{2,50},{3,51},{4,52},{5,53},{6,54},{7,55},{8,56},{9,... | collective-permute-start | bytes 1769480 | tf_op jit(solution)/shard_map/ppermute | solution.py:28
  92.1 21.7 %all-to-all-start.1 = ((f32[128,1,128]{2,1,0:T(1,128)}), f32[128,1,128]{2,1,0:T(1,128)}, u32[]{:S(2)}, u32[]{:S(2)}) async-start(f32[128,1,128]{2,1,0:T(1,128)} %broadcast_in_dim.20), calls=%async_computation.1 | async-start | bytes 131072 | tf_op jit(solution)/shard_map/all_to_all | solution.py:234
  103.0 9.3 %collective-permute-start.11 = (f16[64,1152]{1,0:T(8,128)(2,1)S(1)}, f16[64,1152]{1,0:T(8,128)(2,1)S(1)}, u32[]{:S(2)}, u32[]{:S(2)}) collective-permute-start(f16[64,1152]{1,0:T(8,128)(2,1)S(1)} %get-tuple-element.37), channel_id=1, source_target_pairs={{0,2},{1,65},{2,4},{3,67},{4,6},{5,69},{6,0},{7,71},{8,10},{9,73},... | collective-permute-start | bytes 442376 | tf_op jit(solution)/shard_map/ppermute | solution.py:28
  104.6 7.8 %collective-permute-start.13 = (f16[64,1152]{1,0:T(8,128)(2,1)S(1)}, f16[64,1152]{1,0:T(8,128)(2,1)S(1)}, u32[]{:S(2)}, u32[]{:S(2)}) collective-permute-start(f16[64,1152]{1,0:T(8,128)(2,1)S(1)} %get-tuple-element.38), channel_id=1, source_target_pairs={{0,6},{1,73},{2,0},{3,75},{4,2},{5,77},{6,4},{7,79},{8,14},{9,65},... | collective-permute-start | bytes 442376 | tf_op jit(solution)/shard_map/ppermute | solution.py:28
  106.4 6.1 %collective-permute-start.12 = (f16[64,1152]{1,0:T(8,128)(2,1)S(1)}, f16[64,1152]{1,0:T(8,128)(2,1)S(1)}, u32[]{:S(2)}, u32[]{:S(2)}) collective-permute-start(f16[64,1152]{1,0:T(8,128)(2,1)S(1)} %get-tuple-element.39), channel_id=1, source_target_pairs={{0,4},{1,9},{2,6},{3,11},{4,0},{5,13},{6,2},{7,15},{8,12},{9,1},{1... | collective-permute-start | bytes 442376 | tf_op jit(solution)/shard_map/ppermute | solution.py:28
